TPU v7x, 32 devices: a whole 2x2x4 slice. The times are simulated.
32 devices in a mesh: tensor: 4 (over z), mirror: 2 (over core), dp: 4 (over y, x).
Axes of the slice: x: 2, y: 2, z: 4, core: 2. Of those that a mesh axis runs over, the one named last changes fastest.
Arguments:
- layer_input: bfloat16 [8, 256, 4096], P(('mirror', 'dp'), 'tensor'), may hold values from -6 to 6
- qk_weight: bfloat16 [4096, 2, 4096], P(None, None, 'tensor'), may hold values from -0.09375 to 0.09375
- query_proj: bfloat16 [8, 256, 4096], P(('mirror', 'dp'), None, 'tensor'), may hold values from -24 to 24
- key_proj: bfloat16 [8, 256, 4096], P(('mirror', 'dp'), None, 'tensor'), may hold values from -24 to 24
- value_proj: bfloat16 [8, 256, 4096], P(('mirror', 'dp'), None, 'tensor'), may hold values from -6 to 6
- head_grad: bfloat16 [8, 256, 4096], P(('mirror', 'dp'), None, 'tensor'), may hold values from -6 to 6
- doc_ids: int32 [8, 256], P(('mirror', 'dp')), may hold values from 0 to 3, as said below
Outputs:
- input_grad: bfloat16 [8, 256, 4096], P(('mirror', 'dp'), 'tensor')
- qk_weight_grad: float32 [4096, 2, 4096], P(('mirror', 'dp'), None, 'tensor')
Inputs may be any that keep to these rules, and one draw needn't show every extreme that they name: `doc_ids`: within each sequence of 128 tokens the ids start at 0, never fall, and each of the four documents holds a multiple of 8 tokens.
All inputs are finite; a program needn't handle non-finite values.
Results may differ from a plain program's by a relative error of at most 0.023.
Values may be sent and summed in bfloat16 or wider, within the bound.
No kernel may reach another device: no remote copies, remote signals or barrier semaphores. Data moves between devices by JAX's collectives and lax.ppermute only.
A program may use at most 128 MiB of HBM per device.

v0:
```python
import math

import jax
import jax.numpy as jnp
from jax import lax
from jax.sharding import PartitionSpec as P

HD = 128
SEQ = 128


def rotate_pairs(values, cosine, sine_table):
    half = values.shape[-1] // 2
    first_half = values[..., :half]
    second_half = values[..., half:]
    cos_b = cosine[None, :, None, :]
    sin_b = sine_table[None, :, None, :]
    return jnp.concatenate(
        [first_half * cos_b - second_half * sin_b, second_half * cos_b + first_half * sin_b],
        axis=-1,
    )


def unrotate_pairs(values, cosine, sine_table):
    half = values.shape[-1] // 2
    first_half = values[..., :half]
    second_half = values[..., half:]
    cos_b = cosine[None, :, None, :]
    sin_b = sine_table[None, :, None, :]
    return jnp.concatenate(
        [first_half * cos_b + second_half * sin_b, second_half * cos_b - first_half * sin_b],
        axis=-1,
    )


def attention_grads(query_rows, key_rows, value_rows, grad_rows, doc_row):
    token_count, full_width = query_rows.shape
    head_count = full_width // HD
    micro_count = token_count // SEQ
    shape_four = (micro_count, SEQ, head_count, HD)
    positions = jnp.arange(SEQ).astype(jnp.float32)
    inverse = jnp.exp(-(2.0 * jnp.arange(HD // 2).astype(jnp.float32) / HD) * math.log(10000.0))
    angles = positions[:, None] * inverse[None, :]
    cosine = jnp.cos(angles)
    sine_table = jnp.sin(angles)
    q_rot = rotate_pairs(
        query_rows.reshape(shape_four).astype(jnp.float32), cosine, sine_table
    ).astype(jnp.bfloat16)
    k_rot = rotate_pairs(
        key_rows.reshape(shape_four).astype(jnp.float32), cosine, sine_table
    ).astype(jnp.bfloat16)
    scale = 1.0 / math.sqrt(HD)
    scores = jnp.einsum("bshd,bthd->bhst", q_rot, k_rot, preferred_element_type=jnp.float32) * scale
    docs = doc_row.reshape(micro_count, SEQ)
    index_seq = jnp.arange(SEQ)
    causal = index_seq[None, :] <= index_seq[:, None]
    allowed = causal[None, :, :] & (docs[:, :, None] == docs[:, None, :])
    scores = jnp.where(allowed[:, None, :, :], scores, -1e30)
    highest = jnp.max(scores, axis=-1, keepdims=True)
    exps = jnp.exp(scores - highest)
    probs = exps / jnp.sum(exps, axis=-1, keepdims=True)
    dprob = jnp.einsum(
        "bshd,bthd->bhst",
        grad_rows.reshape(shape_four),
        value_rows.reshape(shape_four),
        preferred_element_type=jnp.float32,
    )
    delta = jnp.sum(probs * dprob, axis=-1, keepdims=True)
    dscore = (probs * (dprob - delta)).astype(jnp.bfloat16)
    dq_rot = (
        jnp.einsum("bhst,bthd->bshd", dscore, k_rot, preferred_element_type=jnp.float32) * scale
    )
    dk_rot = (
        jnp.einsum("bhst,bshd->bthd", dscore, q_rot, preferred_element_type=jnp.float32) * scale
    )
    query_grad = (
        unrotate_pairs(dq_rot, cosine, sine_table)
        .astype(jnp.bfloat16)
        .reshape(token_count, full_width)
    )
    key_grad = (
        unrotate_pairs(dk_rot, cosine, sine_table)
        .astype(jnp.bfloat16)
        .reshape(token_count, full_width)
    )
    return (query_grad, key_grad)


def shards(layer_input, qk_weight, query_proj, key_proj, value_proj, head_grad, doc_ids):
    tensor_count = lax.axis_size("tensor")
    mirror_count = lax.axis_size("mirror")
    data_count = lax.axis_size("dp")
    replicas = mirror_count * data_count
    token_count = query_proj.shape[1]
    group_width = query_proj.shape[2]
    model_width = layer_input.shape[2]
    block_rows = model_width // replicas
    query_grad, key_grad = attention_grads(
        query_proj[0], key_proj[0], value_proj[0], head_grad[0], doc_ids[0]
    )
    grad_pair = jnp.concatenate([query_grad, key_grad], axis=1)
    weight_flat = qk_weight.reshape(model_width, 2 * group_width)
    summed_input = lax.psum_scatter(
        lax.dot_general(
            grad_pair, weight_flat, (((1,), (1,)), ((), ())), preferred_element_type=jnp.float32
        ).astype(jnp.bfloat16),
        "tensor",
        scatter_dimension=0,
        tiled=True,
    )
    input_grad = summed_input.reshape(1, token_count // tensor_count, model_width)
    gathered = lax.all_gather(layer_input, "tensor", axis=1, tiled=True)[0]
    own_columns = lax.all_to_all(
        gathered, ("mirror", "dp"), split_axis=1, concat_axis=0, tiled=True
    )
    piece_rows = lax.all_gather(grad_pair, ("mirror", "dp"), axis=0, tiled=True)
    row_count = piece_rows.shape[0]
    shard_count = row_count // token_count
    terms = jnp.einsum(
        "rti,rtc->ric",
        own_columns.reshape(shard_count, token_count, block_rows),
        piece_rows.reshape(shard_count, token_count, 2 * group_width),
        preferred_element_type=jnp.float32,
    )
    rounded = lax.optimization_barrier(terms.astype(jnp.bfloat16)).astype(jnp.float32)
    summed = jnp.sum(rounded, axis=0)
    weight_grad = (summed / replicas).reshape(block_rows, 2, group_width)
    return (input_grad, weight_grad)


def solution(mesh):
    in_specs = (
        P(("mirror", "dp"), "tensor", None),
        P(None, None, "tensor"),
        P(("mirror", "dp"), None, "tensor"),
        P(("mirror", "dp"), None, "tensor"),
        P(("mirror", "dp"), None, "tensor"),
        P(("mirror", "dp"), None, "tensor"),
        P(("mirror", "dp"), None),
    )
    out_specs = (P(("mirror", "dp"), "tensor", None), P(("mirror", "dp"), None, "tensor"))
    return jax.shard_map(shards, mesh=mesh, in_specs=in_specs, out_specs=out_specs, check_vma=False)
```

profile of v0, /device:TPU:0, one launch (start us, length us, event | category | flops | bytes accessed | tf_op | source)
XLA Modules:
  0.0 187.7 jit_solution(8540577315614197054)
XLA Ops:
  7.2 0.0 copy-start.2
  7.2 0.0 copy-start.3
  7.2 0.0 all-gather.5.cloned.1.call-start
  7.2 0.7 all-gather.5.cloned.1.call-update
  7.9 0.0 all-gather.3.cloned.1.call-start
  8.0 0.0 copy-start.4
  8.0 1.2 convert_bitcast_fusion.2
  9.2 0.0 copy-start.5
  9.2 0.2 copy.63
  9.4 0.0 copy-done.2
  9.5 0.1 convert_bitcast_fusion.1
  9.6 0.2 copy.64
  9.8 0.0 copy-done.3
  9.8 0.9 copy.66
  10.7 0.0 copy-done.4
  10.7 0.9 copy.65
  11.6 0.0 copy-done.5
  11.6 0.1 compare_and_fusion
  11.7 0.7 fusion.18
  12.4 0.3 multiply_cosine_fusion
  12.7 0.8 subtract_convert_fusion.3
  13.5 0.9 fusion.20
  14.4 1.7 multiply_reduce_fusion
  16.1 0.2 multiply_convert_fusion
  16.3 0.5 fusion.4
  16.8 0.6 fusion.5
  17.3 0.8 add_convert_fusion
  18.1 0.3 pad_maximum_fusion.2
  18.4 0.3 copy.43
  18.8 0.3 pad_maximum_fusion.3
  19.1 0.3 copy.47
  19.4 0.1 bitcast_dynamic-update-slice_fusion.1
  19.5 0.1 bitcast_dynamic-update-slice_fusion
  19.6 0.0 copy-start
  19.6 1.0 copy-done
  20.6 0.0 all-gather.3.cloned.1.call-update
  20.6 17.2 %copy.69 = bf16[512,8,2,1024]{3,1,2,0:T(8,128)(2,1)} copy(bf16[512,8,2,1024]{3,2,1,0:T(2,128)(2,1)} %bitcast.47) | data formatting | bytes 33554432
  37.8 20.5 %all-gather.5.cloned.1.call-done = bf16[1,256,4096]{2,1,0:T(8,128)(2,1)} async-done(((bf16[1,64,4096]{2,1,0:T(8,128)(2,1)}), bf16[1,256,4096]{2,1,0:T(8,128)(2,1)}) %all-gather.5.cloned.1.call-update) | async-done | bytes 2097168 | tf_op jit(solution)/shard_map/all_gather | solution.py:112
  58.3 3.3 %copy.48 = bf16[1,256,4096]{1,2,0:T(8,128)(2,1)S(1)} copy(bf16[1,256,4096]{2,1,0:T(8,128)(2,1)} %all-gather.5.cloned.1.call-done) | data formatting | bytes 4194304 | tf_op jit(solution)/shard_map/all_gather | solution.py:112
  61.5 0.0 copy-start.1
  61.5 2.4 %copy.49 = bf16[256,8,512]{2,0,1:T(8,128)(2,1)} copy(bf16[256,8,512]{0,2,1:T(8,128)(2,1)S(1)} %bitcast.53) | data formatting | bytes 4194304 | tf_op jit(solution)/shard_map/all_to_all | solution.py:113
  63.9 3.6 %all-to-all-start = ((bf16[256,8,512]{2,0,1:T(8,128)(2,1)}), bf16[256,8,512]{2,0,1:T(8,128)(2,1)S(1)}, u32[]{:S(2)}, u32[]{:S(2)}) async-start(bf16[256,8,512]{2,0,1:T(8,128)(2,1)} %copy.49), calls=%async_computation.1 | async-start | bytes 4194304 | tf_op jit(solution)/shard_map/all_to_all | solution.py:113
  67.6 0.2 reduce-scatter.2.cloned.1.call-start
  67.8 0.0 copy-done.1
  67.8 18.1 %convolution_convert_fusion = bf16[256,4096]{1,0:T(8,128)(2,1)} fusion(bf16[256,2048]{1,0:T(8,128)(2,1)S(1)} %copy-done.1, bf16[4096,2048]{1,0:T(8,128)(2,1)} %bitcast.48), kind=kOutput, calls=%fused_computation.3 | convolution fusion | flops 4296015872 | bytes 19922944 | tf_op jit(solution)/shard_map/dot_general | solution.py:104
  86.0 0.0 reduce-scatter.2.cloned.1.call-update
  86.0 17.8 %all-to-all-done = bf16[256,8,512]{2,0,1:T(8,128)(2,1)S(1)} async-done(((bf16[256,8,512]{2,0,1:T(8,128)(2,1)}), bf16[256,8,512]{2,0,1:T(8,128)(2,1)S(1)}, u32[]{:S(2)}, u32[]{:S(2)}) %all-to-all-start) | async-done | bytes 2097184 | tf_op jit(solution)/shard_map/all_to_all | solution.py:113
  103.8 30.7 %all-gather.3.cloned.1.call-done = bf16[2048,2048]{1,0:T(8,128)(2,1)} async-done(((bf16[256,2048]{1,0:T(8,128)(2,1)}), bf16[2048,2048]{1,0:T(8,128)(2,1)}) %all-gather.3.cloned.1.call-update) | async-done | bytes 8388624 | tf_op jit(solution)/shard_map/all_gather | solution.py:116
  134.4 10.6 %convert_bitcast_fusion = bf16[8,512,2048]{1,2,0:T(8,128)(2,1)} fusion(bf16[8,256,2048]{2,1,0:T(8,128)(2,1)} %bitcast.50, bf16[256,8,512]{2,0,1:T(8,128)(2,1)S(1)} %all-to-all-done), kind=kOutput, calls=%fused_computation.2 | convolution fusion | flops 4303355904 | bytes 27262976 | tf_op jit(solution)/shard_map/rti,rtc->ric/dot_general | solution.py:119
  145.0 7.1 %convert_reduce_fusion = f32[512,2048]{0,1:T(8,128)S(1)} fusion(bf16[8,512,2048]{1,2,0:T(8,128)(2,1)} %convert_bitcast_fusion), kind=kLoop, calls=%fused_computation.1 | loop fusion | flops 15728640 | bytes 20971520 | tf_op jit(solution)/shard_map/reduce_sum | solution.py:126
  152.1 2.4 %broadcast_multiply_fusion = f32[512,2048]{0,1:T(8,128)} fusion(f32[512,2048]{0,1:T(8,128)S(1)} %convert_reduce_fusion), kind=kLoop, calls=%fused_computation.5 | loop fusion | flops 1048576 | bytes 8388608 | tf_op jit(solution)/shard_map/div | solution.py:127
  154.5 7.3 %copy.51 = f32[512,2,1024]{2,1,0:T(2,128)} copy(f32[512,2,1024]{0,2,1:T(8,128)} %bitcast.49) | data formatting | bytes 8388608
  161.8 19.4 %reduce-scatter.2.cloned.1.call-done = bf16[64,4096]{1,0:T(8,128)(2,1)} async-done(((bf16[256,4096]{1,0:T(8,128)(2,1)}), bf16[64,4096]{1,0:T(8,128)(2,1)}) %reduce-scatter.2.cloned.1.call-update) | async-done | bytes 524304 | tf_op jit(solution)/shard_map/reduce_scatter | solution.py:103
  (3 shorter events, 0.0 us)
Async XLA Ops:
  7.2 2.3 %copy-start.2 = (bf16[1,256,1024]{2,1,0:T(8,128)(2,1)S(1)}, bf16[1,256,1024]{2,1,0:T(8,128)(2,1)}, u32[]{:S(2)}) copy-start(bf16[1,256,1024]{2,1,0:T(8,128)(2,1)} %param.9) | copy-start | bytes 1572868
  7.2 2.6 %copy-start.3 = (bf16[1,256,1024]{2,1,0:T(8,128)(2,1)S(1)}, bf16[1,256,1024]{2,1,0:T(8,128)(2,1)}, u32[]{:S(2)}) copy-start(bf16[1,256,1024]{2,1,0:T(8,128)(2,1)} %param.11) | copy-start | bytes 1572868
  7.2 51.1 %all-gather.5.cloned.1.call-start = ((), (), s32[]{:S(2)}) async-start(), calls=%async_computation.4 | async-start | bytes 2621440 | tf_op jit(solution)/shard_map/all_gather | solution.py:112
  7.9 126.5 %all-gather.3.cloned.1.call-start = ((), (), s32[]{:S(2)}) async-start(), calls=%async_computation.3 | async-start | bytes 9437184 | tf_op jit(solution)/shard_map/all_gather | solution.py:116
  8.0 2.7 %copy-start.4 = (bf16[1,256,1024]{2,1,0:T(8,128)(2,1)S(1)}, bf16[1,256,1024]{2,1,0:T(8,128)(2,1)}, u32[]{:S(2)}) copy-start(bf16[1,256,1024]{2,1,0:T(8,128)(2,1)} %param.12) | copy-start | bytes 1572868
  9.2 2.4 %copy-start.5 = (s32[1,256]{1,0:T(1,128)S(1)}, s32[1,256]{1,0:T(1,128)}, u32[]{:S(2)}) copy-start(s32[1,256]{1,0:T(1,128)} %param.13) | copy-start | bytes 3076
  19.6 1.0 copy-start
  61.5 6.3 %copy-start.1 = (bf16[256,2048]{1,0:T(8,128)(2,1)S(1)}, bf16[256,2048]{1,0:T(8,128)(2,1)}, u32[]{:S(2)}) copy-start(bf16[256,2048]{1,0:T(8,128)(2,1)} %copy-done) | copy-start | bytes 3145732
  63.9 39.8 %all-to-all-start = ((bf16[256,8,512]{2,0,1:T(8,128)(2,1)}), bf16[256,8,512]{2,0,1:T(8,128)(2,1)S(1)}, u32[]{:S(2)}, u32[]{:S(2)}) async-start(bf16[256,8,512]{2,0,1:T(8,128)(2,1)} %copy.49), calls=%async_computation.1 | async-start | bytes 4194304 | tf_op jit(solution)/shard_map/all_to_all | solution.py:113
  67.6 113.6 %reduce-scatter.2.cloned.1.call-start = ((), (), s32[]{:S(2)}) async-start(), calls=%async_computation.2 | async-start | bytes 2621440 | tf_op jit(solution)/shard_map/reduce_scatter | solution.py:103
Sparse Core Ops, SparseCore 0:
  9.6 48.6 all-gather.4
  60.1 74.2 all-gather.2
  137.3 43.8 reduce-scatter.1
where the time goes:
time: 188 us
  waiting for transfers between devices  89 us (47%)
  local copies, waits for them, and re-layouts  34.8 us (19%)
  matrix products  32.3 us (17%)
  between operations  14 us (7%)
  other arithmetic  13.7 us (7%)
  starting transfers between devices  3.94 us (2%)
    all_gather x1, waiting for transfers between devices, shards(): piece_rows = lax.all_gather(grad_pair, ('mirror', 'dp'), axis=0, tiled=True)  30.7 us
    unnamed x19, local copies, waits for them, and re-layouts  27.7 us
    all_gather x1, waiting for transfers between devices, shards(): gathered = lax.all_gather(layer_input, 'tensor', axis=1, tiled=True)[0]  20.5 us
    reduce_scatter x1, waiting for transfers between devices, shards(): lax.psum_scatter(lax.dot_general(grad_pair, weight_flat, (((1,), (1,)), (...  19.4 us
    dot_general x1, matrix products, shards(): lax.dot_general(grad_pair, weight_flat, (((1,), (1,)), ((), ())), preferr...  18.1 us
    all_to_all x1, waiting for transfers between devices, shards(): lax.all_to_all(gathered, ('mirror', 'dp'), split_axis=1, concat_axis=0, t...  17.8 us
    dot_general x1, matrix products, shards(): jnp.einsum('rti,rtc->ric', own_columns.reshape(shard_count, token_count,...  10.6 us
    reduce_sum x1, other arithmetic, shards(): summed = jnp.sum(rounded, axis=0)  7.07 us
  transfers between devices with their start and end apart: 4, of which 4 were waited for; matrix products, arithmetic and copies ran while one was open for 43% of the time, Pallas kernels for 0%

commit v1 on v0

v1 whole, which is shorter than its diff:
```python
import functools
import math

import jax
import jax.numpy as jnp
import numpy as np
from jax import lax
from jax.experimental import pallas as pl
from jax.experimental.pallas import tpu as pltpu
from jax.sharding import PartitionSpec as P

HD = 128
SEQ = 128
VMEM_LIMIT = 48 << 20
ROWS = (((1,), (1,)), ((), ()))
COLS = (((0,), (0,)), ((), ()))


def rope_tables():
    half = HD // 2
    inverse = np.exp(-(np.float32(2.0) * np.arange(half, dtype=np.float32) / np.float32(HD)) * np.float32(math.log(10000.0)))
    angles = np.arange(SEQ, dtype=np.float32)[:, None] * inverse[None, :].astype(np.float32)
    cosine, sine = np.cos(angles), np.sin(angles)
    return np.concatenate([cosine, cosine], axis=1), np.concatenate([-sine, sine], axis=1)


def attention_kernel(doc_ref, cos_ref, sin_ref, q_ref, k_ref, v_ref, h_ref, qg_ref, kg_ref):
    cosine, sine = cos_ref[...], sin_ref[...]
    scale = 1.0 / math.sqrt(HD)
    keys = lax.broadcast_in_dim(doc_ref[0], (SEQ, SEQ), (0, 1))
    row = lax.broadcasted_iota(jnp.int32, (SEQ, SEQ), 0)
    col = lax.broadcasted_iota(jnp.int32, (SEQ, SEQ), 1)
    allowed = (col <= row) & (keys == keys.T)

    def rope(values):
        values = values.astype(jnp.float32)
        return (values * cosine + pltpu.roll(values, HD // 2, 1) * sine).astype(jnp.bfloat16)

    def unrope(values):
        values = values * scale
        return (values * cosine - pltpu.roll(values, HD // 2, 1) * sine).astype(jnp.bfloat16)

    for head in range(q_ref.shape[1] // HD):
        at = slice(head * HD, (head + 1) * HD)
        q_rot, k_rot = rope(q_ref[:, at]), rope(k_ref[:, at])
        scores = lax.dot_general(q_rot, k_rot, ROWS, preferred_element_type=jnp.float32) * scale
        scores = jnp.where(allowed, scores, -1e30)
        exps = jnp.exp(scores - jnp.max(scores, axis=1, keepdims=True))
        probs = exps / jnp.sum(exps, axis=1, keepdims=True)
        dprob = lax.dot_general(h_ref[:, at], v_ref[:, at], ROWS, preferred_element_type=jnp.float32)
        delta = jnp.sum(probs * dprob, axis=1, keepdims=True)
        dscore = (probs * (dprob - delta)).astype(jnp.bfloat16)
        qg_ref[:, at] = unrope(jnp.dot(dscore, k_rot, preferred_element_type=jnp.float32))
        kg_ref[:, at] = unrope(lax.dot_general(dscore, q_rot, COLS, preferred_element_type=jnp.float32))


def attention_grads(query, key, value, grad, docs):
    tokens, width = query.shape
    micro = tokens // SEQ
    split = 2 if (width // HD) % 2 == 0 else 1
    cosine, sine = rope_tables()
    table = pl.BlockSpec((SEQ, HD), lambda b, h: (0, 0))
    block = pl.BlockSpec((SEQ, width // split), lambda b, h: (b, h))
    return pl.pallas_call(
        attention_kernel,
        grid=(micro, split),
        in_specs=[pl.BlockSpec((1, 1, SEQ), lambda b, h: (b, 0, 0)), table, table] + [block] * 4,
        out_specs=[block, block],
        out_shape=[jax.ShapeDtypeStruct((tokens, width), jnp.bfloat16)] * 2,
        compiler_params=pltpu.CompilerParams(vmem_limit_bytes=VMEM_LIMIT),
        name="attention_grads",
    )(docs.reshape(micro, 1, SEQ), cosine, sine, query, key, value, grad)


def partials_kernel(qg_ref, kg_ref, w_ref, out_ref):
    depth, _, width = w_ref.shape
    weights = w_ref[...].reshape(depth, 2 * width)
    rows = lax.dot_general(qg_ref[...], weights[:, :width], ROWS, preferred_element_type=jnp.float32)
    rows = rows + lax.dot_general(kg_ref[...], weights[:, width:], ROWS, preferred_element_type=jnp.float32)
    out_ref[...] = rows.astype(jnp.bfloat16).reshape(out_ref.shape)


def input_partials(query_grad, key_grad, weight, owners, blocks):
    tokens, width = query_grad.shape
    model = weight.shape[0]
    columns = model // blocks
    depth = min(512, columns)
    per = columns // depth
    grads = pl.BlockSpec((tokens, width), lambda j: (0, 0))
    return pl.pallas_call(
        partials_kernel,
        grid=(model // depth,),
        in_specs=[grads, grads, pl.BlockSpec((depth, 2, width), lambda j: (j, 0, 0))],
        out_specs=pl.BlockSpec((owners, 1, tokens // owners, depth), lambda j: (0, j // per, 0, j % per)),
        out_shape=jax.ShapeDtypeStruct((owners, blocks, tokens // owners, columns), jnp.bfloat16),
        compiler_params=pltpu.CompilerParams(vmem_limit_bytes=VMEM_LIMIT),
        name="input_partials",
    )(query_grad, key_grad, weight)


def split_kernel(index_ref, x_ref, *out_refs):
    mirrors = index_ref.shape[0] - 1
    data_count = len(out_refs)
    width = x_ref.shape[1] // (mirrors * data_count)
    for distance, out_ref in enumerate(out_refs):
        owner = index_ref[mirrors] ^ distance
        for k in range(mirrors):
            start = pl.multiple_of((index_ref[k] * data_count + owner) * width, width)
            out_ref[:, k * width : (k + 1) * width] = x_ref[:, pl.ds(start, width)]


def split_columns(rows, mirrors, data_count):
    mirror = lax.axis_index("mirror")
    index = jnp.stack([(mirror + k) % mirrors for k in range(mirrors)] + [lax.axis_index("dp")])
    tokens, model = rows.shape
    out = jax.ShapeDtypeStruct((tokens, model // data_count), rows.dtype)
    return pl.pallas_call(
        split_kernel,
        in_specs=[pl.BlockSpec(memory_space=pltpu.SMEM), pl.BlockSpec(memory_space=pltpu.VMEM)],
        out_specs=[pl.BlockSpec(memory_space=pltpu.VMEM)] * data_count,
        out_shape=[out] * data_count,
        name="split_columns",
    )(index.astype(jnp.int32), rows)


def swap(values, distance, size):
    return lax.ppermute(values, "dp", [(i, i ^ distance) for i in range(size)])


def gathered(block, bits, size):
    blocks = {0: block}
    for bit in bits:
        blocks.update({d ^ bit: swap(b, bit, size) for d, b in list(blocks.items())})
    return [blocks[d] for d in range(size)]


def shards(layer_input, qk_weight, query_proj, key_proj, value_proj, head_grad, doc_ids):
    owners = lax.axis_size("tensor")
    mirrors = lax.axis_size("mirror")
    data_count = lax.axis_size("dp")
    tokens, width = query_proj.shape[1:]
    model = layer_input.shape[2]
    block_rows = model // (mirrors * data_count)
    own_tokens = tokens // owners
    me = lax.axis_index("tensor")

    columns = split_columns(layer_input[0], mirrors, data_count)
    columns = [columns[0]] + [swap(columns[d], d, data_count) for d in range(1, data_count)]
    piece = jnp.concatenate(columns, axis=0)

    query_grad, key_grad = attention_grads(
        query_proj[0], key_proj[0], value_proj[0], head_grad[0], doc_ids[0]
    )
    bits = [1 << b for b in range(data_count.bit_length() - 1)]
    query_all = gathered(query_grad, bits, data_count)
    key_all = gathered(key_grad, bits[1:] + bits[:1], data_count)

    partials = input_partials(query_grad, key_grad, qk_weight, owners, data_count)
    partials = partials.reshape(owners, *piece.shape)

    right = [(i, i + 1) for i in range(owners - 1)]
    left = [(i + 1, i) for i in range(owners - 1)]
    from_left, from_right = [piece], [piece]
    for slot in range(1, owners + 1):
        send_right, send_left = from_left[-1], from_right[-1]
        if slot > 1:
            ahead = owners - slot + 1
            term = lax.dynamic_index_in_dim(partials, jnp.minimum(me + ahead, owners - 1), 0, False)
            send_right = send_right + jnp.where(me + ahead < owners, term, jnp.zeros_like(term))
            term = lax.dynamic_index_in_dim(partials, jnp.maximum(me - ahead, 0), 0, False)
            send_left = send_left + jnp.where(me - ahead >= 0, term, jnp.zeros_like(term))
        from_left.append(lax.ppermute(send_right, "tensor", right))
        from_right.append(lax.ppermute(send_left, "tensor", left))
    own = lax.dynamic_index_in_dim(partials, me, 0, False).astype(jnp.float32)
    own = own + from_left[owners].astype(jnp.float32) + from_right[owners].astype(jnp.float32)
    own = own.astype(jnp.bfloat16).reshape(data_count, own_tokens, model // data_count)
    input_grad = jnp.swapaxes(own, 0, 1).reshape(1, own_tokens, model)

    pieces = [piece] + [
        jnp.where(me >= t, from_left[t], from_right[owners - t]) for t in range(1, owners)
    ]
    stacked = jnp.stack(pieces)
    stacked = jnp.take(stacked, (me - jnp.arange(owners)) % owners, axis=0)
    stacked = stacked.reshape(owners, data_count, own_tokens, mirrors * block_rows)
    inputs = jnp.swapaxes(stacked, 0, 1).reshape(data_count * tokens, mirrors * block_rows)

    halves = []
    for blocks in (query_all, key_all):
        grads = jnp.concatenate(blocks, axis=0)
        total = lax.dot_general(inputs, grads, COLS, preferred_element_type=jnp.float32)
        half = total[:block_rows]
        for k in range(1, mirrors):
            away = total[k * block_rows : (k + 1) * block_rows].astype(jnp.bfloat16)
            away = lax.ppermute(away, "mirror", [(i, (i + k) % mirrors) for i in range(mirrors)])
            half = half + away.astype(jnp.float32)
        halves.append(half / (mirrors * data_count))
    weight_grad = jnp.stack(halves, axis=1)
    return (input_grad, weight_grad)


def solution(mesh):
    in_specs = (
        P(("mirror", "dp"), "tensor", None),
        P(None, None, "tensor"),
        P(("mirror", "dp"), None, "tensor"),
        P(("mirror", "dp"), None, "tensor"),
        P(("mirror", "dp"), None, "tensor"),
        P(("mirror", "dp"), None, "tensor"),
        P(("mirror", "dp"), None),
    )
    out_specs = (P(("mirror", "dp"), "tensor", None), P(("mirror", "dp"), None, "tensor"))
    return jax.shard_map(shards, mesh=mesh, in_specs=in_specs, out_specs=out_specs, check_vma=False)
```

time: 188 us -> 129 us (0.69)
  waiting for transfers between devices: 89 us -> 22 us
  starting transfers between devices: 3.94 us -> 32.8 us
  matrix products: 32.3 us -> 8.02 us
  Pallas kernels: 0 us -> 21.9 us
  between operations: 14 us -> 0.89 us
  local copies, waits for them, and re-layouts: 34.8 us -> 24.9 us
  other arithmetic: 13.7 us -> 17.1 us
    all_gather x2 -> x0, waiting for transfers between devices: 51.2 us -> none  [the longest x1 30.7 us: shards(): piece_rows = lax.all_gather(grad_pair, ('mirror', 'dp'), axis=0, tiled=True)]
    ppermute x0 -> x19, starting transfers between devices: none -> 32.8 us  [the longest x4 18.3 us: shards(): from_left.append(lax.ppermute(send_right, 'tensor', right))]
    dot_general x5 -> x2, matrix products: 31.4 us -> 8.02 us  [shards(): lax.dot_general(inputs, grads, COLS, preferred_element_type=jnp.float32)]
    ppermute x0 -> x19, waiting for transfers between devices: none -> 22 us  [the longest x4 9.78 us: shards(): from_right.append(lax.ppermute(send_left, 'tensor', left))]
    pallas_call x0 -> x3, Pallas kernels: none -> 21.9 us  [the longest x1 11.6 us: input_partials(): pl.pallas_call(partials_kernel, grid=(model // depth,), in_specs=[grads,...]
    reduce_scatter x1 -> x0, waiting for transfers between devices: 19.4 us -> none  [shards(): lax.psum_scatter(lax.dot_general(grad_pair, weight_flat, (((1,), (1,)), (...]
    all_to_all x1 -> x0, waiting for transfers between devices: 17.8 us -> none  [shards(): lax.all_to_all(gathered, ('mirror', 'dp'), split_axis=1, concat_axis=0, t...]
    unnamed x19 -> x26, local copies, waits for them, and re-layouts: 27.7 us -> 16.5 us
  transfers between devices with their start and end apart: 4 -> 19, of which waited for: 4 -> 6; matrix products, arithmetic and copies ran while one was open for 43% -> 25% of each run, Pallas kernels for 0% -> 16%
where the time goes in v1:
time: 129 us; the launch traced here: 128 us
  starting transfers between devices  32.8 us (25%)
  local copies, waits for them, and re-layouts  24.9 us (19%)
  waiting for transfers between devices  22 us (17%)
  Pallas kernels  21.9 us (17%)
  other arithmetic  17.1 us (13%)
  matrix products  8.02 us (6%)
    ppermute x4, starting transfers between devices, shards(): from_left.append(lax.ppermute(send_right, 'tensor', right))  18.3 us
    unnamed x26, local copies, waits for them, and re-layouts  16.5 us
    pallas_call x1, Pallas kernels, input_partials(): pl.pallas_call(partials_kernel, grid=(model // depth,), in_specs=[grads,...  11.6 us
    ppermute x4, waiting for transfers between devices, shards(): from_right.append(lax.ppermute(send_left, 'tensor', left))  9.78 us
    ppermute x9, starting transfers between devices, swap(): return lax.ppermute(values, 'dp', [(i, i ^ distance) for i in range(size)])  9.25 us
    pallas_call x1, Pallas kernels, attention_grads(): pl.pallas_call(attention_kernel, grid=(micro, split), in_specs=[pl.BlockS...  8.42 us
    dot_general x2, matrix products, shards(): lax.dot_general(inputs, grads, COLS, preferred_element_type=jnp.float32)  8.02 us
    ppermute x4, waiting for transfers between devices, shards(): from_left.append(lax.ppermute(send_right, 'tensor', right))  7.98 us
  transfers between devices with their start and end apart: 19, of which 6 were waited for; matrix products, arithmetic and copies ran while one was open for 25% of the time, Pallas kernels for 16%

profile of v1, /device:TPU:0, one launch (start us, length us, event | category | flops | bytes accessed | tf_op | source)
XLA Modules:
  0.0 127.6 jit_solution(14628123364241004119)
XLA Ops:
  0.6 0.6 pad_add_fusion.index_ref
  1.3 1.9 %split_columns.1 = (bf16[64,1024]{1,0:T(8,128)(2,1)}, bf16[64,1024]{1,0:T(8,128)(2,1)}, bf16[64,1024]{1,0:T(8,128)(2,1)}, bf16[64,1024]{1,0:T(8,128)(2,1)}) custom-call(s32[3]{0:T(128)} %pad_add_fusion.index_ref, bf16[64,4096]{1,0:T(8,128)(2,1)} %bitcast.60), custom_call_target="tpu_custom_call" | custom-call | tf_op jit(solution)/shard_map/split_columns/pallas_call | solution.py:117
  3.1 2.9 %collective-permute-start = (bf16[64,1024]{1,0:T(8,128)(2,1)}, bf16[64,1024]{1,0:T(8,128)(2,1)S(1)}, u32[]{:S(2)}, u32[]{:S(2)}) collective-permute-start(bf16[64,1024]{1,0:T(8,128)(2,1)} %get-tuple-element.11), channel_id=1, source_target_pairs={{0,1},{1,0},{2,3},{3,2},{4,5},{5,4},{6,7},{7,6},{8,9},{9,8},{10,11... | collective-permute-start | bytes 393224 | tf_op jit(solution)/shard_map/ppermute | solution.py:127
  6.1 1.5 %collective-permute-start.1 = (bf16[64,1024]{1,0:T(8,128)(2,1)}, bf16[64,1024]{1,0:T(8,128)(2,1)S(1)}, u32[]{:S(2)}, u32[]{:S(2)}) collective-permute-start(bf16[64,1024]{1,0:T(8,128)(2,1)} %get-tuple-element.12), channel_id=1, source_target_pairs={{0,2},{1,3},{2,0},{3,1},{4,6},{5,7},{6,4},{7,5},{8,10},{9,11},{10,... | collective-permute-start | bytes 393224 | tf_op jit(solution)/shard_map/ppermute | solution.py:127
  7.6 0.0 collective-permute-start.2
  7.6 1.6 %constant_dynamic-update-slice_fusion.3 = bf16[256,1024]{1,0:T(8,128)(2,1)} fusion(bf16[64,1024]{1,0:T(8,128)(2,1)} %get-tuple-element.10), kind=kLoop, calls=%fused_computation.43 | loop fusion | bytes 262144
  9.2 1.1 collective-permute-done
  10.3 0.7 constant_dynamic-update-slice_fusion.2
  11.0 3.1 %collective-permute-done.1 = bf16[64,1024]{1,0:T(8,128)(2,1)S(1)} collective-permute-done((bf16[64,1024]{1,0:T(8,128)(2,1)}, bf16[64,1024]{1,0:T(8,128)(2,1)S(1)}, u32[]{:S(2)}, u32[]{:S(2)}) %collective-permute-start.1) | collective-permute-done | bytes 131104 | tf_op jit(solution)/shard_map/ppermute | solution.py:127
  14.1 0.7 constant_dynamic-update-slice_fusion.1
  14.7 0.7 constant_dynamic-update-slice_fusion
  15.4 4.3 %collective-permute-start.3 = (bf16[256,1024]{1,0:T(8,128)(2,1)}, bf16[256,1024]{1,0:T(8,128)(2,1)}, u32[]{:S(2)}, u32[]{:S(2)}) collective-permute-start(bf16[256,1024]{1,0:T(8,128)(2,1)} %constant_dynamic-update-slice_fusion), channel_id=1, source_target_pairs={{0,8},{8,16},{16,24},{1,9},{9,17},{17,25},{2,10},{10,18},{18,26},{... | collective-permute-start | bytes 1572872 | tf_op jit(solution)/shard_map/ppermute | solution.py:172
  19.7 1.3 %collective-permute-start.7 = (bf16[256,1024]{1,0:T(8,128)(2,1)}, bf16[256,1024]{1,0:T(8,128)(2,1)}, u32[]{:S(2)}, u32[]{:S(2)}) collective-permute-start(bf16[256,1024]{1,0:T(8,128)(2,1)} %constant_dynamic-update-slice_fusion), channel_id=1, source_target_pairs={{8,0},{16,8},{24,16},{9,1},{17,9},{25,17},{10,2},{18,10},{26,18},{... | collective-permute-start | bytes 1572872 | tf_op jit(solution)/shard_map/ppermute | solution.py:173
  21.0 0.0 copy-start
  21.0 1.0 copy-done
  22.0 1.0 copy-done.1
  23.1 1.0 copy-done.2
  24.1 1.0 copy-done.3
  25.1 0.8 copy-done.4
  26.0 0.8 copy-done.5
  26.8 0.7 copy-done.6
  27.5 8.4 %attention_grads.1 = (bf16[256,1024]{1,0:T(8,128)(2,1)S(1)}, bf16[256,1024]{1,0:T(8,128)(2,1)S(1)}) custom-call(s32[2,1,128]{2,1,0:T(1,128)S(1)} %bitcast.55, f32[128,128]{1,0:T(8,128)S(1)} %copy-done.4, f32[128,128]{1,0:T(8,128)S(1)} %copy-done.5, bf16[256,1024]{1,0:T(8,128)(2,1)S(1)} %bitcast.51, bf16[256,1024]{1,0:T(8,128)(2,1)S(1)} %bitcast.52, ...), custom_call_target="tpu_custom_call" | custom-call | tf_op jit(solution)/shard_map/attention_grads/pallas_call | solution.py:64
  35.9 11.6 %input_partials.1 = bf16[4,4,64,1024]{3,2,1,0:T(8,128)(2,1)S(1)} custom-call(bf16[256,1024]{1,0:T(8,128)(2,1)S(1)} %get-tuple-element.8.qg_ref, bf16[256,1024]{1,0:T(8,128)(2,1)S(1)} %get-tuple-element.9.kg_ref, bf16[4096,2,1024]{2,1,0:T(2,128)(2,1)} %w_ref.1), custom_call_target="tpu_custom_call" | custom-call | tf_op jit(solution)/shard_map/input_partials/pallas_call | solution.py:90
  47.6 0.0 collective-permute-done.3
  47.6 2.3 %bitcast_add_fusion.5 = (bf16[256,1024]{1,0:T(8,128)(2,1)}, bf16[256,1024]{1,0:T(8,128)(2,1)}) fusion(bf16[256,1024]{1,0:T(8,128)(2,1)} %collective-permute-done.3, bf16[4,256,1024]{2,1,0:T(8,128)(2,1)S(1)} %bitcast.47, s32[]{:T(128)S(6)} %select_n.143, pred[]{:T(512)S(6)} %lt.61, bf16[256,1024]{1,0:T(8,128)(2,1)} %collective-permute-done.7, s32[]{:T(128)S(6)} %max.9, ...), kind=kLoop, calls=%fused_computation.36 | loop fusion | flops 1048576 | bytes 3145738 | tf_op jit(solution)/shard_map/add | solution.py:169
  49.9 5.3 %collective-permute-start.4 = (bf16[256,1024]{1,0:T(8,128)(2,1)}, bf16[256,1024]{1,0:T(8,128)(2,1)}, u32[]{:S(2)}, u32[]{:S(2)}) collective-permute-start(bf16[256,1024]{1,0:T(8,128)(2,1)} %get-tuple-element.22), channel_id=1, source_target_pairs={{0,8},{8,16},{16,24},{1,9},{9,17},{17,25},{2,10},{10,18},{18,26},{... | collective-permute-start | bytes 1572872 | tf_op jit(solution)/shard_map/ppermute | solution.py:172
  55.2 1.3 %collective-permute-start.8 = (bf16[256,1024]{1,0:T(8,128)(2,1)}, bf16[256,1024]{1,0:T(8,128)(2,1)}, u32[]{:S(2)}, u32[]{:S(2)}) collective-permute-start(bf16[256,1024]{1,0:T(8,128)(2,1)} %get-tuple-element.23), channel_id=1, source_target_pairs={{8,0},{16,8},{24,16},{9,1},{17,9},{25,17},{10,2},{18,10},{26,18},{... | collective-permute-start | bytes 1572872 | tf_op jit(solution)/shard_map/ppermute | solution.py:173
  56.5 1.6 %collective-permute-start.16 = (bf16[256,1024]{1,0:T(8,128)(2,1)S(1)}, bf16[256,1024]{1,0:T(8,128)(2,1)}, u32[]{:S(2)}, u32[]{:S(2)}) collective-permute-start(bf16[256,1024]{1,0:T(8,128)(2,1)S(1)} %get-tuple-element.9.kg_ref), channel_id=1, source_target_pairs={{0,2},{1,3},{2,0},{3,1},{4,6},{5,7},{6,4},{7,5},{8,10},{9,11},{10,... | collective-permute-start | bytes 1572872 | tf_op jit(solution)/shard_map/ppermute | solution.py:127
  58.0 0.5 collective-permute-start.11
  58.6 4.8 %collective-permute-done.4 = bf16[256,1024]{1,0:T(8,128)(2,1)} collective-permute-done((bf16[256,1024]{1,0:T(8,128)(2,1)}, bf16[256,1024]{1,0:T(8,128)(2,1)}, u32[]{:S(2)}, u32[]{:S(2)}) %collective-permute-start.4) | collective-permute-done | bytes 524320 | tf_op jit(solution)/shard_map/ppermute | solution.py:172
  63.4 4.9 %collective-permute-done.8 = bf16[256,1024]{1,0:T(8,128)(2,1)} collective-permute-done((bf16[256,1024]{1,0:T(8,128)(2,1)}, bf16[256,1024]{1,0:T(8,128)(2,1)}, u32[]{:S(2)}, u32[]{:S(2)}) %collective-permute-start.8) | collective-permute-done | bytes 524320 | tf_op jit(solution)/shard_map/ppermute | solution.py:173
  68.2 2.4 %bitcast_add_fusion.4 = (bf16[256,1024]{1,0:T(8,128)(2,1)}, bf16[256,1024]{1,0:T(8,128)(2,1)}, bf16[1,256,1024]{2,1,0:T(8,128)(2,1)}) fusion(bf16[256,1024]{1,0:T(8,128)(2,1)} %collective-permute-done.4, bf16[4,256,1024]{2,1,0:T(8,128)(2,1)S(1)} %bitcast.48, s32[]{:T(128)S(6)} %select_n.147, pred[]{:T(512)S(6)} %lt.63, ...), kind=kLoop, calls=%fused_computation.35 | loop fusion | flops 1310720 | bytes 3670027 | tf_op jit(solution)/shard_map/add | solution.py:169
  70.6 3.3 %collective-permute-start.5 = (bf16[256,1024]{1,0:T(8,128)(2,1)}, bf16[256,1024]{1,0:T(8,128)(2,1)}, u32[]{:S(2)}, u32[]{:S(2)}) collective-permute-start(bf16[256,1024]{1,0:T(8,128)(2,1)} %get-tuple-element.20), channel_id=1, source_target_pairs={{0,8},{8,16},{16,24},{1,9},{9,17},{17,25},{2,10},{10,18},{18,26},{... | collective-permute-start | bytes 1572872 | tf_op jit(solution)/shard_map/ppermute | solution.py:172
  74.0 1.3 %collective-permute-start.9 = (bf16[256,1024]{1,0:T(8,128)(2,1)}, bf16[256,1024]{1,0:T(8,128)(2,1)}, u32[]{:S(2)}, u32[]{:S(2)}) collective-permute-start(bf16[256,1024]{1,0:T(8,128)(2,1)} %get-tuple-element.21), channel_id=1, source_target_pairs={{8,0},{16,8},{24,16},{9,1},{17,9},{25,17},{10,2},{18,10},{26,18},{... | collective-permute-start | bytes 1572872 | tf_op jit(solution)/shard_map/ppermute | solution.py:173
  75.3 1.7 %collective-permute-start.15 = (bf16[256,1024]{1,0:T(8,128)(2,1)S(1)}, bf16[256,1024]{1,0:T(8,128)(2,1)}, u32[]{:S(2)}, u32[]{:S(2)}) collective-permute-start(bf16[256,1024]{1,0:T(8,128)(2,1)S(1)} %get-tuple-element.9.kg_ref), channel_id=1, source_target_pairs={{0,1},{1,0},{2,3},{3,2},{4,5},{5,4},{6,7},{7,6},{8,9},{9,8},{10,11... | collective-permute-start | bytes 1572872 | tf_op jit(solution)/shard_map/ppermute | solution.py:127
  77.0 0.0 collective-permute-done.16
  77.0 0.6 collective-permute-start.12
  77.6 0.0 collective-permute-done.11
  77.6 0.4 collective-permute-start.17
  78.0 3.2 %collective-permute-done.5 = bf16[256,1024]{1,0:T(8,128)(2,1)} collective-permute-done((bf16[256,1024]{1,0:T(8,128)(2,1)}, bf16[256,1024]{1,0:T(8,128)(2,1)}, u32[]{:S(2)}, u32[]{:S(2)}) %collective-permute-start.5) | collective-permute-done | bytes 524320 | tf_op jit(solution)/shard_map/ppermute | solution.py:172
  81.2 4.9 %collective-permute-done.9 = bf16[256,1024]{1,0:T(8,128)(2,1)} collective-permute-done((bf16[256,1024]{1,0:T(8,128)(2,1)}, bf16[256,1024]{1,0:T(8,128)(2,1)}, u32[]{:S(2)}, u32[]{:S(2)}) %collective-permute-start.9) | collective-permute-done | bytes 524320 | tf_op jit(solution)/shard_map/ppermute | solution.py:173
  86.1 2.6 %bitcast_add_fusion.3 = (bf16[256,1024]{1,0:T(8,128)(2,1)}, bf16[256,1024]{1,0:T(8,128)(2,1)}, bf16[1,256,1024]{2,1,0:T(8,128)(2,1)S(1)}, bf16[1,256,1024]{2,1,0:T(8,128)(2,1)S(1)}) fusion(bf16[256,1024]{1,0:T(8,128)(2,1)} %collective-permute-done.5, bf16[4,256,1024]{2,1,0:T(8,128)(2,1)S(1)} %bitcast.49, s32[]{:T(128)S(6)} %select_n.151, pred[]{:T(512)S(6)} %lt.65, ...), kind=kLoop, calls=%fused_computation.34 | loop fusion | flops 1572864 | bytes 5242892 | tf_op jit(solution)/shard_map/add | solution.py:169
  88.7 1.3 %collective-permute-start.10 = (bf16[256,1024]{1,0:T(8,128)(2,1)}, bf16[256,1024]{1,0:T(8,128)(2,1)}, u32[]{:S(2)}, u32[]{:S(2)}) collective-permute-start(bf16[256,1024]{1,0:T(8,128)(2,1)} %get-tuple-element.19), channel_id=1, source_target_pairs={{8,0},{16,8},{24,16},{9,1},{17,9},{25,17},{10,2},{18,10},{26,18},{... | collective-permute-start | bytes 1572872 | tf_op jit(solution)/shard_map/ppermute | solution.py:173
  90.0 2.6 %pad_maximum_fusion.1 = bf16[4,256,1024]{2,1,0:T(8,128)(2,1)} fusion(bf16[1,256,1024]{2,1,0:T(8,128)(2,1)S(1)} %get-tuple-element.26, bf16[1,256,1024]{2,1,0:T(8,128)(2,1)S(1)} %copy-done.10, bf16[1,256,1024]{2,1,0:T(8,128)(2,1)S(1)} %get-tuple-element.25, bf16[1,256,1024]{2,1,0:T(8,128)(2,1)} %bitcast.19), kind=kLoop, calls=%fused_computation.10 | loop fusion | flops 3145728 | bytes 4194304 | tf_op jit(solution)/shard_map/stack | solution.py:182
  92.7 3.6 %gather_fusion = bf16[4,256,1024]{2,1,0:T(8,128)(2,1)} fusion(bf16[4,256,1024]{2,1,0:T(8,128)(2,1)} %pad_maximum_fusion.1, s32[1024]{0:T(1024)S(1)} %pad_clamp_fusion), kind=kCustom, calls=%fused_computation | custom fusion | bytes 4194320 | tf_op jit(solution)/shard_map/jit(_take)/gather | solution.py:183
  96.3 1.9 %copy_select_fusion = bf16[4,4,64,1024]{3,2,0,1:T(8,128)(2,1)S(1)} fusion(bf16[4,4,64,1024]{3,2,1,0:T(8,128)(2,1)} %bitcast.56, pred[4]{0:T(512)(128)(4,1)S(1)} %compare_and_fusion), kind=kLoop, calls=%fused_computation.27 | loop fusion | flops 1048576 | bytes 4194308 | tf_op jit(solution)/shard_map/jit(_take)/select_n | solution.py:183
  98.1 0.0 collective-permute-done.15
  98.1 5.4 %collective-permute-start.6 = (bf16[256,1024]{1,0:T(8,128)(2,1)}, bf16[256,1024]{1,0:T(8,128)(2,1)}, u32[]{:S(2)}, u32[]{:S(2)}) collective-permute-start(bf16[256,1024]{1,0:T(8,128)(2,1)} %get-tuple-element.18), channel_id=1, source_target_pairs={{0,8},{8,16},{16,24},{1,9},{9,17},{17,25},{2,10},{10,18},{18,26},{... | collective-permute-start | bytes 1572872 | tf_op jit(solution)/shard_map/ppermute | solution.py:172
  103.5 0.0 collective-permute-done.17
  103.5 3.8 %fusion.12 = f32[1024,1024]{1,0:T(8,128)S(1)} fusion(bf16[1024,1024]{1,0:T(8,128)(2,1)S(1)} %bitcast.58, bf16[256,1024]{1,0:T(8,128)(2,1)} %collective-permute-done.17, bf16[256,1024]{1,0:T(8,128)(2,1)} %collective-permute-done.16, bf16[256,1024]{1,0:T(8,128)(2,1)} %collective-permute-done.15, bf16[256,1024]{1,0:T(8,128)(2,1)S(1)} %get-tuple-element.9.kg_ref), kind=kOutput, calls=%fused_computation.19 | convolution fusion | flops 2155872256 | bytes 8388608 | tf_op jit(solution)/shard_map/dot_general | solution.py:190
  107.3 0.0 copy-start.7
  107.3 1.3 %slice.36 = bf16[512,1024]{1,0:T(8,128)(2,1)} slice(f32[1024,1024]{1,0:T(8,128)S(1)} %fusion.12), slice={[512:1024], [0:1024]} | slice | bytes 2097152 | tf_op jit(solution)/shard_map/slice | solution.py:193
  108.7 4.2 %fusion.4 = f32[1024,1024]{1,0:T(8,128)S(1)} fusion(bf16[1024,1024]{1,0:T(8,128)(2,1)S(1)} %bitcast.59, bf16[256,1024]{1,0:T(8,128)(2,1)} %collective-permute-done.13, bf16[256,1024]{1,0:T(8,128)(2,1)} %collective-permute-done.12, bf16[256,1024]{1,0:T(8,128)(2,1)} %collective-permute-done.11, bf16[256,1024]{1,0:T(8,128)(2,1)S(1)} %get-tuple-element.8.qg_ref), kind=kOutput, calls=%fused_computation.11 | convolution fusion | flops 2155872256 | bytes 8388608 | tf_op jit(solution)/shard_map/dot_general | solution.py:190
  112.9 1.3 slice.37
  114.2 1.0 copy-done.8
  115.2 0.1 collective-permute-start.14
  115.3 1.5 %fusion.21 = bf16[256,1024]{1,0:T(8,128)(2,1)S(1)} fusion(bf16[256,1024]{1,0:T(8,128)(2,1)} %collective-permute-done.10, bf16[256,1024]{1,0:T(8,128)(2,1)} %collective-permute-done.6, bf16[4,256,1024]{2,1,0:T(8,128)(2,1)S(1)} %bitcast.50, s32[]{:T(128)S(6)} %select_n.139), kind=kLoop, calls=%fused_computation.30 | loop fusion | flops 1572864 | bytes 2097156 | tf_op jit(solution)/shard_map/convert_element_type | solution.py:176
  116.8 0.4 copy.13
  117.2 1.2 reshape.94
  118.4 2.3 %fusion.1 = f32[512,1,1024]{2,0,1:T(8,128)S(1)} fusion(f32[1024,1024]{1,0:T(8,128)} %copy-done.7, bf16[512,1024]{1,0:T(8,128)(2,1)} %collective-permute-done.18), kind=kLoop, calls=%fused_computation.5 | loop fusion | flops 1572864 | bytes 5242880 | tf_op jit(solution)/shard_map/stack | solution.py:197
  120.7 0.8 copy-done.9
  121.5 0.4 fusion.3
  121.9 0.5 pad_maximum_fusion
  122.4 5.2 %copy.15 = f32[512,2,1024]{2,1,0:T(2,128)} copy(f32[512,2,1024]{2,0,1:T(8,128)S(1)} %pad_maximum_fusion) | data formatting | bytes 8388608
  (24 shorter events, 0.1 us)
Async XLA Ops:
  3.1 7.2 %collective-permute-start = (bf16[64,1024]{1,0:T(8,128)(2,1)}, bf16[64,1024]{1,0:T(8,128)(2,1)S(1)}, u32[]{:S(2)}, u32[]{:S(2)}) collective-permute-start(bf16[64,1024]{1,0:T(8,128)(2,1)} %get-tuple-element.11), channel_id=1, source_target_pairs={{0,1},{1,0},{2,3},{3,2},{4,5},{5,4},{6,7},{7,6},{8,9},{9,8},{10,11... | collective-permute-start | bytes 393224 | tf_op jit(solution)/shard_map/ppermute | solution.py:127
  6.1 8.0 %collective-permute-start.1 = (bf16[64,1024]{1,0:T(8,128)(2,1)}, bf16[64,1024]{1,0:T(8,128)(2,1)S(1)}, u32[]{:S(2)}, u32[]{:S(2)}) collective-permute-start(bf16[64,1024]{1,0:T(8,128)(2,1)} %get-tuple-element.12), channel_id=1, source_target_pairs={{0,2},{1,3},{2,0},{3,1},{4,6},{5,7},{6,4},{7,5},{8,10},{9,11},{10,... | collective-permute-start | bytes 393224 | tf_op jit(solution)/shard_map/ppermute | solution.py:127
  7.6 7.1 %collective-permute-start.2 = (bf16[64,1024]{1,0:T(8,128)(2,1)}, bf16[64,1024]{1,0:T(8,128)(2,1)S(1)}, u32[]{:S(2)}, u32[]{:S(2)}) collective-permute-start(bf16[64,1024]{1,0:T(8,128)(2,1)} %get-tuple-element.13), channel_id=1, source_target_pairs={{0,3},{1,2},{2,1},{3,0},{4,7},{5,6},{6,5},{7,4},{8,11},{9,10},{10,... | collective-permute-start | bytes 393224 | tf_op jit(solution)/shard_map/ppermute | solution.py:127
  15.4 32.2 %collective-permute-start.3 = (bf16[256,1024]{1,0:T(8,128)(2,1)}, bf16[256,1024]{1,0:T(8,128)(2,1)}, u32[]{:S(2)}, u32[]{:S(2)}) collective-permute-start(bf16[256,1024]{1,0:T(8,128)(2,1)} %constant_dynamic-update-slice_fusion), channel_id=1, source_target_pairs={{0,8},{8,16},{16,24},{1,9},{9,17},{17,25},{2,10},{10,18},{18,26},{... | collective-permute-start | bytes 1572872 | tf_op jit(solution)/shard_map/ppermute | solution.py:172
  19.7 27.9 %collective-permute-start.7 = (bf16[256,1024]{1,0:T(8,128)(2,1)}, bf16[256,1024]{1,0:T(8,128)(2,1)}, u32[]{:S(2)}, u32[]{:S(2)}) collective-permute-start(bf16[256,1024]{1,0:T(8,128)(2,1)} %constant_dynamic-update-slice_fusion), channel_id=1, source_target_pairs={{8,0},{16,8},{24,16},{9,1},{17,9},{25,17},{10,2},{18,10},{26,18},{... | collective-permute-start | bytes 1572872 | tf_op jit(solution)/shard_map/ppermute | solution.py:173
  21.0 1.0 copy-start
  22.0 1.0 copy-start.1
  23.1 1.0 copy-start.2
  24.1 1.0 copy-start.3
  25.1 0.8 copy-start.4
  26.0 0.8 copy-start.5
  26.8 0.7 copy-start.6
  49.9 13.5 %collective-permute-start.4 = (bf16[256,1024]{1,0:T(8,128)(2,1)}, bf16[256,1024]{1,0:T(8,128)(2,1)}, u32[]{:S(2)}, u32[]{:S(2)}) collective-permute-start(bf16[256,1024]{1,0:T(8,128)(2,1)} %get-tuple-element.22), channel_id=1, source_target_pairs={{0,8},{8,16},{16,24},{1,9},{9,17},{17,25},{2,10},{10,18},{18,26},{... | collective-permute-start | bytes 1572872 | tf_op jit(solution)/shard_map/ppermute | solution.py:172
  55.2 13.1 %collective-permute-start.8 = (bf16[256,1024]{1,0:T(8,128)(2,1)}, bf16[256,1024]{1,0:T(8,128)(2,1)}, u32[]{:S(2)}, u32[]{:S(2)}) collective-permute-start(bf16[256,1024]{1,0:T(8,128)(2,1)} %get-tuple-element.23), channel_id=1, source_target_pairs={{8,0},{16,8},{24,16},{9,1},{17,9},{25,17},{10,2},{18,10},{26,18},{... | collective-permute-start | bytes 1572872 | tf_op jit(solution)/shard_map/ppermute | solution.py:173
  56.5 20.6 %collective-permute-start.16 = (bf16[256,1024]{1,0:T(8,128)(2,1)S(1)}, bf16[256,1024]{1,0:T(8,128)(2,1)}, u32[]{:S(2)}, u32[]{:S(2)}) collective-permute-start(bf16[256,1024]{1,0:T(8,128)(2,1)S(1)} %get-tuple-element.9.kg_ref), channel_id=1, source_target_pairs={{0,2},{1,3},{2,0},{3,1},{4,6},{5,7},{6,4},{7,5},{8,10},{9,11},{10,... | collective-permute-start | bytes 1572872 | tf_op jit(solution)/shard_map/ppermute | solution.py:127
  58.0 19.6 %collective-permute-start.11 = (bf16[256,1024]{1,0:T(8,128)(2,1)S(1)}, bf16[256,1024]{1,0:T(8,128)(2,1)}, u32[]{:S(2)}, u32[]{:S(2)}) collective-permute-start(bf16[256,1024]{1,0:T(8,128)(2,1)S(1)} %get-tuple-element.8.qg_ref), channel_id=1, source_target_pairs={{0,1},{1,0},{2,3},{3,2},{4,5},{5,4},{6,7},{7,6},{8,9},{9,8},{10,11... | collective-permute-start | bytes 1572872 | tf_op jit(solution)/shard_map/ppermute | solution.py:127
  70.6 10.6 %collective-permute-start.5 = (bf16[256,1024]{1,0:T(8,128)(2,1)}, bf16[256,1024]{1,0:T(8,128)(2,1)}, u32[]{:S(2)}, u32[]{:S(2)}) collective-permute-start(bf16[256,1024]{1,0:T(8,128)(2,1)} %get-tuple-element.20), channel_id=1, source_target_pairs={{0,8},{8,16},{16,24},{1,9},{9,17},{17,25},{2,10},{10,18},{18,26},{... | collective-permute-start | bytes 1572872 | tf_op jit(solution)/shard_map/ppermute | solution.py:172
  74.0 12.1 %collective-permute-start.9 = (bf16[256,1024]{1,0:T(8,128)(2,1)}, bf16[256,1024]{1,0:T(8,128)(2,1)}, u32[]{:S(2)}, u32[]{:S(2)}) collective-permute-start(bf16[256,1024]{1,0:T(8,128)(2,1)} %get-tuple-element.21), channel_id=1, source_target_pairs={{8,0},{16,8},{24,16},{9,1},{17,9},{25,17},{10,2},{18,10},{26,18},{... | collective-permute-start | bytes 1572872 | tf_op jit(solution)/shard_map/ppermute | solution.py:173
  75.3 22.9 %collective-permute-start.15 = (bf16[256,1024]{1,0:T(8,128)(2,1)S(1)}, bf16[256,1024]{1,0:T(8,128)(2,1)}, u32[]{:S(2)}, u32[]{:S(2)}) collective-permute-start(bf16[256,1024]{1,0:T(8,128)(2,1)S(1)} %get-tuple-element.9.kg_ref), channel_id=1, source_target_pairs={{0,1},{1,0},{2,3},{3,2},{4,5},{5,4},{6,7},{7,6},{8,9},{9,8},{10,11... | collective-permute-start | bytes 1572872 | tf_op jit(solution)/shard_map/ppermute | solution.py:127
  77.0 13.0 %copy-start.10 = (bf16[1,256,1024]{2,1,0:T(8,128)(2,1)S(1)}, bf16[1,256,1024]{2,1,0:T(8,128)(2,1)}, u32[]{:S(2)}) copy-start(bf16[1,256,1024]{2,1,0:T(8,128)(2,1)} %get-tuple-element.24) | copy-start | bytes 1572868
  77.0 31.6 %collective-permute-start.12 = (bf16[256,1024]{1,0:T(8,128)(2,1)S(1)}, bf16[256,1024]{1,0:T(8,128)(2,1)}, u32[]{:S(2)}, u32[]{:S(2)}) collective-permute-start(bf16[256,1024]{1,0:T(8,128)(2,1)S(1)} %get-tuple-element.8.qg_ref), channel_id=1, source_target_pairs={{0,2},{1,3},{2,0},{3,1},{4,6},{5,7},{6,4},{7,5},{8,10},{9,11},{10,... | collective-permute-start | bytes 1572872 | tf_op jit(solution)/shard_map/ppermute | solution.py:127
  77.6 25.9 %collective-permute-start.17 = (bf16[256,1024]{1,0:T(8,128)(2,1)}, bf16[256,1024]{1,0:T(8,128)(2,1)}, u32[]{:S(2)}, u32[]{:S(2)}) collective-permute-start(bf16[256,1024]{1,0:T(8,128)(2,1)} %collective-permute-done.16), channel_id=1, source_target_pairs={{0,1},{1,0},{2,3},{3,2},{4,5},{5,4},{6,7},{7,6},{8,9},{9,8},{10,11... | collective-permute-start | bytes 1572872 | tf_op jit(solution)/shard_map/ppermute | solution.py:127
  81.2 27.5 %collective-permute-start.13 = (bf16[256,1024]{1,0:T(8,128)(2,1)}, bf16[256,1024]{1,0:T(8,128)(2,1)}, u32[]{:S(2)}, u32[]{:S(2)}) collective-permute-start(bf16[256,1024]{1,0:T(8,128)(2,1)} %collective-permute-done.11), channel_id=1, source_target_pairs={{0,2},{1,3},{2,0},{3,1},{4,6},{5,7},{6,4},{7,5},{8,10},{9,11},{10,... | collective-permute-start | bytes 1572872 | tf_op jit(solution)/shard_map/ppermute | solution.py:127
  88.7 26.6 %collective-permute-start.10 = (bf16[256,1024]{1,0:T(8,128)(2,1)}, bf16[256,1024]{1,0:T(8,128)(2,1)}, u32[]{:S(2)}, u32[]{:S(2)}) collective-permute-start(bf16[256,1024]{1,0:T(8,128)(2,1)} %get-tuple-element.19), channel_id=1, source_target_pairs={{8,0},{16,8},{24,16},{9,1},{17,9},{25,17},{10,2},{18,10},{26,18},{... | collective-permute-start | bytes 1572872 | tf_op jit(solution)/shard_map/ppermute | solution.py:173
  98.1 17.2 %collective-permute-start.6 = (bf16[256,1024]{1,0:T(8,128)(2,1)}, bf16[256,1024]{1,0:T(8,128)(2,1)}, u32[]{:S(2)}, u32[]{:S(2)}) collective-permute-start(bf16[256,1024]{1,0:T(8,128)(2,1)} %get-tuple-element.18), channel_id=1, source_target_pairs={{0,8},{8,16},{16,24},{1,9},{9,17},{17,25},{2,10},{10,18},{18,26},{... | collective-permute-start | bytes 1572872 | tf_op jit(solution)/shard_map/ppermute | solution.py:172
  107.3 5.6 %copy-start.7 = (f32[1024,1024]{1,0:T(8,128)}, f32[1024,1024]{1,0:T(8,128)S(1)}, u32[]{:S(2)}) copy-start(f32[1024,1024]{1,0:T(8,128)S(1)} %fusion.12) | copy-start | bytes 12582916
  108.7 9.7 %collective-permute-start.18 = (bf16[512,1024]{1,0:T(8,128)(2,1)}, bf16[512,1024]{1,0:T(8,128)(2,1)}, u32[]{:S(2)}, u32[]{:S(2)}) collective-permute-start(bf16[512,1024]{1,0:T(8,128)(2,1)} %slice.36), channel_id=1, source_target_pairs={{0,4},{4,0},{1,5},{5,1},{2,6},{6,2},{3,7},{7,3},{8,12},{12,8},{9,1... | collective-permute-start | bytes 3145736 | tf_op jit(solution)/shard_map/ppermute | solution.py:194
  112.9 2.3 %copy-start.8 = (f32[1024,1024]{1,0:T(8,128)}, f32[1024,1024]{1,0:T(8,128)S(1)}, u32[]{:S(2)}) copy-start(f32[1024,1024]{1,0:T(8,128)S(1)} %fusion.4) | copy-start | bytes 12582916
  115.2 5.5 %collective-permute-start.14 = (bf16[512,1024]{1,0:T(8,128)(2,1)}, bf16[512,1024]{1,0:T(8,128)(2,1)S(1)}, u32[]{:S(2)}, u32[]{:S(2)}) collective-permute-start(bf16[512,1024]{1,0:T(8,128)(2,1)} %slice.37), channel_id=1, source_target_pairs={{0,4},{4,0},{1,5},{5,1},{2,6},{6,2},{3,7},{7,3},{8,12},{12,8},{9,1... | collective-permute-start | bytes 3145736 | tf_op jit(solution)/shard_map/ppermute | solution.py:194
  118.4 3.1 %copy-start.9 = (f32[1024,1024]{1,0:T(8,128)S(1)}, f32[1024,1024]{1,0:T(8,128)}, u32[]{:S(2)}) copy-start(f32[1024,1024]{1,0:T(8,128)} %copy-done.8) | copy-start | bytes 12582916

commit v2 on v1

v2 whole, which is shorter than its diff:
```python
import functools
import math

import jax
import jax.numpy as jnp
import numpy as np
from jax import lax
from jax.experimental import pallas as pl
from jax.experimental.pallas import tpu as pltpu
from jax.sharding import PartitionSpec as P

HD = 128
SEQ = 128
GROUP = 4
MIB = 1 << 20
ROWS = (((1,), (1,)), ((), ()))
COLS = (((0,), (0,)), ((), ()))
NEAR = pl.BlockSpec(memory_space=pltpu.VMEM)
FAR = pl.BlockSpec(memory_space=pl.ANY)


def params(mib):
    return pltpu.CompilerParams(vmem_limit_bytes=mib * MIB)


def rope_tables():
    half = HD // 2
    inverse = np.exp(-(np.float32(2.0) * np.arange(half, dtype=np.float32) / np.float32(HD)) * np.float32(math.log(10000.0)))
    angles = np.arange(SEQ, dtype=np.float32)[:, None] * inverse[None, :].astype(np.float32)
    cosine, sine = np.cos(angles), np.sin(angles)
    return np.stack([np.concatenate([cosine, cosine], axis=1), np.concatenate([-sine, sine], axis=1)])


def attention_kernel(doc_ref, table_ref, q_ref, k_ref, v_ref, h_ref, grad_ref, in_s, in_sem):
    tokens, width = q_ref.shape
    scale = 1.0 / math.sqrt(HD)
    loads = []
    for b in range(tokens // SEQ):
        at = pl.ds(b * SEQ, SEQ)
        refs = enumerate((q_ref, k_ref, v_ref, h_ref))
        loads.append([pltpu.make_async_copy(ref.at[at], in_s.at[i, at], in_sem.at[b, i]) for i, ref in refs])
    for copy in [c for load in loads for c in load]:
        copy.start()

    cosine, sine = table_ref[0], table_ref[1]
    back_cosine, back_sine = cosine * scale, sine * scale
    row = lax.broadcasted_iota(jnp.int32, (SEQ, SEQ), 0)
    col = lax.broadcasted_iota(jnp.int32, (SEQ, SEQ), 1)

    def rope(values):
        values = values.astype(jnp.float32)
        return (values * cosine + pltpu.roll(values, HD // 2, 1) * sine).astype(jnp.bfloat16)

    def unrope(values):
        return (values * back_cosine - pltpu.roll(values, HD // 2, 1) * back_sine).astype(jnp.bfloat16)

    for b in range(tokens // SEQ):
        rows = slice(b * SEQ, (b + 1) * SEQ)
        queries = lax.broadcast_in_dim(doc_ref[b], (SEQ, SEQ), (0, 1))
        allowed = (row <= col) & (queries == queries.T)
        for copy in loads[b]:
            copy.wait()
        for first in range(0, width // HD, GROUP):
            ats = [slice(h * HD, (h + 1) * HD) for h in range(first, min(first + GROUP, width // HD))]
            q_rot = [rope(in_s[0, rows, at]) for at in ats]
            k_rot = [rope(in_s[1, rows, at]) for at in ats]
            scores = [
                lax.dot_general(k, q, ROWS, preferred_element_type=jnp.float32) for q, k in zip(q_rot, k_rot)
            ]
            dprob = [
                lax.dot_general(in_s[2, rows, at], in_s[3, rows, at], ROWS, preferred_element_type=jnp.float32)
                for at in ats
            ]
            scores = [jnp.where(allowed, s, -1e30) for s in scores]
            exps = [
                jnp.exp2((s - jnp.max(s, axis=0, keepdims=True)) * (scale * math.log2(math.e))) for s in scores
            ]
            probs = [e * (1.0 / jnp.sum(e, axis=0, keepdims=True)) for e in exps]
            dscore = [
                (p * (d - jnp.sum(p * d, axis=0, keepdims=True))).astype(jnp.bfloat16)
                for p, d in zip(probs, dprob)
            ]
            for at, ds, q, k in zip(ats, dscore, q_rot, k_rot):
                grad_ref[0, rows, at] = unrope(lax.dot_general(ds, k, COLS, preferred_element_type=jnp.float32))
                grad_ref[1, rows, at] = unrope(jnp.dot(ds, q, preferred_element_type=jnp.float32))


def attention_grads(query, key, value, grad, docs):
    tokens, width = query.shape
    micro = tokens // SEQ
    return pl.pallas_call(
        attention_kernel,
        in_specs=[NEAR, NEAR] + [FAR] * 4,
        out_specs=NEAR,
        out_shape=jax.ShapeDtypeStruct((2, tokens, width), jnp.bfloat16),
        scratch_shapes=[
            pltpu.VMEM((4, tokens, width), jnp.bfloat16),
            pltpu.SemaphoreType.DMA((micro, 4)),
        ],
        compiler_params=params(56),
        name="attention_grads",
    )(docs.reshape(micro, 1, SEQ), rope_tables(), query, key, value, grad)


def partials_kernel(pieces, grad_ref, w_ref, out_ref, w_s, out_s, w_sem, out_sem):
    owners, blocks, own_tokens, columns = out_ref.shape
    width = w_ref.shape[2]
    depth = columns // pieces
    fetches = []
    for c in range(blocks * pieces):
        at = pl.ds(c * depth, depth)
        fetches.append(pltpu.make_async_copy(w_ref.at[at], w_s.at[at], w_sem.at[c]))
    for copy in fetches:
        copy.start()
    stores = []
    for block in range(blocks):
        for copy in fetches[block * pieces : (block + 1) * pieces]:
            copy.wait()
        weights = w_s[block * columns : (block + 1) * columns].reshape(columns, 2 * width)
        out = lax.dot_general(grad_ref[0], weights[:, :width], ROWS, preferred_element_type=jnp.float32)
        out = out + lax.dot_general(grad_ref[1], weights[:, width:], ROWS, preferred_element_type=jnp.float32)
        out_s[:, block] = out.astype(jnp.bfloat16).reshape(owners, own_tokens, columns)
        stores.append(pltpu.make_async_copy(out_s.at[:, block], out_ref.at[:, block], out_sem.at[block]))
        stores[-1].start()
    for copy in stores:
        copy.wait()


def input_partials(grads, weight, owners, blocks):
    _, tokens, width = grads.shape
    model = weight.shape[0]
    pieces = 2
    shape = (owners, blocks, tokens // owners, model // blocks)
    return pl.pallas_call(
        functools.partial(partials_kernel, pieces),
        in_specs=[NEAR, FAR],
        out_specs=FAR,
        out_shape=jax.ShapeDtypeStruct(shape, jnp.bfloat16),
        scratch_shapes=[
            pltpu.VMEM(weight.shape, jnp.bfloat16),
            pltpu.VMEM(shape, jnp.bfloat16),
            pltpu.SemaphoreType.DMA((blocks * pieces,)),
            pltpu.SemaphoreType.DMA((blocks,)),
        ],
        compiler_params=params(52),
        name="input_partials",
    )(grads, weight)


def split_kernel(mirrors, x_ref, *refs):
    out_refs, sem = refs[:-1], refs[-1]
    data_count = len(out_refs)
    width = x_ref.shape[1] // (mirrors * data_count)
    copies = []
    for distance, out_ref in enumerate(out_refs):
        owner = lax.axis_index("dp") ^ distance
        for k in range(mirrors):
            block = lax.rem(lax.axis_index("mirror") + k, mirrors) * data_count + owner
            source = x_ref.at[:, pl.ds(pl.multiple_of(block * width, width), width)]
            target = out_ref.at[:, pl.ds(k * width, width)]
            copies.append(pltpu.make_async_copy(source, target, sem.at[distance, k]))
    for copy in copies:
        copy.start()
    for copy in copies:
        copy.wait()


def split_columns(rows, mirrors, data_count):
    tokens, model = rows.shape
    out = jax.ShapeDtypeStruct((tokens, model // data_count), rows.dtype)
    return pl.pallas_call(
        functools.partial(split_kernel, mirrors),
        in_specs=[FAR],
        out_specs=[FAR] * data_count,
        out_shape=[out] * data_count,
        scratch_shapes=[pltpu.SemaphoreType.DMA((data_count, mirrors))],
        compiler_params=params(16),
        name="split_columns",
    )(rows)


def merge_kernel(*refs):
    in_refs, out_ref = refs[:-1], refs[-1]
    tokens = in_refs[0].shape[0]
    for i, in_ref in enumerate(in_refs):
        out_ref[i * tokens : (i + 1) * tokens, :] = in_ref[...]


def merge_tokens(columns):
    tokens, width = columns[0].shape
    return pl.pallas_call(
        merge_kernel,
        in_specs=[NEAR] * len(columns),
        out_specs=NEAR,
        out_shape=jax.ShapeDtypeStruct((len(columns) * tokens, width), columns[0].dtype),
        compiler_params=params(16),
        name="merge_tokens",
    )(*columns)


def hop(values, parity, size):
    pairs = []
    for i in range(size):
        j = i + 1 if i % 2 == parity else i - 1
        pairs.append((i, j if 0 <= j < size else i))
    return lax.ppermute(values, "tensor", pairs)


def has_partner(me, parity, size):
    ahead = lax.rem(me, 2) == parity
    partner = jnp.where(ahead, me + 1, me - 1)
    return (partner >= 0) & (partner < size), ahead


def pass_kernel(parity, distance, flow_ref, part_ref, out_ref, part_s, sem):
    size = part_ref.shape[0]
    me = lax.axis_index("tensor")
    ahead = lax.rem(me, 2) == parity
    owner = jnp.where(ahead, me + distance, me - distance)
    active = (owner >= 0) & (owner < size)
    flows, _ = has_partner(me, 1 - parity, size)
    copy = pltpu.make_async_copy(part_ref.at[jnp.clip(owner, 0, size - 1)], part_s, sem)
    copy.start()
    copy.wait()

    @pl.when(flows & active)
    def _():
        out_ref[...] = flow_ref[...] + part_s[...]

    @pl.when(jnp.logical_not(flows))
    def _():
        out_ref[...] = part_s[...]

    @pl.when(flows & jnp.logical_not(active))
    def _():
        out_ref[...] = flow_ref[...]


def pass_on(flow, partials, parity, distance):
    return pl.pallas_call(
        functools.partial(pass_kernel, parity, distance),
        in_specs=[NEAR, FAR],
        out_specs=NEAR,
        out_shape=jax.ShapeDtypeStruct(flow.shape, flow.dtype),
        scratch_shapes=[pltpu.VMEM(flow.shape, flow.dtype), pltpu.SemaphoreType.DMA(())],
        compiler_params=params(16),
        name="pass_on",
    )(flow, partials)


def finish_kernel(blocks, even_ref, odd_ref, part_ref, out_ref, part_s, sem):
    size = part_ref.shape[0]
    me = lax.axis_index("tensor")
    copy = pltpu.make_async_copy(part_ref.at[me], part_s, sem)
    copy.start()
    copy.wait()
    tokens, columns = out_ref.shape[0], out_ref.shape[1] // blocks

    def store(total):
        for block in range(blocks):
            rows = total[block * tokens : (block + 1) * tokens]
            out_ref[:, block * columns : (block + 1) * columns] = rows.astype(out_ref.dtype)

    for parity, (flow_ref, other_ref) in enumerate(((odd_ref, even_ref), (even_ref, odd_ref))):
        alone = jnp.logical_not(has_partner(me, 1 - parity, size)[0])

        @pl.when(alone)
        def _(other_ref=other_ref):
            store(part_s[...].astype(jnp.float32) + other_ref[...].astype(jnp.float32))

    both = has_partner(me, 0, size)[0] & has_partner(me, 1, size)[0]

    @pl.when(both)
    def _():
        total = part_s[...].astype(jnp.float32) + even_ref[...].astype(jnp.float32)
        store(total + odd_ref[...].astype(jnp.float32))


def finish(even, odd, partials, blocks):
    rows, columns = even.shape
    return pl.pallas_call(
        functools.partial(finish_kernel, blocks),
        in_specs=[NEAR, NEAR, FAR],
        out_specs=NEAR,
        out_shape=jax.ShapeDtypeStruct((rows // blocks, columns * blocks), even.dtype),
        scratch_shapes=[pltpu.VMEM(even.shape, even.dtype), pltpu.SemaphoreType.DMA(())],
        compiler_params=params(16),
        name="finish_input_grad",
    )(even, odd, partials)


def weight_kernel(counts, places, *refs):
    size, data_count, side, away = counts
    pieces = 2 * size - 1
    piece_refs, grad_refs = refs[:pieces], refs[pieces:-5]
    out_ref, x_s, grad_s, x_sem, grad_sem = refs[-5:]
    own_ref, even_refs, odd_refs = piece_refs[0], piece_refs[1 : size], piece_refs[size:]
    me = lax.axis_index("tensor")
    tokens = x_s.shape[0] // data_count
    own_tokens = tokens // size
    rows, width = x_s.shape[1], grad_s.shape[2]

    def fetch(ref, slot, k):
        owner = lax.rem(me - slot + size, size)
        start = pl.multiple_of(k * tokens + owner * own_tokens, own_tokens)
        source = ref.at[pl.ds(k * own_tokens, own_tokens), pl.ds(side * rows, rows)]
        return pltpu.make_async_copy(source, x_s.at[pl.ds(start, own_tokens)], x_sem.at[slot, k])

    odd_place = lax.rem(me, 2) == 1
    for k in range(data_count):
        fetch(own_ref, 0, k).start()
    for slot in range(1, size):
        behind = me >= slot
        came = (
            (behind & odd_place, even_refs[slot - 1]),
            (behind & jnp.logical_not(odd_place), odd_refs[slot - 1]),
            (jnp.logical_not(behind) & odd_place, odd_refs[size - slot - 1]),
            (jnp.logical_not(behind) & jnp.logical_not(odd_place), even_refs[size - slot - 1]),
        )
        for condition, ref in came:

            @pl.when(condition)
            def _(ref=ref, slot=slot):
                for k in range(data_count):
                    fetch(ref, slot, k).start()

    loads = []
    for j in range(2):
        for k in range(data_count):
            which, half = places[k][j]
            source = grad_refs[which] if half is None else grad_refs[which].at[half]
            target = grad_s.at[j, pl.ds(k * tokens, tokens)]
            loads.append(pltpu.make_async_copy(source, target, grad_sem.at[j, k]))
    for copy in loads:
        copy.start()
    for slot in range(size):
        for k in range(data_count):
            fetch(own_ref, slot, k).wait()
    for j in range(2):
        for copy in loads[j * data_count : (j + 1) * data_count]:
            copy.wait()
        total = lax.dot_general(x_s[...], grad_s[j], COLS, preferred_element_type=jnp.float32)
        out_ref[:, j * width : (j + 1) * width] = total.astype(out_ref.dtype)


def weight_sums(own, even, odd, grads, mirrors, side, dtype):
    size, data_count = len(even) + 1, len(grads)
    rows = own.shape[1] // mirrors
    arrays, places = [], []
    for pair in grads:
        place = []
        for array, half in pair:
            if not any(array is a for a in arrays):
                arrays.append(array)
            place.append(([i for i, a in enumerate(arrays) if a is array][0], half))
        places.append(place)
    tokens, width = arrays[0].shape[-2:]
    pieces = [own] + even + odd
    return pl.pallas_call(
        functools.partial(weight_kernel, (size, data_count, side, mirrors), places),
        in_specs=[FAR] * (len(pieces) + len(arrays)),
        out_specs=NEAR,
        out_shape=jax.ShapeDtypeStruct((rows, 2 * width), dtype),
        scratch_shapes=[
            pltpu.VMEM((data_count * tokens, rows), jnp.bfloat16),
            pltpu.VMEM((2, data_count * tokens, width), jnp.bfloat16),
            pltpu.SemaphoreType.DMA((size, data_count)),
            pltpu.SemaphoreType.DMA((2, data_count)),
        ],
        compiler_params=params(32),
        name="weight_sums",
    )(*pieces, *arrays)


def average_kernel(replicas, own_ref, *refs):
    away_refs, out_ref = refs[:-1], refs[-1]
    total = own_ref[...]
    for away_ref in away_refs:
        total = total + away_ref[...].astype(jnp.float32)
    out_ref[...] = (total * (1.0 / replicas)).reshape(out_ref.shape)


def average(own, away, replicas):
    rows, columns = own.shape
    depth = min(rows, 128)
    block = pl.BlockSpec((depth, columns), lambda i: (i, 0))
    return pl.pallas_call(
        functools.partial(average_kernel, replicas),
        grid=(rows // depth,),
        in_specs=[block] * (1 + len(away)),
        out_specs=pl.BlockSpec((depth, 2, columns // 2), lambda i: (i, 0, 0)),
        out_shape=jax.ShapeDtypeStruct((rows, 2, columns // 2), jnp.float32),
        compiler_params=params(32),
        name="average_weight_grad",
    )(own, *away)


def swap(values, distance, size):
    return lax.ppermute(values, "dp", [(i, i ^ distance) for i in range(size)])


def across(values, distance, size):
    return lax.ppermute(values, "mirror", [(i, (i + distance) % size) for i in range(size)])


def gathered(grads, size):
    bits = [1 << b for b in range(size.bit_length() - 1)]
    near = {bit: swap(grads, bit, size) for bit in bits}
    found = []
    for half, order in enumerate((bits, bits[1:] + bits[:1])):
        blocks = {0: (grads, half)}
        for bit in order:
            for distance, (array, part) in list(blocks.items()):
                if distance == 0:
                    blocks[bit] = (near[bit], half)
                else:
                    moved = array if part is None else array[part]
                    blocks[distance ^ bit] = (swap(moved, bit, size), None)
        found.append(blocks)
    return [(found[0][d], found[1][d]) for d in range(size)]


def shards(layer_input, qk_weight, query_proj, key_proj, value_proj, head_grad, doc_ids):
    size = lax.axis_size("tensor")
    mirrors = lax.axis_size("mirror")
    data_count = lax.axis_size("dp")

    columns = split_columns(layer_input[0], mirrors, data_count)
    columns = [columns[0]] + [swap(columns[d], d, data_count) for d in range(1, data_count)]
    grads = attention_grads(query_proj[0], key_proj[0], value_proj[0], head_grad[0], doc_ids[0])
    columns, grads = lax.optimization_barrier((columns, grads))
    piece = merge_tokens(columns)

    gathered_grads = gathered(grads, data_count)
    partials = input_partials(grads, qk_weight, size, data_count)
    partials = partials.reshape(size, *piece.shape)

    even, odd = [hop(piece, 0, size)], [hop(piece, 1, size)]
    for distance in range(size - 1, 0, -1):
        send_even = pass_on(odd[-1], partials, 0, distance)
        send_odd = pass_on(even[-1], partials, 1, distance)
        even.append(hop(send_even, 0, size))
        odd.append(hop(send_odd, 1, size))
    input_grad = finish(even[-1], odd[-1], partials, data_count)[None]

    away = []
    for r in range(1, mirrors):
        sums = weight_sums(piece, even[:-1], odd[:-1], gathered_grads, mirrors, r, jnp.bfloat16)
        away.append(across(sums, r, mirrors))
    own = weight_sums(piece, even[:-1], odd[:-1], gathered_grads, mirrors, 0, jnp.float32)
    weight_grad = average(own, away, mirrors * data_count)
    return (input_grad, weight_grad)


def solution(mesh):
    in_specs = (
        P(("mirror", "dp"), "tensor", None),
        P(None, None, "tensor"),
        P(("mirror", "dp"), None, "tensor"),
        P(("mirror", "dp"), None, "tensor"),
        P(("mirror", "dp"), None, "tensor"),
        P(("mirror", "dp"), None, "tensor"),
        P(("mirror", "dp"), None),
    )
    out_specs = (P(("mirror", "dp"), "tensor", None), P(("mirror", "dp"), None, "tensor"))
    return jax.shard_map(shards, mesh=mesh, in_specs=in_specs, out_specs=out_specs, check_vma=False)
```

time: 129 us -> 81.2 us (0.63)
  local copies, waits for them, and re-layouts: 24.9 us -> 3.92 us
  other arithmetic: 17.1 us -> 0 us
  starting transfers between devices: 32.8 us -> 24.7 us
  matrix products: 8.02 us -> 0 us
  Pallas kernels: 21.9 us -> 26.5 us
  waiting for transfers between devices: 22 us -> 24.1 us
    unnamed x26 -> x8, local copies, waits for them, and re-layouts: 16.5 us -> 3.85 us
    ppermute x10 -> x9, starting transfers between devices: 23.5 us -> 14.3 us  [the longest x8 14.2 us: hop(): return lax.ppermute(values, 'tensor', pairs)]
    dot_general x2 -> x0, matrix products: 8.02 us -> none  [shards(): lax.dot_general(inputs, grads, COLS, preferred_element_type=jnp.float32)]
    add x3 -> x0, other arithmetic: 7.3 us -> none  [shards(): send_right + jnp.where(me + ahead < owners, term, jnp.zeros_like(term))]
    another operation x5 -> x0, other arithmetic: 6.42 us -> none  [the longest x3 3.18 us: shards(): weight_grad = jnp.stack(halves, axis=1)]
    pallas_call x3 -> x14, Pallas kernels: 21.9 us -> 26.5 us  [the longest x1 9.45 us: input_partials(): pl.pallas_call(functools.partial(partials_kernel, pieces), in_specs=[NEAR...]
    gather x1 -> x0, local copies, waits for them, and re-layouts: 3.62 us -> none  [shards(): stacked = jnp.take(stacked, (me - jnp.arange(owners)) % owners, axis=0)]
    ppermute x10 -> x9, waiting for transfers between devices: 17.8 us -> 20.5 us  [the longest x8 20.5 us: hop(): return lax.ppermute(values, 'tensor', pairs)]
  transfers between devices with their start and end apart: 19 -> 16, of which waited for: 6 -> 6; matrix products, arithmetic and copies ran while one was open for 25% -> 0% of each run, Pallas kernels for 16% -> 25%
where the time goes in v2:
time: 81.2 us; the launch traced here: 80.1 us
  Pallas kernels  26.5 us (33%)
  starting transfers between devices  24.7 us (30%)
  waiting for transfers between devices  24.1 us (30%)
  local copies, waits for them, and re-layouts  3.92 us (5%)
  between operations  0.86 us (1%)
    ppermute x8, waiting for transfers between devices, hop(): return lax.ppermute(values, 'tensor', pairs)  20.5 us
    ppermute x8, starting transfers between devices, hop(): return lax.ppermute(values, 'tensor', pairs)  14.2 us
    ppermute x7, starting transfers between devices, swap(): return lax.ppermute(values, 'dp', [(i, i ^ distance) for i in range(size)])  10.4 us
    pallas_call x1, Pallas kernels, input_partials(): pl.pallas_call(functools.partial(partials_kernel, pieces), in_specs=[NEAR...  9.45 us
    pallas_call x2, Pallas kernels, weight_sums(): pl.pallas_call(functools.partial(weight_kernel, (size, data_count, side,...  6.9 us
    pallas_call x1, Pallas kernels, attention_grads(): pl.pallas_call(attention_kernel, in_specs=[NEAR, NEAR] + [FAR] * 4, out_s...  5.54 us
    unnamed x8, local copies, waits for them, and re-layouts  3.85 us
    ppermute x7, waiting for transfers between devices, swap(): return lax.ppermute(values, 'dp', [(i, i ^ distance) for i in range(size)])  3.6 us
  transfers between devices with their start and end apart: 16, of which 6 were waited for; matrix products, arithmetic and copies ran while one was open for 0% of the time, Pallas kernels for 25%

profile of v2, /device:TPU:0, one launch (start us, length us, event | category | flops | bytes accessed | tf_op | source)
XLA Modules:
  0.0 80.1 jit_solution(2087021303789783180)
XLA Ops:
  0.6 0.0 copy-start.3
  0.6 1.0 %copy-done.3 = bf16[1,64,4096]{2,1,0:T(8,128)(2,1)S(1)} copy-done((bf16[1,64,4096]{2,1,0:T(8,128)(2,1)S(1)}, bf16[1,64,4096]{2,1,0:T(8,128)(2,1)}, u32[]{:S(2)}) %copy-start.3) | copy-done | bytes 524312
  1.7 0.2 split_columns.1
  1.9 3.0 %collective-permute-start = (bf16[64,1024]{1,0:T(8,128)(2,1)S(1)}, bf16[64,1024]{1,0:T(8,128)(2,1)S(1)}, u32[]{:S(2)}, u32[]{:S(2)}) collective-permute-start(bf16[64,1024]{1,0:T(8,128)(2,1)S(1)} %get-tuple-element.12), channel_id=1, source_target_pairs={{0,1},{1,0},{2,3},{3,2},{4,5},{5,4},{6,7},{7,6},{8,9},{9,8},{10,11... | collective-permute-start | bytes 393224 | tf_op jit(solution)/shard_map/ppermute | solution.py:399
  4.9 1.5 %collective-permute-start.1 = (bf16[64,1024]{1,0:T(8,128)(2,1)S(1)}, bf16[64,1024]{1,0:T(8,128)(2,1)S(1)}, u32[]{:S(2)}, u32[]{:S(2)}) collective-permute-start(bf16[64,1024]{1,0:T(8,128)(2,1)S(1)} %get-tuple-element.13), channel_id=1, source_target_pairs={{0,2},{1,3},{2,0},{3,1},{4,6},{5,7},{6,4},{7,5},{8,10},{9,11},{10,... | collective-permute-start | bytes 393224 | tf_op jit(solution)/shard_map/ppermute | solution.py:399
  6.4 0.0 collective-permute-start.2
  6.4 5.5 %attention_grads.1.grad_ref.refs_7_ = bf16[2,256,1024]{2,1,0:T(8,128)(2,1)} custom-call(s32[2,1,128]{2,1,0:T(1,128)} %bitcast.25, f32[2,128,128]{2,1,0:T(8,128)} %constant.2.clone.table_ref, bf16[256,1024]{1,0:T(8,128)(2,1)} %bitcast.21, bf16[256,1024]{1,0:T(8,128)(2,1)} %bitcast.22, bf16[256,1024]{1,0:T(8,128)(2,1)} %bitcast.23, bf16[256,1024]{1,0:T(8,128)(2,1)} %bitcast.24), custom_call_target="tpu_custom_call" | custom-call | tf_op jit(solution)/shard_map/attention_grads/pallas_call | solution.py:91
  12.0 0.0 collective-permute-done.refs_1_
  12.0 0.7 collective-permute-done.1.refs_2_
  12.6 0.0 collective-permute-done.2.refs_3_
  12.6 1.5 %collective-permute-start.12 = (bf16[2,256,1024]{2,1,0:T(8,128)(2,1)}, bf16[2,256,1024]{2,1,0:T(8,128)(2,1)S(1)}, u32[]{:S(2)}, u32[]{:S(2)}) collective-permute-start(bf16[2,256,1024]{2,1,0:T(8,128)(2,1)} %attention_grads.1.grad_ref.refs_7_), channel_id=1, source_target_pairs={{0,2},{1,3},{2,0},{3,1},{4,6},{5,7},{6,4},{7,5},{8,10},{9,11},{10,... | collective-permute-start | bytes 3145736 | tf_op jit(solution)/shard_map/ppermute | solution.py:399
  14.2 1.4 %collective-permute-start.11 = (bf16[2,256,1024]{2,1,0:T(8,128)(2,1)}, bf16[2,256,1024]{2,1,0:T(8,128)(2,1)S(1)}, u32[]{:S(2)}, u32[]{:S(2)}) collective-permute-start(bf16[2,256,1024]{2,1,0:T(8,128)(2,1)} %attention_grads.1.grad_ref.refs_7_), channel_id=1, source_target_pairs={{0,1},{1,0},{2,3},{3,2},{4,5},{5,4},{6,7},{7,6},{8,9},{9,8},{10,11... | collective-permute-start | bytes 3145736 | tf_op jit(solution)/shard_map/ppermute | solution.py:399
  15.6 0.7 collective-permute-start.3
  16.3 4.4 %collective-permute-start.7 = (bf16[256,1024]{1,0:T(8,128)(2,1)S(1)}, bf16[256,1024]{1,0:T(8,128)(2,1)S(1)}, u32[]{:S(2)}, u32[]{:S(2)}) collective-permute-start(bf16[256,1024]{1,0:T(8,128)(2,1)S(1)} %merge_tokens.1.refs_0_), channel_id=1, source_target_pairs={{0,8},{8,0},{16,24},{24,16},{1,9},{9,1},{17,25},{25,17},{2,10},{10... | collective-permute-start | bytes 1572872 | tf_op jit(solution)/shard_map/ppermute | solution.py:206
  20.7 0.0 copy-start.2
  20.7 1.2 %copy-done.2 = bf16[2,256,1024]{2,1,0:T(8,128)(2,1)S(1)} copy-done((bf16[2,256,1024]{2,1,0:T(8,128)(2,1)S(1)}, bf16[2,256,1024]{2,1,0:T(8,128)(2,1)}, u32[]{:S(2)}) %copy-start.2) | copy-done | bytes 1048600
  21.9 9.4 %input_partials.1 = bf16[4,4,64,1024]{3,2,1,0:T(8,128)(2,1)} custom-call(bf16[2,256,1024]{2,1,0:T(8,128)(2,1)S(1)} %copy-done.2, bf16[4096,2,1024]{2,1,0:T(2,128)(2,1)} %w_ref.1), custom_call_target="tpu_custom_call" | custom-call | tf_op jit(solution)/shard_map/input_partials/pallas_call | solution.py:134
  31.4 0.0 collective-permute-done.3.flow_ref.refs_4_
  31.4 0.0 copy-start
  31.4 1.6 %copy-done = bf16[4,4,64,1024]{3,2,1,0:T(8,128)(2,1)S(1)} copy-done((bf16[4,4,64,1024]{3,2,1,0:T(8,128)(2,1)S(1)}, bf16[4,4,64,1024]{3,2,1,0:T(8,128)(2,1)}, u32[]{:S(2)}) %copy-start) | copy-done | bytes 2097176
  33.0 0.1 pass_on.6
  33.1 0.1 collective-permute-start.4
  33.1 0.0 collective-permute-done.7.flow_ref.refs_1_
  33.2 0.1 pass_on.9
  33.3 0.7 collective-permute-start.8
  34.0 2.6 %collective-permute-done.12.refs_9_ = bf16[2,256,1024]{2,1,0:T(8,128)(2,1)S(1)} collective-permute-done((bf16[2,256,1024]{2,1,0:T(8,128)(2,1)}, bf16[2,256,1024]{2,1,0:T(8,128)(2,1)S(1)}, u32[]{:S(2)}, u32[]{:S(2)}) %collective-permute-start.12) | collective-permute-done | bytes 1048608 | tf_op jit(solution)/shard_map/ppermute | solution.py:399
  36.6 1.7 %collective-permute-start.14 = (bf16[256,1024]{1,0:T(8,128)(2,1)S(1)}, bf16[256,1024]{1,0:T(8,128)(2,1)S(1)}, u32[]{:S(2)}, u32[]{:S(2)}) collective-permute-start(bf16[256,1024]{1,0:T(8,128)(2,1)S(1)} %slice_bitcast_fusion), channel_id=1, source_target_pairs={{0,1},{1,0},{2,3},{3,2},{4,5},{5,4},{6,7},{7,6},{8,9},{9,8},{10,11... | collective-permute-start | bytes 1572872 | tf_op jit(solution)/shard_map/ppermute | solution.py:399
  38.4 0.3 collective-permute-done.11.refs_8_
  38.7 1.3 %collective-permute-start.13 = (bf16[256,1024]{1,0:T(8,128)(2,1)S(1)}, bf16[256,1024]{1,0:T(8,128)(2,1)S(1)}, u32[]{:S(2)}, u32[]{:S(2)}) collective-permute-start(bf16[256,1024]{1,0:T(8,128)(2,1)S(1)} %slice_bitcast_fusion.1), channel_id=1, source_target_pairs={{0,2},{1,3},{2,0},{3,1},{4,6},{5,7},{6,4},{7,5},{8,10},{9,11},{10,... | collective-permute-start | bytes 1572872 | tf_op jit(solution)/shard_map/ppermute | solution.py:399
  40.0 4.8 %collective-permute-done.4.flow_ref.refs_2_ = bf16[256,1024]{1,0:T(8,128)(2,1)S(1)} collective-permute-done((bf16[256,1024]{1,0:T(8,128)(2,1)S(1)}, bf16[256,1024]{1,0:T(8,128)(2,1)S(1)}, u32[]{:S(2)}, u32[]{:S(2)}) %collective-permute-start.4) | collective-permute-done | bytes 524320 | tf_op jit(solution)/shard_map/ppermute | solution.py:206
  44.8 0.1 pass_on.7
  44.9 0.7 collective-permute-start.5
  45.6 0.0 collective-permute-done.8.flow_ref.refs_5_
  45.6 0.1 pass_on.10
  45.8 0.0 copy-start.1
  45.8 4.5 %collective-permute-start.9 = (bf16[256,1024]{1,0:T(8,128)(2,1)S(1)}, bf16[256,1024]{1,0:T(8,128)(2,1)S(1)}, u32[]{:S(2)}, u32[]{:S(2)}) collective-permute-start(bf16[256,1024]{1,0:T(8,128)(2,1)S(1)} %pass_on.10), channel_id=1, source_target_pairs={{0,8},{8,0},{16,24},{24,16},{1,9},{9,1},{17,25},{25,17},{2,10},{10... | collective-permute-start | bytes 1572872 | tf_op jit(solution)/shard_map/ppermute | solution.py:206
  50.3 0.0 collective-permute-done.14.refs_11_
  50.3 0.0 collective-permute-done.13.refs_10_
  50.3 0.0 collective-permute-done.5.flow_ref.refs_6_
  50.3 7.2 %collective-permute-done.9.flow_ref.refs_3_ = bf16[256,1024]{1,0:T(8,128)(2,1)S(1)} collective-permute-done((bf16[256,1024]{1,0:T(8,128)(2,1)S(1)}, bf16[256,1024]{1,0:T(8,128)(2,1)S(1)}, u32[]{:S(2)}, u32[]{:S(2)}) %collective-permute-start.9) | collective-permute-done | bytes 524320 | tf_op jit(solution)/shard_map/ppermute | solution.py:206
  57.5 3.5 %weight_sums.3 = bf16[512,2048]{1,0:T(8,128)(2,1)S(1)} custom-call(bf16[256,1024]{1,0:T(8,128)(2,1)S(1)} %merge_tokens.1.refs_0_, bf16[256,1024]{1,0:T(8,128)(2,1)S(1)} %collective-permute-done.7.flow_ref.refs_1_, bf16[256,1024]{1,0:T(8,128)(2,1)S(1)} %collective-permute-done.4.flow_ref.refs_2_, ...), custom_call_target="tpu_custom_call" | custom-call | tf_op jit(solution)/shard_map/weight_sums/pallas_call | solution.py:359
  61.0 0.1 collective-permute-start.15
  61.1 0.0 copy-done.1
  61.1 0.1 pass_on.8
  61.2 2.4 %collective-permute-start.6 = (bf16[256,1024]{1,0:T(8,128)(2,1)S(1)}, bf16[256,1024]{1,0:T(8,128)(2,1)S(1)}, u32[]{:S(2)}, u32[]{:S(2)}) collective-permute-start(bf16[256,1024]{1,0:T(8,128)(2,1)S(1)} %pass_on.8), channel_id=1, source_target_pairs={{0,8},{8,0},{16,24},{24,16},{1,9},{9,1},{17,25},{25,17},{2,10},{10... | collective-permute-start | bytes 1572872 | tf_op jit(solution)/shard_map/ppermute | solution.py:206
  63.6 0.1 pass_on.11
  63.7 0.7 collective-permute-start.10
  64.4 3.4 %weight_sums.2.own_ref = f32[512,2048]{1,0:T(8,128)S(1)} custom-call(bf16[256,1024]{1,0:T(8,128)(2,1)S(1)} %merge_tokens.1.refs_0_, bf16[256,1024]{1,0:T(8,128)(2,1)S(1)} %collective-permute-done.7.flow_ref.refs_1_, bf16[256,1024]{1,0:T(8,128)(2,1)S(1)} %collective-permute-done.4.flow_ref.refs_2_, ...), custom_call_target="tpu_custom_call" | custom-call | tf_op jit(solution)/shard_map/weight_sums/pallas_call | solution.py:359
  67.8 8.4 %collective-permute-done.6.even_ref = bf16[256,1024]{1,0:T(8,128)(2,1)S(1)} collective-permute-done((bf16[256,1024]{1,0:T(8,128)(2,1)S(1)}, bf16[256,1024]{1,0:T(8,128)(2,1)S(1)}, u32[]{:S(2)}, u32[]{:S(2)}) %collective-permute-start.6) | collective-permute-done | bytes 524320 | tf_op jit(solution)/shard_map/ppermute | solution.py:206
  76.2 0.0 collective-permute-done.10.odd_ref
  76.2 1.0 %finish_input_grad.1 = bf16[64,4096]{1,0:T(8,128)(2,1)} custom-call(bf16[256,1024]{1,0:T(8,128)(2,1)S(1)} %collective-permute-done.6.even_ref, bf16[256,1024]{1,0:T(8,128)(2,1)S(1)} %collective-permute-done.10.odd_ref, bf16[4,256,1024]{2,1,0:T(8,128)(2,1)S(1)} %bitcast.18), custom_call_target="tpu_custom_call" | custom-call | tf_op jit(solution)/shard_map/finish_input_grad/pallas_call | solution.py:281
  77.2 0.0 collective-permute-done.15.refs_0_
  77.2 2.9 %average_weight_grad.1 = f32[512,2,1024]{2,1,0:T(2,128)} custom-call(f32[512,2048]{1,0:T(8,128)S(1)} %weight_sums.2.own_ref, bf16[512,2048]{1,0:T(8,128)(2,1)S(1)} %collective-permute-done.15.refs_0_), custom_call_target="tpu_custom_call" | custom-call | tf_op jit(solution)/shard_map/average_weight_grad/pallas_call | solution.py:387
  (3 shorter events, 0.1 us)
Async XLA Ops:
  0.6 1.0 %copy-start.3 = (bf16[1,64,4096]{2,1,0:T(8,128)(2,1)S(1)}, bf16[1,64,4096]{2,1,0:T(8,128)(2,1)}, u32[]{:S(2)}) copy-start(bf16[1,64,4096]{2,1,0:T(8,128)(2,1)} %param.8) | copy-start | bytes 1572868
  1.9 10.1 %collective-permute-start = (bf16[64,1024]{1,0:T(8,128)(2,1)S(1)}, bf16[64,1024]{1,0:T(8,128)(2,1)S(1)}, u32[]{:S(2)}, u32[]{:S(2)}) collective-permute-start(bf16[64,1024]{1,0:T(8,128)(2,1)S(1)} %get-tuple-element.12), channel_id=1, source_target_pairs={{0,1},{1,0},{2,3},{3,2},{4,5},{5,4},{6,7},{7,6},{8,9},{9,8},{10,11... | collective-permute-start | bytes 393224 | tf_op jit(solution)/shard_map/ppermute | solution.py:399
  4.9 7.8 %collective-permute-start.1 = (bf16[64,1024]{1,0:T(8,128)(2,1)S(1)}, bf16[64,1024]{1,0:T(8,128)(2,1)S(1)}, u32[]{:S(2)}, u32[]{:S(2)}) collective-permute-start(bf16[64,1024]{1,0:T(8,128)(2,1)S(1)} %get-tuple-element.13), channel_id=1, source_target_pairs={{0,2},{1,3},{2,0},{3,1},{4,6},{5,7},{6,4},{7,5},{8,10},{9,11},{10,... | collective-permute-start | bytes 393224 | tf_op jit(solution)/shard_map/ppermute | solution.py:399
  6.4 6.3 %collective-permute-start.2 = (bf16[64,1024]{1,0:T(8,128)(2,1)S(1)}, bf16[64,1024]{1,0:T(8,128)(2,1)S(1)}, u32[]{:S(2)}, u32[]{:S(2)}) collective-permute-start(bf16[64,1024]{1,0:T(8,128)(2,1)S(1)} %get-tuple-element.14), channel_id=1, source_target_pairs={{0,3},{1,2},{2,1},{3,0},{4,7},{5,6},{6,5},{7,4},{8,11},{9,10},{10,... | collective-permute-start | bytes 393224 | tf_op jit(solution)/shard_map/ppermute | solution.py:399
  12.6 24.0 %collective-permute-start.12 = (bf16[2,256,1024]{2,1,0:T(8,128)(2,1)}, bf16[2,256,1024]{2,1,0:T(8,128)(2,1)S(1)}, u32[]{:S(2)}, u32[]{:S(2)}) collective-permute-start(bf16[2,256,1024]{2,1,0:T(8,128)(2,1)} %attention_grads.1.grad_ref.refs_7_), channel_id=1, source_target_pairs={{0,2},{1,3},{2,0},{3,1},{4,6},{5,7},{6,4},{7,5},{8,10},{9,11},{10,... | collective-permute-start | bytes 3145736 | tf_op jit(solution)/shard_map/ppermute | solution.py:399
  14.2 24.5 %collective-permute-start.11 = (bf16[2,256,1024]{2,1,0:T(8,128)(2,1)}, bf16[2,256,1024]{2,1,0:T(8,128)(2,1)S(1)}, u32[]{:S(2)}, u32[]{:S(2)}) collective-permute-start(bf16[2,256,1024]{2,1,0:T(8,128)(2,1)} %attention_grads.1.grad_ref.refs_7_), channel_id=1, source_target_pairs={{0,1},{1,0},{2,3},{3,2},{4,5},{5,4},{6,7},{7,6},{8,9},{9,8},{10,11... | collective-permute-start | bytes 3145736 | tf_op jit(solution)/shard_map/ppermute | solution.py:399
  15.6 15.8 %collective-permute-start.3 = (bf16[256,1024]{1,0:T(8,128)(2,1)S(1)}, bf16[256,1024]{1,0:T(8,128)(2,1)S(1)}, u32[]{:S(2)}, u32[]{:S(2)}) collective-permute-start(bf16[256,1024]{1,0:T(8,128)(2,1)S(1)} %merge_tokens.1.refs_0_), channel_id=1, source_target_pairs={{0,0},{8,16},{16,8},{24,24},{1,1},{9,17},{17,9},{25,25},{2,2},{10,... | collective-permute-start | bytes 1572872 | tf_op jit(solution)/shard_map/ppermute | solution.py:206
  16.3 16.9 %collective-permute-start.7 = (bf16[256,1024]{1,0:T(8,128)(2,1)S(1)}, bf16[256,1024]{1,0:T(8,128)(2,1)S(1)}, u32[]{:S(2)}, u32[]{:S(2)}) collective-permute-start(bf16[256,1024]{1,0:T(8,128)(2,1)S(1)} %merge_tokens.1.refs_0_), channel_id=1, source_target_pairs={{0,8},{8,0},{16,24},{24,16},{1,9},{9,1},{17,25},{25,17},{2,10},{10... | collective-permute-start | bytes 1572872 | tf_op jit(solution)/shard_map/ppermute | solution.py:206
  20.7 1.2 %copy-start.2 = (bf16[2,256,1024]{2,1,0:T(8,128)(2,1)S(1)}, bf16[2,256,1024]{2,1,0:T(8,128)(2,1)}, u32[]{:S(2)}) copy-start(bf16[2,256,1024]{2,1,0:T(8,128)(2,1)} %attention_grads.1.grad_ref.refs_7_) | copy-start | bytes 3145732
  31.4 1.6 %copy-start = (bf16[4,4,64,1024]{3,2,1,0:T(8,128)(2,1)S(1)}, bf16[4,4,64,1024]{3,2,1,0:T(8,128)(2,1)}, u32[]{:S(2)}) copy-start(bf16[4,4,64,1024]{3,2,1,0:T(8,128)(2,1)} %input_partials.1) | copy-start | bytes 6291460
  33.1 11.8 %collective-permute-start.4 = (bf16[256,1024]{1,0:T(8,128)(2,1)S(1)}, bf16[256,1024]{1,0:T(8,128)(2,1)S(1)}, u32[]{:S(2)}, u32[]{:S(2)}) collective-permute-start(bf16[256,1024]{1,0:T(8,128)(2,1)S(1)} %pass_on.6), channel_id=1, source_target_pairs={{0,8},{8,0},{16,24},{24,16},{1,9},{9,1},{17,25},{25,17},{2,10},{10... | collective-permute-start | bytes 1572872 | tf_op jit(solution)/shard_map/ppermute | solution.py:206
  33.3 12.4 %collective-permute-start.8 = (bf16[256,1024]{1,0:T(8,128)(2,1)S(1)}, bf16[256,1024]{1,0:T(8,128)(2,1)S(1)}, u32[]{:S(2)}, u32[]{:S(2)}) collective-permute-start(bf16[256,1024]{1,0:T(8,128)(2,1)S(1)} %pass_on.9), channel_id=1, source_target_pairs={{0,0},{8,16},{16,8},{24,24},{1,1},{9,17},{17,9},{25,25},{2,2},{10,... | collective-permute-start | bytes 1572872 | tf_op jit(solution)/shard_map/ppermute | solution.py:206
  36.6 13.6 %collective-permute-start.14 = (bf16[256,1024]{1,0:T(8,128)(2,1)S(1)}, bf16[256,1024]{1,0:T(8,128)(2,1)S(1)}, u32[]{:S(2)}, u32[]{:S(2)}) collective-permute-start(bf16[256,1024]{1,0:T(8,128)(2,1)S(1)} %slice_bitcast_fusion), channel_id=1, source_target_pairs={{0,1},{1,0},{2,3},{3,2},{4,5},{5,4},{6,7},{7,6},{8,9},{9,8},{10,11... | collective-permute-start | bytes 1572872 | tf_op jit(solution)/shard_map/ppermute | solution.py:399
  38.7 11.6 %collective-permute-start.13 = (bf16[256,1024]{1,0:T(8,128)(2,1)S(1)}, bf16[256,1024]{1,0:T(8,128)(2,1)S(1)}, u32[]{:S(2)}, u32[]{:S(2)}) collective-permute-start(bf16[256,1024]{1,0:T(8,128)(2,1)S(1)} %slice_bitcast_fusion.1), channel_id=1, source_target_pairs={{0,2},{1,3},{2,0},{3,1},{4,6},{5,7},{6,4},{7,5},{8,10},{9,11},{10,... | collective-permute-start | bytes 1572872 | tf_op jit(solution)/shard_map/ppermute | solution.py:399
  44.9 5.3 %collective-permute-start.5 = (bf16[256,1024]{1,0:T(8,128)(2,1)S(1)}, bf16[256,1024]{1,0:T(8,128)(2,1)S(1)}, u32[]{:S(2)}, u32[]{:S(2)}) collective-permute-start(bf16[256,1024]{1,0:T(8,128)(2,1)S(1)} %pass_on.7), channel_id=1, source_target_pairs={{0,0},{8,16},{16,8},{24,24},{1,1},{9,17},{17,9},{25,25},{2,2},{10,... | collective-permute-start | bytes 1572872 | tf_op jit(solution)/shard_map/ppermute | solution.py:206
  45.8 15.4 %copy-start.1 = (bf16[4,4,64,1024]{3,2,1,0:T(8,128)(2,1)S(1)}, bf16[4,4,64,1024]{3,2,1,0:T(8,128)(2,1)}, u32[]{:S(2)}) copy-start(bf16[4,4,64,1024]{3,2,1,0:T(8,128)(2,1)} %input_partials.1) | copy-start | bytes 6291460
  45.8 11.7 %collective-permute-start.9 = (bf16[256,1024]{1,0:T(8,128)(2,1)S(1)}, bf16[256,1024]{1,0:T(8,128)(2,1)S(1)}, u32[]{:S(2)}, u32[]{:S(2)}) collective-permute-start(bf16[256,1024]{1,0:T(8,128)(2,1)S(1)} %pass_on.10), channel_id=1, source_target_pairs={{0,8},{8,0},{16,24},{24,16},{1,9},{9,1},{17,25},{25,17},{2,10},{10... | collective-permute-start | bytes 1572872 | tf_op jit(solution)/shard_map/ppermute | solution.py:206
  61.0 16.1 %collective-permute-start.15 = (bf16[512,2048]{1,0:T(8,128)(2,1)S(1)}, bf16[512,2048]{1,0:T(8,128)(2,1)S(1)}, u32[]{:S(2)}, u32[]{:S(2)}) collective-permute-start(bf16[512,2048]{1,0:T(8,128)(2,1)S(1)} %weight_sums.3), channel_id=1, source_target_pairs={{0,4},{4,0},{1,5},{5,1},{2,6},{6,2},{3,7},{7,3},{8,12},{12,8},{9,1... | collective-permute-start | bytes 6291464 | tf_op jit(solution)/shard_map/ppermute | solution.py:403
  61.2 15.0 %collective-permute-start.6 = (bf16[256,1024]{1,0:T(8,128)(2,1)S(1)}, bf16[256,1024]{1,0:T(8,128)(2,1)S(1)}, u32[]{:S(2)}, u32[]{:S(2)}) collective-permute-start(bf16[256,1024]{1,0:T(8,128)(2,1)S(1)} %pass_on.8), channel_id=1, source_target_pairs={{0,8},{8,0},{16,24},{24,16},{1,9},{9,1},{17,25},{25,17},{2,10},{10... | collective-permute-start | bytes 1572872 | tf_op jit(solution)/shard_map/ppermute | solution.py:206
  63.7 12.5 %collective-permute-start.10 = (bf16[256,1024]{1,0:T(8,128)(2,1)S(1)}, bf16[256,1024]{1,0:T(8,128)(2,1)S(1)}, u32[]{:S(2)}, u32[]{:S(2)}) collective-permute-start(bf16[256,1024]{1,0:T(8,128)(2,1)S(1)} %pass_on.11), channel_id=1, source_target_pairs={{0,0},{8,16},{16,8},{24,24},{1,1},{9,17},{17,9},{25,25},{2,2},{10,... | collective-permute-start | bytes 1572872 | tf_op jit(solution)/shard_map/ppermute | solution.py:206

commit v3 on v2

--- a/solution.py
+++ b/solution.py
@@ -12,15 +12,21 @@
 HD = 128
 SEQ = 128
 GROUP = 4
+SPAN = 1024
 MIB = 1 << 20
 ROWS = (((1,), (1,)), ((), ()))
 COLS = (((0,), (0,)), ((), ()))
+BRIEF = pl.CostEstimate(flops=1, bytes_accessed=1, transcendentals=0)
 NEAR = pl.BlockSpec(memory_space=pltpu.VMEM)
 FAR = pl.BlockSpec(memory_space=pl.ANY)
 
 
 def params(mib):
     return pltpu.CompilerParams(vmem_limit_bytes=mib * MIB)
+
+
+def in_hbm(array):
+    return pltpu.with_memory_space_constraint(array, pltpu.HBM)
 
 
 def rope_tables():
@@ -31,7 +37,7 @@
     return np.stack([np.concatenate([cosine, cosine], axis=1), np.concatenate([-sine, sine], axis=1)])
 
 
-def attention_kernel(doc_ref, table_ref, q_ref, k_ref, v_ref, h_ref, grad_ref, in_s, in_sem):
+def attention_kernel(doc_ref, table_ref, q_ref, k_ref, v_ref, h_ref, w_ref, grad_ref, near_ref, doc_s, table_s, in_s, doc_sem, in_sem, w_sem):
     tokens, width = q_ref.shape
     scale = 1.0 / math.sqrt(HD)
     loads = []
@@ -39,10 +45,14 @@
         at = pl.ds(b * SEQ, SEQ)
         refs = enumerate((q_ref, k_ref, v_ref, h_ref))
         loads.append([pltpu.make_async_copy(ref.at[at], in_s.at[i, at], in_sem.at[b, i]) for i, ref in refs])
-    for copy in [c for load in loads for c in load]:
+    first = [pltpu.make_async_copy(doc_ref, doc_s, doc_sem.at[0]), pltpu.make_async_copy(table_ref, table_s, doc_sem.at[1])]
+    fetch = pltpu.make_async_copy(w_ref.at[pl.ds(0, near_ref.shape[0])], near_ref, w_sem)
+    for copy in first + [c for load in loads for c in load] + [fetch]:
         copy.start()
-
-    cosine, sine = table_ref[0], table_ref[1]
+    for copy in first:
+        copy.wait()
+
+    cosine, sine = table_s[0], table_s[1]
     back_cosine, back_sine = cosine * scale, sine * scale
     row = lax.broadcasted_iota(jnp.int32, (SEQ, SEQ), 0)
     col = lax.broadcasted_iota(jnp.int32, (SEQ, SEQ), 1)
@@ -56,7 +66,7 @@
 
     for b in range(tokens // SEQ):
         rows = slice(b * SEQ, (b + 1) * SEQ)
-        queries = lax.broadcast_in_dim(doc_ref[b], (SEQ, SEQ), (0, 1))
+        queries = lax.broadcast_in_dim(doc_s[b], (SEQ, SEQ), (0, 1))
         allowed = (row <= col) & (queries == queries.T)
         for copy in loads[b]:
             copy.wait()
@@ -83,68 +93,82 @@
             for at, ds, q, k in zip(ats, dscore, q_rot, k_rot):
                 grad_ref[0, rows, at] = unrope(lax.dot_general(ds, k, COLS, preferred_element_type=jnp.float32))
                 grad_ref[1, rows, at] = unrope(jnp.dot(ds, q, preferred_element_type=jnp.float32))
-
-
-def attention_grads(query, key, value, grad, docs):
+    fetch.wait()
+
+
+def attention_grads(query, key, value, grad, docs, weight, near):
     tokens, width = query.shape
     micro = tokens // SEQ
     return pl.pallas_call(
         attention_kernel,
-        in_specs=[NEAR, NEAR] + [FAR] * 4,
-        out_specs=NEAR,
-        out_shape=jax.ShapeDtypeStruct((2, tokens, width), jnp.bfloat16),
+        in_specs=[FAR] * 7,
+        out_specs=[NEAR, NEAR],
+        out_shape=[
+            pltpu.VMEM((2, tokens, width), jnp.bfloat16),
+            pltpu.VMEM((near, *weight.shape[1:]), jnp.bfloat16),
+        ],
         scratch_shapes=[
+            pltpu.VMEM((micro, 1, SEQ), jnp.int32),
+            pltpu.VMEM((2, SEQ, HD), jnp.float32),
             pltpu.VMEM((4, tokens, width), jnp.bfloat16),
+            pltpu.SemaphoreType.DMA((2,)),
             pltpu.SemaphoreType.DMA((micro, 4)),
+            pltpu.SemaphoreType.DMA(()),
         ],
-        compiler_params=params(56),
+        cost_estimate=BRIEF,
+        compiler_params=params(20),
         name="attention_grads",
-    )(docs.reshape(micro, 1, SEQ), rope_tables(), query, key, value, grad)
-
-
-def partials_kernel(pieces, grad_ref, w_ref, out_ref, w_s, out_s, w_sem, out_sem):
+    )(
+        *(in_hbm(a) for a in (docs.reshape(micro, 1, SEQ), jnp.asarray(rope_tables()), query, key, value, grad, weight))
+    )
+
+
+def partials_kernel(pieces, grad_ref, near_ref, w_ref, out_ref, w_s, w_sem):
     owners, blocks, own_tokens, columns = out_ref.shape
     width = w_ref.shape[2]
+    near = near_ref.shape[0] // columns
     depth = columns // pieces
     fetches = []
-    for c in range(blocks * pieces):
-        at = pl.ds(c * depth, depth)
-        fetches.append(pltpu.make_async_copy(w_ref.at[at], w_s.at[at], w_sem.at[c]))
+    for c in range((blocks - near) * pieces):
+        source = w_ref.at[pl.ds(near * columns + c * depth, depth)]
+        fetches.append(pltpu.make_async_copy(source, w_s.at[pl.ds(c * depth, depth)], w_sem.at[c]))
     for copy in fetches:
         copy.start()
-    stores = []
-    for block in range(blocks):
-        for copy in fetches[block * pieces : (block + 1) * pieces]:
-            copy.wait()
-        weights = w_s[block * columns : (block + 1) * columns].reshape(columns, 2 * width)
-        out = lax.dot_general(grad_ref[0], weights[:, :width], ROWS, preferred_element_type=jnp.float32)
-        out = out + lax.dot_general(grad_ref[1], weights[:, width:], ROWS, preferred_element_type=jnp.float32)
-        out_s[:, block] = out.astype(jnp.bfloat16).reshape(owners, own_tokens, columns)
-        stores.append(pltpu.make_async_copy(out_s.at[:, block], out_ref.at[:, block], out_sem.at[block]))
-        stores[-1].start()
-    for copy in stores:
-        copy.wait()
-
-
-def input_partials(grads, weight, owners, blocks):
+    for start, ref in ((0, near_ref), (near, w_s)):
+        if start:
+            for copy in fetches:
+                copy.wait()
+        count = ref.shape[0] // columns
+        step = min(count, max(1, SPAN // columns))
+        for block in range(0, count, step):
+            span = min(step, count - block) * columns
+            weights = ref[block * columns : block * columns + span].reshape(span, 2 * width)
+            out = lax.dot_general(grad_ref[0], weights[:, :width], ROWS, preferred_element_type=jnp.float32)
+            out = out + lax.dot_general(grad_ref[1], weights[:, width:], ROWS, preferred_element_type=jnp.float32)
+            out = out.astype(jnp.bfloat16)
+            for at in range(span // columns):
+                rows = out[:, at * columns : (at + 1) * columns]
+                out_ref[:, start + block + at] = rows.reshape(owners, own_tokens, columns)
+
+
+def input_partials(grads, near, weight, owners, blocks):
     _, tokens, width = grads.shape
     model = weight.shape[0]
     pieces = 2
-    shape = (owners, blocks, tokens // owners, model // blocks)
+    left = model - near.shape[0]
     return pl.pallas_call(
         functools.partial(partials_kernel, pieces),
-        in_specs=[NEAR, FAR],
-        out_specs=FAR,
-        out_shape=jax.ShapeDtypeStruct(shape, jnp.bfloat16),
+        in_specs=[NEAR, NEAR, FAR],
+        out_specs=NEAR,
+        out_shape=pltpu.VMEM((owners, blocks, tokens // owners, model // blocks), jnp.bfloat16),
         scratch_shapes=[
-            pltpu.VMEM(weight.shape, jnp.bfloat16),
-            pltpu.VMEM(shape, jnp.bfloat16),
-            pltpu.SemaphoreType.DMA((blocks * pieces,)),
-            pltpu.SemaphoreType.DMA((blocks,)),
+            pltpu.VMEM((left, *weight.shape[1:]), jnp.bfloat16),
+            pltpu.SemaphoreType.DMA((left * blocks * pieces // model,)),
         ],
-        compiler_params=params(52),
+        cost_estimate=BRIEF,
+        compiler_params=params(36),
         name="input_partials",
-    )(grads, weight)
+    )(grads, near, in_hbm(weight))
 
 
 def split_kernel(mirrors, x_ref, *refs):
@@ -174,9 +198,10 @@
         out_specs=[FAR] * data_count,
         out_shape=[out] * data_count,
         scratch_shapes=[pltpu.SemaphoreType.DMA((data_count, mirrors))],
+        cost_estimate=BRIEF,
         compiler_params=params(16),
         name="split_columns",
-    )(rows)
+    )(in_hbm(rows))
 
 
 def merge_kernel(*refs):
@@ -193,17 +218,20 @@
         in_specs=[NEAR] * len(columns),
         out_specs=NEAR,
         out_shape=jax.ShapeDtypeStruct((len(columns) * tokens, width), columns[0].dtype),
+        cost_estimate=BRIEF,
         compiler_params=params(16),
         name="merge_tokens",
     )(*columns)
 
 
-def hop(values, parity, size):
+def hop(values, parity, size, mirrors):
     pairs = []
     for i in range(size):
         j = i + 1 if i % 2 == parity else i - 1
-        pairs.append((i, j if 0 <= j < size else i))
-    return lax.ppermute(values, "tensor", pairs)
+        for r in range(mirrors):
+            to = (j, r) if 0 <= j < size else (i, (r + 1) % mirrors)
+            pairs.append((i * mirrors + r, to[0] * mirrors + to[1]))
+    return lax.ppermute(values, ("tensor", "mirror"), pairs)
 
 
 def has_partner(me, parity, size):
@@ -212,24 +240,22 @@
     return (partner >= 0) & (partner < size), ahead
 
 
-def pass_kernel(parity, distance, flow_ref, part_ref, out_ref, part_s, sem):
+def pass_kernel(parity, distance, flow_ref, part_ref, out_ref):
     size = part_ref.shape[0]
     me = lax.axis_index("tensor")
     ahead = lax.rem(me, 2) == parity
     owner = jnp.where(ahead, me + distance, me - distance)
     active = (owner >= 0) & (owner < size)
     flows, _ = has_partner(me, 1 - parity, size)
-    copy = pltpu.make_async_copy(part_ref.at[jnp.clip(owner, 0, size - 1)], part_s, sem)
-    copy.start()
-    copy.wait()
+    owner = jnp.clip(owner, 0, size - 1)
 
     @pl.when(flows & active)
     def _():
-        out_ref[...] = flow_ref[...] + part_s[...]
+        out_ref[...] = flow_ref[...] + part_ref[owner]
 
     @pl.when(jnp.logical_not(flows))
     def _():
-        out_ref[...] = part_s[...]
+        out_ref[...] = part_ref[owner]
 
     @pl.when(flows & jnp.logical_not(active))
     def _():
@@ -239,21 +265,18 @@
 def pass_on(flow, partials, parity, distance):
     return pl.pallas_call(
         functools.partial(pass_kernel, parity, distance),
-        in_specs=[NEAR, FAR],
+        in_specs=[NEAR, NEAR],
         out_specs=NEAR,
         out_shape=jax.ShapeDtypeStruct(flow.shape, flow.dtype),
-        scratch_shapes=[pltpu.VMEM(flow.shape, flow.dtype), pltpu.SemaphoreType.DMA(())],
+        cost_estimate=BRIEF,
         compiler_params=params(16),
         name="pass_on",
     )(flow, partials)
 
 
-def finish_kernel(blocks, even_ref, odd_ref, part_ref, out_ref, part_s, sem):
+def finish_kernel(blocks, even_ref, odd_ref, part_ref, out_ref):
     size = part_ref.shape[0]
     me = lax.axis_index("tensor")
-    copy = pltpu.make_async_copy(part_ref.at[me], part_s, sem)
-    copy.start()
-    copy.wait()
     tokens, columns = out_ref.shape[0], out_ref.shape[1] // blocks
 
     def store(total):
@@ -266,13 +289,13 @@
 
         @pl.when(alone)
         def _(other_ref=other_ref):
-            store(part_s[...].astype(jnp.float32) + other_ref[...].astype(jnp.float32))
+            store(part_ref[me].astype(jnp.float32) + other_ref[...].astype(jnp.float32))
 
     both = has_partner(me, 0, size)[0] & has_partner(me, 1, size)[0]
 
     @pl.when(both)
     def _():
-        total = part_s[...].astype(jnp.float32) + even_ref[...].astype(jnp.float32)
+        total = part_ref[me].astype(jnp.float32) + even_ref[...].astype(jnp.float32)
         store(total + odd_ref[...].astype(jnp.float32))
 
 
@@ -280,10 +303,10 @@
     rows, columns = even.shape
     return pl.pallas_call(
         functools.partial(finish_kernel, blocks),
-        in_specs=[NEAR, NEAR, FAR],
+        in_specs=[NEAR, NEAR, NEAR],
         out_specs=NEAR,
         out_shape=jax.ShapeDtypeStruct((rows // blocks, columns * blocks), even.dtype),
-        scratch_shapes=[pltpu.VMEM(even.shape, even.dtype), pltpu.SemaphoreType.DMA(())],
+        cost_estimate=BRIEF,
         compiler_params=params(16),
         name="finish_input_grad",
     )(even, odd, partials)
@@ -367,6 +390,7 @@
             pltpu.SemaphoreType.DMA((size, data_count)),
             pltpu.SemaphoreType.DMA((2, data_count)),
         ],
+        cost_estimate=pl.CostEstimate(flops=32 << 30, bytes_accessed=1 << 23, transcendentals=0),
         compiler_params=params(32),
         name="weight_sums",
     )(*pieces, *arrays)
@@ -390,6 +414,7 @@
         in_specs=[block] * (1 + len(away)),
         out_specs=pl.BlockSpec((depth, 2, columns // 2), lambda i: (i, 0, 0)),
         out_shape=jax.ShapeDtypeStruct((rows, 2, columns // 2), jnp.float32),
+        cost_estimate=BRIEF,
         compiler_params=params(32),
         name="average_weight_grad",
     )(own, *away)
@@ -427,28 +452,34 @@
 
     columns = split_columns(layer_input[0], mirrors, data_count)
     columns = [columns[0]] + [swap(columns[d], d, data_count) for d in range(1, data_count)]
-    grads = attention_grads(query_proj[0], key_proj[0], value_proj[0], head_grad[0], doc_ids[0])
+    near = (3 * data_count + 3) // 4 * (layer_input.shape[2] // data_count)
+    grads, weight_rows = attention_grads(
+        query_proj[0], key_proj[0], value_proj[0], head_grad[0], doc_ids[0], qk_weight, near
+    )
     columns, grads = lax.optimization_barrier((columns, grads))
     piece = merge_tokens(columns)
 
     gathered_grads = gathered(grads, data_count)
-    partials = input_partials(grads, qk_weight, size, data_count)
+    partials = input_partials(grads, weight_rows, qk_weight, size, data_count)
     partials = partials.reshape(size, *piece.shape)
 
-    even, odd = [hop(piece, 0, size)], [hop(piece, 1, size)]
+    even, odd = [hop(piece, 0, size, mirrors)], [hop(piece, 1, size, mirrors)]
     for distance in range(size - 1, 0, -1):
         send_even = pass_on(odd[-1], partials, 0, distance)
         send_odd = pass_on(even[-1], partials, 1, distance)
-        even.append(hop(send_even, 0, size))
-        odd.append(hop(send_odd, 1, size))
-    input_grad = finish(even[-1], odd[-1], partials, data_count)[None]
+        if distance == 1:
+            send_even, send_odd, own_piece = lax.optimization_barrier((send_even, send_odd, piece))
+        even.append(hop(send_even, 0, size, mirrors))
+        odd.append(hop(send_odd, 1, size, mirrors))
 
     away = []
     for r in range(1, mirrors):
-        sums = weight_sums(piece, even[:-1], odd[:-1], gathered_grads, mirrors, r, jnp.bfloat16)
+        sums = weight_sums(own_piece, even[:-1], odd[:-1], gathered_grads, mirrors, r, jnp.bfloat16)
         away.append(across(sums, r, mirrors))
-    own = weight_sums(piece, even[:-1], odd[:-1], gathered_grads, mirrors, 0, jnp.float32)
+    own = weight_sums(own_piece, even[:-1], odd[:-1], gathered_grads, mirrors, 0, jnp.float32)
     weight_grad = average(own, away, mirrors * data_count)
+    last_even, last_odd, weight_grad = lax.optimization_barrier((even[-1], odd[-1], weight_grad))
+    input_grad = finish(last_even, last_odd, partials, data_count)[None]
     return (input_grad, weight_grad)
 
 

time: 81.2 us -> 69 us (0.85); the launches traced: 80.1 us -> 68.8 us
  waiting for transfers between devices: 24.1 us -> 15.9 us
  starting transfers between devices: 24.7 us -> 28.6 us
  local copies, waits for them, and re-layouts: 3.92 us -> 0.07 us
  Pallas kernels: 26.5 us -> 23.4 us
    ppermute x8, waiting for transfers between devices: 20.5 us -> 10.6 us  [hop(): return lax.ppermute(values, ('tensor', 'mirror'), pairs)]
    ppermute x8, starting transfers between devices: 14.2 us -> 18.3 us  [hop(): return lax.ppermute(values, ('tensor', 'mirror'), pairs)]
    unnamed x8 -> x0, local copies, waits for them, and re-layouts: 3.85 us -> none
    pallas_call x1, Pallas kernels: 9.45 us -> 5.92 us  [input_partials(): pl.pallas_call(functools.partial(partials_kernel, pieces), in_specs=[NEAR...]
    pallas_call x1, Pallas kernels: 0.18 us -> 1.15 us  [split_columns(): pl.pallas_call(functools.partial(split_kernel, mirrors), in_specs=[FAR],...]
    ppermute x7, waiting for transfers between devices: 3.6 us -> 4.56 us  [swap(): return lax.ppermute(values, 'dp', [(i, i ^ distance) for i in range(size)])]
  transfers between devices with their start and end apart: 16 -> 16, of which waited for: 6 -> 7; matrix products, arithmetic and copies ran while one was open for 0% -> 0% of each run, Pallas kernels for 25% -> 31%
where the time goes in v3:
time: 69 us; the launch traced here: 68.8 us
  starting transfers between devices  28.6 us (41%)
  Pallas kernels  23.4 us (34%)
  waiting for transfers between devices  15.9 us (23%)
  between operations  0.79 us (1%)
    ppermute x8, starting transfers between devices, hop(): return lax.ppermute(values, ('tensor', 'mirror'), pairs)  18.3 us
    ppermute x8, waiting for transfers between devices, hop(): return lax.ppermute(values, ('tensor', 'mirror'), pairs)  10.6 us
    ppermute x7, starting transfers between devices, swap(): return lax.ppermute(values, 'dp', [(i, i ^ distance) for i in range(size)])  10.3 us
    pallas_call x2, Pallas kernels, weight_sums(): pl.pallas_call(functools.partial(weight_kernel, (size, data_count, side,...  6.89 us
    pallas_call x1, Pallas kernels, input_partials(): pl.pallas_call(functools.partial(partials_kernel, pieces), in_specs=[NEAR...  5.92 us
    pallas_call x1, Pallas kernels, attention_grads(): pl.pallas_call(attention_kernel, in_specs=[FAR] * 7, out_specs=[NEAR, NEA...  5.39 us
    ppermute x7, waiting for transfers between devices, swap(): return lax.ppermute(values, 'dp', [(i, i ^ distance) for i in range(size)])  4.56 us
    pallas_call x1, Pallas kernels, average(): pl.pallas_call(functools.partial(average_kernel, replicas), grid=(rows //...  2.84 us
  transfers between devices with their start and end apart: 16, of which 7 were waited for; matrix products, arithmetic and copies ran while one was open for 0% of the time, Pallas kernels for 31%

profile of v3, /device:TPU:0, one launch (start us, length us, event | category | flops | bytes accessed | tf_op | source)
XLA Modules:
  0.0 68.8 jit_solution(700601608536139223)
XLA Ops:
  0.6 1.2 %split_columns.1 = (bf16[64,1024]{1,0:T(8,128)(2,1)S(1)}, bf16[64,1024]{1,0:T(8,128)(2,1)S(1)}, bf16[64,1024]{1,0:T(8,128)(2,1)S(1)}, bf16[64,1024]{1,0:T(8,128)(2,1)S(1)}) custom-call(bf16[64,4096]{1,0:T(8,128)(2,1)} %bitcast.24), custom_call_target="tpu_custom_call" | custom-call | flops 1 | bytes 1 | tf_op jit(solution)/shard_map/split_columns/pallas_call | solution.py:195
  1.8 3.0 %collective-permute-start = (bf16[64,1024]{1,0:T(8,128)(2,1)S(1)}, bf16[64,1024]{1,0:T(8,128)(2,1)S(1)}, u32[]{:S(2)}, u32[]{:S(2)}) collective-permute-start(bf16[64,1024]{1,0:T(8,128)(2,1)S(1)} %get-tuple-element.20), channel_id=1, source_target_pairs={{0,1},{1,0},{2,3},{3,2},{4,5},{5,4},{6,7},{7,6},{8,9},{9,8},{10,11... | collective-permute-start | bytes 393224 | tf_op jit(solution)/shard_map/ppermute | solution.py:424
  4.8 1.5 %collective-permute-start.1 = (bf16[64,1024]{1,0:T(8,128)(2,1)S(1)}, bf16[64,1024]{1,0:T(8,128)(2,1)S(1)}, u32[]{:S(2)}, u32[]{:S(2)}) collective-permute-start(bf16[64,1024]{1,0:T(8,128)(2,1)S(1)} %get-tuple-element.21), channel_id=1, source_target_pairs={{0,2},{1,3},{2,0},{3,1},{4,6},{5,7},{6,4},{7,5},{8,10},{9,11},{10,... | collective-permute-start | bytes 393224 | tf_op jit(solution)/shard_map/ppermute | solution.py:424
  6.3 0.0 collective-permute-start.2
  6.3 5.4 %attention_grads.1 = (bf16[2,256,1024]{2,1,0:T(8,128)(2,1)S(1)}, bf16[3072,2,1024]{2,1,0:T(2,128)(2,1)S(1)}) custom-call(s32[2,1,128]{2,1,0:T(1,128)} %bitcast.25, f32[2,128,128]{2,1,0:T(8,128)} %constant.2.clone.table_ref, bf16[256,1024]{1,0:T(8,128)(2,1)} %bitcast.19, bf16[256,1024]{1,0:T(8,128)(2,1)} %bitcast.20, bf16[256,1024]{1,0:T(8,128)(2,1)} %bitcast.21, ...), custom_call_target="tpu_custom_call" | custom-call | flops 1 | bytes 1 | tf_op jit(solution)/shard_map/attention_grads/pallas_call | solution.py:102
  11.7 0.0 collective-permute-done.refs_1_
  11.7 0.8 %collective-permute-done.1.refs_2_ = bf16[64,1024]{1,0:T(8,128)(2,1)S(1)} collective-permute-done((bf16[64,1024]{1,0:T(8,128)(2,1)S(1)}, bf16[64,1024]{1,0:T(8,128)(2,1)S(1)}, u32[]{:S(2)}, u32[]{:S(2)}) %collective-permute-start.1) | collective-permute-done | bytes 131104 | tf_op jit(solution)/shard_map/ppermute | solution.py:424
  12.6 0.0 collective-permute-done.2.refs_3_
  12.6 1.6 %collective-permute-start.6 = (bf16[256,1024]{1,0:T(8,128)(2,1)S(1)}, bf16[256,1024]{1,0:T(8,128)(2,1)S(1)}, u32[]{:S(2)}, u32[]{:S(2)}) collective-permute-start(bf16[256,1024]{1,0:T(8,128)(2,1)S(1)} %merge_tokens.1.refs_0_), channel_id=1, source_target_pairs={{0,8},{4,12},{8,0},{12,4},{16,24},{20,28},{24,16},{28,20},{1,9},{5... | collective-permute-start | bytes 1572872 | tf_op jit(solution)/shard_map/ppermute | solution.py:234
  14.3 0.0 collective-permute-start.3
  14.3 1.5 %collective-permute-start.12 = (bf16[2,256,1024]{2,1,0:T(8,128)(2,1)S(1)}, bf16[2,256,1024]{2,1,0:T(8,128)(2,1)S(1)}, u32[]{:S(2)}, u32[]{:S(2)}) collective-permute-start(bf16[2,256,1024]{2,1,0:T(8,128)(2,1)S(1)} %get-tuple-element.28.grad_ref.refs_7_), channel_id=1, source_target_pairs={{0,2},{1,3},{2,0},{3,1},{4,6},{5,7},{6,4},{7,5},{8,10},{9,11},{10,... | collective-permute-start | bytes 3145736 | tf_op jit(solution)/shard_map/ppermute | solution.py:424
  15.8 1.2 %collective-permute-start.11 = (bf16[2,256,1024]{2,1,0:T(8,128)(2,1)S(1)}, bf16[2,256,1024]{2,1,0:T(8,128)(2,1)S(1)}, u32[]{:S(2)}, u32[]{:S(2)}) collective-permute-start(bf16[2,256,1024]{2,1,0:T(8,128)(2,1)S(1)} %get-tuple-element.28.grad_ref.refs_7_), channel_id=1, source_target_pairs={{0,1},{1,0},{2,3},{3,2},{4,5},{5,4},{6,7},{7,6},{8,9},{9,8},{10,11... | collective-permute-start | bytes 3145736 | tf_op jit(solution)/shard_map/ppermute | solution.py:424
  16.9 5.9 %input_partials.1 = bf16[4,4,64,1024]{3,2,1,0:T(8,128)(2,1)S(1)} custom-call(bf16[2,256,1024]{2,1,0:T(8,128)(2,1)S(1)} %get-tuple-element.28.grad_ref.refs_7_, bf16[3072,2,1024]{2,1,0:T(2,128)(2,1)S(1)} %get-tuple-element.29.near_ref, bf16[4096,2,1024]{2,1,0:T(2,128)(2,1)} %w_ref.3), custom_call_target="tpu_custom_call" | custom-call | flops 1 | bytes 1 | tf_op jit(solution)/shard_map/input_partials/pallas_call | solution.py:159
  22.9 2.2 %collective-permute-done.6.flow_ref.refs_1_ = bf16[256,1024]{1,0:T(8,128)(2,1)S(1)} collective-permute-done((bf16[256,1024]{1,0:T(8,128)(2,1)S(1)}, bf16[256,1024]{1,0:T(8,128)(2,1)S(1)}, u32[]{:S(2)}, u32[]{:S(2)}) %collective-permute-start.6) | collective-permute-done | bytes 524320 | tf_op jit(solution)/shard_map/ppermute | solution.py:234
  25.1 0.1 collective-permute-start.7
  25.2 0.0 collective-permute-done.3.flow_ref.refs_4_
  25.2 0.1 pass_on.6
  25.2 3.4 %collective-permute-start.4 = (bf16[256,1024]{1,0:T(8,128)(2,1)S(1)}, bf16[256,1024]{1,0:T(8,128)(2,1)S(1)}, u32[]{:S(2)}, u32[]{:S(2)}) collective-permute-start(bf16[256,1024]{1,0:T(8,128)(2,1)S(1)} %pass_on.6), channel_id=1, source_target_pairs={{0,8},{4,12},{8,0},{12,4},{16,24},{20,28},{24,16},{28,20},{1,9},{5... | collective-permute-start | bytes 1572872 | tf_op jit(solution)/shard_map/ppermute | solution.py:234
  28.6 0.0 collective-permute-done.7.flow_ref.refs_5_
  28.7 10.5 %collective-permute-start.8 = (bf16[256,1024]{1,0:T(8,128)(2,1)S(1)}, bf16[256,1024]{1,0:T(8,128)(2,1)S(1)}, u32[]{:S(2)}, u32[]{:S(2)}) collective-permute-start(bf16[256,1024]{1,0:T(8,128)(2,1)S(1)} %pass_on.10), channel_id=1, source_target_pairs={{0,8},{4,12},{8,0},{12,4},{16,24},{20,28},{24,16},{28,20},{1,9},{5... | collective-permute-start | bytes 1572872 | tf_op jit(solution)/shard_map/ppermute | solution.py:234
  39.2 2.3 %collective-permute-done.4.flow_ref.refs_2_ = bf16[256,1024]{1,0:T(8,128)(2,1)S(1)} collective-permute-done((bf16[256,1024]{1,0:T(8,128)(2,1)S(1)}, bf16[256,1024]{1,0:T(8,128)(2,1)S(1)}, u32[]{:S(2)}, u32[]{:S(2)}) %collective-permute-start.4) | collective-permute-done | bytes 524320 | tf_op jit(solution)/shard_map/ppermute | solution.py:234
  41.5 0.1 collective-permute-start.5
  41.6 0.0 collective-permute-done.12.refs_9_
  41.6 1.5 %collective-permute-start.14 = (bf16[256,1024]{1,0:T(8,128)(2,1)S(1)}, bf16[256,1024]{1,0:T(8,128)(2,1)S(1)}, u32[]{:S(2)}, u32[]{:S(2)}) collective-permute-start(bf16[256,1024]{1,0:T(8,128)(2,1)S(1)} %slice_bitcast_fusion), channel_id=1, source_target_pairs={{0,1},{1,0},{2,3},{3,2},{4,5},{5,4},{6,7},{7,6},{8,9},{9,8},{10,11... | collective-permute-start | bytes 1572872 | tf_op jit(solution)/shard_map/ppermute | solution.py:424
  43.1 0.0 collective-permute-done.11.refs_8_
  43.2 1.5 %collective-permute-start.13 = (bf16[256,1024]{1,0:T(8,128)(2,1)S(1)}, bf16[256,1024]{1,0:T(8,128)(2,1)S(1)}, u32[]{:S(2)}, u32[]{:S(2)}) collective-permute-start(bf16[256,1024]{1,0:T(8,128)(2,1)S(1)} %slice_bitcast_fusion.1), channel_id=1, source_target_pairs={{0,2},{1,3},{2,0},{3,1},{4,6},{5,7},{6,4},{7,5},{8,10},{9,11},{10,... | collective-permute-start | bytes 1572872 | tf_op jit(solution)/shard_map/ppermute | solution.py:424
  44.7 6.1 %collective-permute-done.8.flow_ref.refs_3_ = bf16[256,1024]{1,0:T(8,128)(2,1)S(1)} collective-permute-done((bf16[256,1024]{1,0:T(8,128)(2,1)S(1)}, bf16[256,1024]{1,0:T(8,128)(2,1)S(1)}, u32[]{:S(2)}, u32[]{:S(2)}) %collective-permute-start.8) | collective-permute-done | bytes 524320 | tf_op jit(solution)/shard_map/ppermute | solution.py:234
  50.9 0.0 collective-permute-done.5.flow_ref.refs_6_
  50.9 0.1 pass_on.8
  51.0 2.6 %collective-permute-start.9 = (bf16[256,1024]{1,0:T(8,128)(2,1)S(1)}, bf16[256,1024]{1,0:T(8,128)(2,1)S(1)}, u32[]{:S(2)}, u32[]{:S(2)}) collective-permute-start(bf16[256,1024]{1,0:T(8,128)(2,1)S(1)} %pass_on.8), channel_id=1, source_target_pairs={{0,8},{4,12},{8,0},{12,4},{16,24},{20,28},{24,16},{28,20},{1,9},{5... | collective-permute-start | bytes 1572872 | tf_op jit(solution)/shard_map/ppermute | solution.py:234
  53.6 0.0 collective-permute-start.10
  53.6 2.4 %collective-permute-done.14.refs_11_ = bf16[256,1024]{1,0:T(8,128)(2,1)S(1)} collective-permute-done((bf16[256,1024]{1,0:T(8,128)(2,1)S(1)}, bf16[256,1024]{1,0:T(8,128)(2,1)S(1)}, u32[]{:S(2)}, u32[]{:S(2)}) %collective-permute-start.14) | collective-permute-done | bytes 524320 | tf_op jit(solution)/shard_map/ppermute | solution.py:424
  56.0 1.3 %collective-permute-done.13.refs_10_ = bf16[256,1024]{1,0:T(8,128)(2,1)S(1)} collective-permute-done((bf16[256,1024]{1,0:T(8,128)(2,1)S(1)}, bf16[256,1024]{1,0:T(8,128)(2,1)S(1)}, u32[]{:S(2)}, u32[]{:S(2)}) %collective-permute-start.13) | collective-permute-done | bytes 524320 | tf_op jit(solution)/shard_map/ppermute | solution.py:424
  57.3 3.5 %weight_sums.3 = bf16[512,2048]{1,0:T(8,128)(2,1)S(1)} custom-call(bf16[256,1024]{1,0:T(8,128)(2,1)S(1)} %merge_tokens.1.refs_0_, bf16[256,1024]{1,0:T(8,128)(2,1)S(1)} %collective-permute-done.6.flow_ref.refs_1_, bf16[256,1024]{1,0:T(8,128)(2,1)S(1)} %collective-permute-done.4.flow_ref.refs_2_, ...), custom_call_target="tpu_custom_call" | custom-call | flops 34359738368 | bytes 8388608 | tf_op jit(solution)/shard_map/weight_sums/pallas_call | solution.py:382
  60.8 0.1 collective-permute-start.15
  60.9 3.4 %weight_sums.2.own_ref = f32[512,2048]{1,0:T(8,128)S(1)} custom-call(bf16[256,1024]{1,0:T(8,128)(2,1)S(1)} %merge_tokens.1.refs_0_, bf16[256,1024]{1,0:T(8,128)(2,1)S(1)} %collective-permute-done.6.flow_ref.refs_1_, bf16[256,1024]{1,0:T(8,128)(2,1)S(1)} %collective-permute-done.4.flow_ref.refs_2_, ...), custom_call_target="tpu_custom_call" | custom-call | flops 34359738368 | bytes 8388608 | tf_op jit(solution)/shard_map/weight_sums/pallas_call | solution.py:382
  64.3 0.8 %collective-permute-done.15.refs_0_ = bf16[512,2048]{1,0:T(8,128)(2,1)S(1)} collective-permute-done((bf16[512,2048]{1,0:T(8,128)(2,1)S(1)}, bf16[512,2048]{1,0:T(8,128)(2,1)S(1)}, u32[]{:S(2)}, u32[]{:S(2)}) %collective-permute-start.15) | collective-permute-done | bytes 2097184 | tf_op jit(solution)/shard_map/ppermute | solution.py:428
  65.0 2.8 %average_weight_grad.1 = f32[512,2,1024]{2,1,0:T(2,128)} custom-call(f32[512,2048]{1,0:T(8,128)S(1)} %weight_sums.2.own_ref, bf16[512,2048]{1,0:T(8,128)(2,1)S(1)} %collective-permute-done.15.refs_0_), custom_call_target="tpu_custom_call" | custom-call | flops 1 | bytes 1 | tf_op jit(solution)/shard_map/average_weight_grad/pallas_call | solution.py:411
  67.9 0.0 collective-permute-done.9.even_ref
  67.9 0.0 collective-permute-done.10.odd_ref
  67.9 0.9 %finish_input_grad.1 = bf16[64,4096]{1,0:T(8,128)(2,1)} custom-call(bf16[256,1024]{1,0:T(8,128)(2,1)S(1)} %collective-permute-done.9.even_ref, bf16[256,1024]{1,0:T(8,128)(2,1)S(1)} %collective-permute-done.10.odd_ref, bf16[4,256,1024]{2,1,0:T(8,128)(2,1)S(1)} %bitcast.18), custom_call_target="tpu_custom_call" | custom-call | flops 1 | bytes 1 | tf_op jit(solution)/shard_map/finish_input_grad/pallas_call | solution.py:304
  (7 shorter events, 0.2 us)
Async XLA Ops:
  1.8 9.9 %collective-permute-start = (bf16[64,1024]{1,0:T(8,128)(2,1)S(1)}, bf16[64,1024]{1,0:T(8,128)(2,1)S(1)}, u32[]{:S(2)}, u32[]{:S(2)}) collective-permute-start(bf16[64,1024]{1,0:T(8,128)(2,1)S(1)} %get-tuple-element.20), channel_id=1, source_target_pairs={{0,1},{1,0},{2,3},{3,2},{4,5},{5,4},{6,7},{7,6},{8,9},{9,8},{10,11... | collective-permute-start | bytes 393224 | tf_op jit(solution)/shard_map/ppermute | solution.py:424
  4.8 7.8 %collective-permute-start.1 = (bf16[64,1024]{1,0:T(8,128)(2,1)S(1)}, bf16[64,1024]{1,0:T(8,128)(2,1)S(1)}, u32[]{:S(2)}, u32[]{:S(2)}) collective-permute-start(bf16[64,1024]{1,0:T(8,128)(2,1)S(1)} %get-tuple-element.21), channel_id=1, source_target_pairs={{0,2},{1,3},{2,0},{3,1},{4,6},{5,7},{6,4},{7,5},{8,10},{9,11},{10,... | collective-permute-start | bytes 393224 | tf_op jit(solution)/shard_map/ppermute | solution.py:424
  6.3 6.3 %collective-permute-start.2 = (bf16[64,1024]{1,0:T(8,128)(2,1)S(1)}, bf16[64,1024]{1,0:T(8,128)(2,1)S(1)}, u32[]{:S(2)}, u32[]{:S(2)}) collective-permute-start(bf16[64,1024]{1,0:T(8,128)(2,1)S(1)} %get-tuple-element.22), channel_id=1, source_target_pairs={{0,3},{1,2},{2,1},{3,0},{4,7},{5,6},{6,5},{7,4},{8,11},{9,10},{10,... | collective-permute-start | bytes 393224 | tf_op jit(solution)/shard_map/ppermute | solution.py:424
  12.6 12.4 %collective-permute-start.6 = (bf16[256,1024]{1,0:T(8,128)(2,1)S(1)}, bf16[256,1024]{1,0:T(8,128)(2,1)S(1)}, u32[]{:S(2)}, u32[]{:S(2)}) collective-permute-start(bf16[256,1024]{1,0:T(8,128)(2,1)S(1)} %merge_tokens.1.refs_0_), channel_id=1, source_target_pairs={{0,8},{4,12},{8,0},{12,4},{16,24},{20,28},{24,16},{28,20},{1,9},{5... | collective-permute-start | bytes 1572872 | tf_op jit(solution)/shard_map/ppermute | solution.py:234
  14.3 10.9 %collective-permute-start.3 = (bf16[256,1024]{1,0:T(8,128)(2,1)S(1)}, bf16[256,1024]{1,0:T(8,128)(2,1)S(1)}, u32[]{:S(2)}, u32[]{:S(2)}) collective-permute-start(bf16[256,1024]{1,0:T(8,128)(2,1)S(1)} %merge_tokens.1.refs_0_), channel_id=1, source_target_pairs={{0,4},{4,0},{8,16},{12,20},{16,8},{20,12},{24,28},{28,24},{1,5},{5... | collective-permute-start | bytes 1572872 | tf_op jit(solution)/shard_map/ppermute | solution.py:234
  14.3 27.3 %collective-permute-start.12 = (bf16[2,256,1024]{2,1,0:T(8,128)(2,1)S(1)}, bf16[2,256,1024]{2,1,0:T(8,128)(2,1)S(1)}, u32[]{:S(2)}, u32[]{:S(2)}) collective-permute-start(bf16[2,256,1024]{2,1,0:T(8,128)(2,1)S(1)} %get-tuple-element.28.grad_ref.refs_7_), channel_id=1, source_target_pairs={{0,2},{1,3},{2,0},{3,1},{4,6},{5,7},{6,4},{7,5},{8,10},{9,11},{10,... | collective-permute-start | bytes 3145736 | tf_op jit(solution)/shard_map/ppermute | solution.py:424
  15.8 27.4 %collective-permute-start.11 = (bf16[2,256,1024]{2,1,0:T(8,128)(2,1)S(1)}, bf16[2,256,1024]{2,1,0:T(8,128)(2,1)S(1)}, u32[]{:S(2)}, u32[]{:S(2)}) collective-permute-start(bf16[2,256,1024]{2,1,0:T(8,128)(2,1)S(1)} %get-tuple-element.28.grad_ref.refs_7_), channel_id=1, source_target_pairs={{0,1},{1,0},{2,3},{3,2},{4,5},{5,4},{6,7},{7,6},{8,9},{9,8},{10,11... | collective-permute-start | bytes 3145736 | tf_op jit(solution)/shard_map/ppermute | solution.py:424
  25.1 3.5 %collective-permute-start.7 = (bf16[256,1024]{1,0:T(8,128)(2,1)S(1)}, bf16[256,1024]{1,0:T(8,128)(2,1)S(1)}, u32[]{:S(2)}, u32[]{:S(2)}) collective-permute-start(bf16[256,1024]{1,0:T(8,128)(2,1)S(1)} %pass_on.9), channel_id=1, source_target_pairs={{0,4},{4,0},{8,16},{12,20},{16,8},{20,12},{24,28},{28,24},{1,5},{5... | collective-permute-start | bytes 1572872 | tf_op jit(solution)/shard_map/ppermute | solution.py:234
  25.2 16.2 %collective-permute-start.4 = (bf16[256,1024]{1,0:T(8,128)(2,1)S(1)}, bf16[256,1024]{1,0:T(8,128)(2,1)S(1)}, u32[]{:S(2)}, u32[]{:S(2)}) collective-permute-start(bf16[256,1024]{1,0:T(8,128)(2,1)S(1)} %pass_on.6), channel_id=1, source_target_pairs={{0,8},{4,12},{8,0},{12,4},{16,24},{20,28},{24,16},{28,20},{1,9},{5... | collective-permute-start | bytes 1572872 | tf_op jit(solution)/shard_map/ppermute | solution.py:234
  28.7 22.2 %collective-permute-start.8 = (bf16[256,1024]{1,0:T(8,128)(2,1)S(1)}, bf16[256,1024]{1,0:T(8,128)(2,1)S(1)}, u32[]{:S(2)}, u32[]{:S(2)}) collective-permute-start(bf16[256,1024]{1,0:T(8,128)(2,1)S(1)} %pass_on.10), channel_id=1, source_target_pairs={{0,8},{4,12},{8,0},{12,4},{16,24},{20,28},{24,16},{28,20},{1,9},{5... | collective-permute-start | bytes 1572872 | tf_op jit(solution)/shard_map/ppermute | solution.py:234
  41.5 9.4 %collective-permute-start.5 = (bf16[256,1024]{1,0:T(8,128)(2,1)S(1)}, bf16[256,1024]{1,0:T(8,128)(2,1)S(1)}, u32[]{:S(2)}, u32[]{:S(2)}) collective-permute-start(bf16[256,1024]{1,0:T(8,128)(2,1)S(1)} %pass_on.7), channel_id=1, source_target_pairs={{0,4},{4,0},{8,16},{12,20},{16,8},{20,12},{24,28},{28,24},{1,5},{5... | collective-permute-start | bytes 1572872 | tf_op jit(solution)/shard_map/ppermute | solution.py:234
  41.6 14.4 %collective-permute-start.14 = (bf16[256,1024]{1,0:T(8,128)(2,1)S(1)}, bf16[256,1024]{1,0:T(8,128)(2,1)S(1)}, u32[]{:S(2)}, u32[]{:S(2)}) collective-permute-start(bf16[256,1024]{1,0:T(8,128)(2,1)S(1)} %slice_bitcast_fusion), channel_id=1, source_target_pairs={{0,1},{1,0},{2,3},{3,2},{4,5},{5,4},{6,7},{7,6},{8,9},{9,8},{10,11... | collective-permute-start | bytes 1572872 | tf_op jit(solution)/shard_map/ppermute | solution.py:424
  43.2 14.1 %collective-permute-start.13 = (bf16[256,1024]{1,0:T(8,128)(2,1)S(1)}, bf16[256,1024]{1,0:T(8,128)(2,1)S(1)}, u32[]{:S(2)}, u32[]{:S(2)}) collective-permute-start(bf16[256,1024]{1,0:T(8,128)(2,1)S(1)} %slice_bitcast_fusion.1), channel_id=1, source_target_pairs={{0,2},{1,3},{2,0},{3,1},{4,6},{5,7},{6,4},{7,5},{8,10},{9,11},{10,... | collective-permute-start | bytes 1572872 | tf_op jit(solution)/shard_map/ppermute | solution.py:424
  51.0 16.9 %collective-permute-start.9 = (bf16[256,1024]{1,0:T(8,128)(2,1)S(1)}, bf16[256,1024]{1,0:T(8,128)(2,1)S(1)}, u32[]{:S(2)}, u32[]{:S(2)}) collective-permute-start(bf16[256,1024]{1,0:T(8,128)(2,1)S(1)} %pass_on.8), channel_id=1, source_target_pairs={{0,8},{4,12},{8,0},{12,4},{16,24},{20,28},{24,16},{28,20},{1,9},{5... | collective-permute-start | bytes 1572872 | tf_op jit(solution)/shard_map/ppermute | solution.py:234
  53.6 14.3 %collective-permute-start.10 = (bf16[256,1024]{1,0:T(8,128)(2,1)S(1)}, bf16[256,1024]{1,0:T(8,128)(2,1)S(1)}, u32[]{:S(2)}, u32[]{:S(2)}) collective-permute-start(bf16[256,1024]{1,0:T(8,128)(2,1)S(1)} %pass_on.11), channel_id=1, source_target_pairs={{0,4},{4,0},{8,16},{12,20},{16,8},{20,12},{24,28},{28,24},{1,5},{5... | collective-permute-start | bytes 1572872 | tf_op jit(solution)/shard_map/ppermute | solution.py:234
  60.8 4.2 %collective-permute-start.15 = (bf16[512,2048]{1,0:T(8,128)(2,1)S(1)}, bf16[512,2048]{1,0:T(8,128)(2,1)S(1)}, u32[]{:S(2)}, u32[]{:S(2)}) collective-permute-start(bf16[512,2048]{1,0:T(8,128)(2,1)S(1)} %weight_sums.3), channel_id=1, source_target_pairs={{0,4},{4,0},{1,5},{5,1},{2,6},{6,2},{3,7},{7,3},{8,12},{12,8},{9,1... | collective-permute-start | bytes 6291464 | tf_op jit(solution)/shard_map/ppermute | solution.py:428

commit v4 on v3

--- a/solution.py
+++ b/solution.py
@@ -16,6 +16,7 @@
 MIB = 1 << 20
 ROWS = (((1,), (1,)), ((), ()))
 COLS = (((0,), (0,)), ((), ()))
+LENGTHY = pl.CostEstimate(flops=32 << 30, bytes_accessed=1 << 23, transcendentals=0)
 BRIEF = pl.CostEstimate(flops=1, bytes_accessed=1, transcendentals=0)
 NEAR = pl.BlockSpec(memory_space=pltpu.VMEM)
 FAR = pl.BlockSpec(memory_space=pl.ANY)
@@ -312,88 +313,154 @@
     )(even, odd, partials)
 
 
-def weight_kernel(counts, places, *refs):
-    size, data_count, side, away = counts
-    pieces = 2 * size - 1
-    piece_refs, grad_refs = refs[:pieces], refs[pieces:-5]
-    out_ref, x_s, grad_s, x_sem, grad_sem = refs[-5:]
-    own_ref, even_refs, odd_refs = piece_refs[0], piece_refs[1 : size], piece_refs[size:]
-    me = lax.axis_index("tensor")
-    tokens = x_s.shape[0] // data_count
-    own_tokens = tokens // size
-    rows, width = x_s.shape[1], grad_s.shape[2]
-
-    def fetch(ref, slot, k):
-        owner = lax.rem(me - slot + size, size)
-        start = pl.multiple_of(k * tokens + owner * own_tokens, own_tokens)
-        source = ref.at[pl.ds(k * own_tokens, own_tokens), pl.ds(side * rows, rows)]
-        return pltpu.make_async_copy(source, x_s.at[pl.ds(start, own_tokens)], x_sem.at[slot, k])
-
+def piece_cases(me, size, even_refs, odd_refs):
     odd_place = lax.rem(me, 2) == 1
-    for k in range(data_count):
-        fetch(own_ref, 0, k).start()
+    even_place = jnp.logical_not(odd_place)
+    cases = []
     for slot in range(1, size):
         behind = me >= slot
-        came = (
-            (behind & odd_place, even_refs[slot - 1]),
-            (behind & jnp.logical_not(odd_place), odd_refs[slot - 1]),
-            (jnp.logical_not(behind) & odd_place, odd_refs[size - slot - 1]),
-            (jnp.logical_not(behind) & jnp.logical_not(odd_place), even_refs[size - slot - 1]),
+        beyond = jnp.logical_not(behind)
+        back = size - slot
+        cases.append(
+            (
+                (behind & odd_place, even_refs, slot),
+                (behind & even_place, odd_refs, slot),
+                (beyond & odd_place, odd_refs, back),
+                (beyond & even_place, even_refs, back),
+            )
         )
-        for condition, ref in came:
+    return [[(c, refs[hop - 1] if hop <= len(refs) else None, hop == size - 1) for c, refs, hop in case] for case in cases]
+
+
+def early_kernel(size, side, places, *refs):
+    out_ref, x_s = refs[-2:]
+    hops = size - 2
+    own_ref, even_refs, odd_refs = refs[0], refs[1 : 1 + hops], refs[1 + hops : 1 + 2 * hops]
+    grad_refs = views(refs[1 + 2 * hops : -2], places)
+    count = len(grad_refs) // 2
+    me = lax.axis_index("tensor")
+    tokens, rows = x_s.shape[1:]
+    own_tokens = tokens // size
+    width = out_ref.shape[1] // 2
+
+    def place(ref, slot):
+        start = pl.multiple_of(lax.rem(me - slot + size, size) * own_tokens, own_tokens)
+        for k in range(count):
+            if ref is None:
+                values = jnp.zeros((own_tokens, rows), x_s.dtype)
+            else:
+                values = ref[k * own_tokens : (k + 1) * own_tokens, side * rows : (side + 1) * rows]
+            x_s[k, pl.ds(start, own_tokens), :] = values
+
+    place(own_ref, 0)
+    for slot, case in enumerate(piece_cases(me, size, even_refs, odd_refs), 1):
+        for condition, ref, _ in case:
 
             @pl.when(condition)
             def _(ref=ref, slot=slot):
-                for k in range(data_count):
-                    fetch(ref, slot, k).start()
-
-    loads = []
+                place(ref, slot)
+
+    turned = [x_s[k].T for k in range(count)]
     for j in range(2):
-        for k in range(data_count):
-            which, half = places[k][j]
-            source = grad_refs[which] if half is None else grad_refs[which].at[half]
-            target = grad_s.at[j, pl.ds(k * tokens, tokens)]
-            loads.append(pltpu.make_async_copy(source, target, grad_sem.at[j, k]))
-    for copy in loads:
-        copy.start()
-    for slot in range(size):
-        for k in range(data_count):
-            fetch(own_ref, slot, k).wait()
+        total = None
+        for k in range(count):
+            term = jnp.dot(turned[k], grad_refs[j * count + k][...], preferred_element_type=jnp.float32)
+            total = term if total is None else total + term
+        out_ref[:, j * width : (j + 1) * width] = total
+
+
+def late_kernel(size, side, places, *refs):
+    sum_ref, refs = refs[0], refs[1:]
+    out_ref, x_s, last_s, grad_s = refs[-4:]
+    hops = size - 1
+    own_ref, even_refs, odd_refs = refs[0], refs[1 : 1 + hops], refs[1 + hops : 1 + 2 * hops]
+    grad_refs = views(refs[1 + 2 * hops : -4], places)
+    count = len(grad_refs) // 2
+    me = lax.axis_index("tensor")
+    tokens, rows = x_s.shape
+    own_tokens = tokens // size
+    width = out_ref.shape[1] // 2
+    columns = slice(side * rows, (side + 1) * rows)
+    far = slice((count - 1) * own_tokens, count * own_tokens)
+
+    def place(ref, slot):
+        start = pl.multiple_of(lax.rem(me - slot + size, size) * own_tokens, own_tokens)
+        x_s[pl.ds(start, own_tokens), :] = ref[far, columns]
+
+    place(own_ref, 0)
+    last_s[...] = jnp.zeros_like(last_s)
+    for slot, case in enumerate(piece_cases(me, size, even_refs, odd_refs), 1):
+        for condition, ref, last in case:
+
+            @pl.when(condition)
+            def _(ref=ref, slot=slot, last=last):
+                place(ref, slot)
+                if last:
+                    last_s[...] = ref[: last_s.shape[0], columns]
+
+    owner = jnp.where(me == 0, size - 1, 0)
+    start = pl.multiple_of(owner * own_tokens, own_tokens)
     for j in range(2):
-        for copy in loads[j * data_count : (j + 1) * data_count]:
-            copy.wait()
-        total = lax.dot_general(x_s[...], grad_s[j], COLS, preferred_element_type=jnp.float32)
-        out_ref[:, j * width : (j + 1) * width] = total.astype(out_ref.dtype)
-
-
-def weight_sums(own, even, odd, grads, mirrors, side, dtype):
-    size, data_count = len(even) + 1, len(grads)
+        for k in range(count - 1):
+            grad_s[j, k * own_tokens : (k + 1) * own_tokens, :] = grad_refs[j * count + k][pl.ds(start, own_tokens), :]
+    turned, last_turned = x_s[...].T, last_s[...].T
+    for j in range(2):
+        at = slice(j * width, (j + 1) * width)
+        total = jnp.dot(turned, grad_refs[j * count + count - 1][...], preferred_element_type=jnp.float32)
+        total = total + jnp.dot(last_turned, grad_s[j], preferred_element_type=jnp.float32)
+        out_ref[:, at] = (sum_ref[:, at] + total).astype(out_ref.dtype)
+
+
+def views(refs, places):
+    return [refs[which] if half is None else refs[which].at[half] for which, half in places]
+
+
+def grad_operands(grads):
+    arrays, places = [], []
+    for array, half in grads:
+        if not any(array is a for a in arrays):
+            arrays.append(array)
+        places.append(([i for i, a in enumerate(arrays) if a is array][0], half))
+    return arrays, places
+
+
+def early_sums(own, even, odd, grads, mirrors, side, size):
     rows = own.shape[1] // mirrors
-    arrays, places = [], []
-    for pair in grads:
-        place = []
-        for array, half in pair:
-            if not any(array is a for a in arrays):
-                arrays.append(array)
-            place.append(([i for i, a in enumerate(arrays) if a is array][0], half))
-        places.append(place)
-    tokens, width = arrays[0].shape[-2:]
-    pieces = [own] + even + odd
-    return pl.pallas_call(
-        functools.partial(weight_kernel, (size, data_count, side, mirrors), places),
-        in_specs=[FAR] * (len(pieces) + len(arrays)),
+    grads, places = grad_operands([g for half in grads for g in half[:-1]])
+    tokens, width = grads[0].shape[-2:]
+    pieces = [own, *even, *odd]
+    return pl.pallas_call(
+        functools.partial(early_kernel, size, side, places),
+        in_specs=[NEAR] * (len(pieces) + len(grads)),
+        out_specs=NEAR,
+        out_shape=jax.ShapeDtypeStruct((rows, 2 * width), jnp.float32),
+        scratch_shapes=[pltpu.VMEM((len(places) // 2, tokens, rows), jnp.bfloat16)],
+        cost_estimate=LENGTHY,
+        compiler_params=params(24),
+        name="early_sums",
+    )(*pieces, *grads)
+
+
+def late_sums(sums, own, even, odd, grads, mirrors, side, size, dtype):
+    rows = own.shape[1] // mirrors
+    grads, places = grad_operands([g for half in grads for g in half])
+    tokens, width = grads[0].shape[-2:]
+    pieces = [sums, own, *even, *odd]
+    last = (len(places) // 2 - 1) * (tokens // size)
+    return pl.pallas_call(
+        functools.partial(late_kernel, size, side, places),
+        in_specs=[NEAR] * (len(pieces) + len(grads)),
         out_specs=NEAR,
         out_shape=jax.ShapeDtypeStruct((rows, 2 * width), dtype),
         scratch_shapes=[
-            pltpu.VMEM((data_count * tokens, rows), jnp.bfloat16),
-            pltpu.VMEM((2, data_count * tokens, width), jnp.bfloat16),
-            pltpu.SemaphoreType.DMA((size, data_count)),
-            pltpu.SemaphoreType.DMA((2, data_count)),
+            pltpu.VMEM((tokens, rows), jnp.bfloat16),
+            pltpu.VMEM((last, rows), jnp.bfloat16),
+            pltpu.VMEM((2, last, width), jnp.bfloat16),
         ],
-        cost_estimate=pl.CostEstimate(flops=32 << 30, bytes_accessed=1 << 23, transcendentals=0),
-        compiler_params=params(32),
-        name="weight_sums",
-    )(*pieces, *arrays)
+        cost_estimate=LENGTHY,
+        compiler_params=params(24),
+        name="late_sums",
+    )(*pieces, *grads)
 
 
 def average_kernel(replicas, own_ref, *refs):
@@ -441,8 +508,8 @@
                 else:
                     moved = array if part is None else array[part]
                     blocks[distance ^ bit] = (swap(moved, bit, size), None)
-        found.append(blocks)
-    return [(found[0][d], found[1][d]) for d in range(size)]
+        found.append([blocks[d] for d in range(size)])
+    return found
 
 
 def shards(layer_input, qk_weight, query_proj, key_proj, value_proj, head_grad, doc_ids):
@@ -458,8 +525,6 @@
     )
     columns, grads = lax.optimization_barrier((columns, grads))
     piece = merge_tokens(columns)
-
-    gathered_grads = gathered(grads, data_count)
     partials = input_partials(grads, weight_rows, qk_weight, size, data_count)
     partials = partials.reshape(size, *piece.shape)
 
@@ -472,11 +537,14 @@
         even.append(hop(send_even, 0, size, mirrors))
         odd.append(hop(send_odd, 1, size, mirrors))
 
+    grads = gathered(grads, data_count)
+    sides = range(mirrors)
+    early = [early_sums(piece, even[:-2], odd[:-2], grads, mirrors, side, size) for side in sides]
     away = []
-    for r in range(1, mirrors):
-        sums = weight_sums(own_piece, even[:-1], odd[:-1], gathered_grads, mirrors, r, jnp.bfloat16)
-        away.append(across(sums, r, mirrors))
-    own = weight_sums(own_piece, even[:-1], odd[:-1], gathered_grads, mirrors, 0, jnp.float32)
+    for side in sides[1:]:
+        sums = late_sums(early[side], own_piece, even[:-1], odd[:-1], grads, mirrors, side, size, jnp.bfloat16)
+        away.append(across(sums, side, mirrors))
+    own = late_sums(early[0], own_piece, even[:-1], odd[:-1], grads, mirrors, 0, size, jnp.float32)
     weight_grad = average(own, away, mirrors * data_count)
     last_even, last_odd, weight_grad = lax.optimization_barrier((even[-1], odd[-1], weight_grad))
     input_grad = finish(last_even, last_odd, partials, data_count)[None]

time: 69 us -> 66.8 us (0.968)
  waiting for transfers between devices: 15.9 us -> 13.9 us
    ppermute x8, waiting for transfers between devices: 10.6 us -> 6.55 us  [hop(): return lax.ppermute(values, ('tensor', 'mirror'), pairs)]
    ppermute x1, waiting for transfers between devices: 0.78 us -> 2.76 us  [across(): lax.ppermute(values, 'mirror', [(i, (i + distance) % size) for i in range...]
    pallas_call x2 -> x4, Pallas kernels: 6.89 us -> 6.79 us  [the longest x2 4.03 us: early_sums(): pl.pallas_call(functools.partial(early_kernel, size, side, places), in_sp...]
  transfers between devices with their start and end apart: 16 -> 16, of which waited for: 7 -> 7; matrix products, arithmetic and copies ran while one was open for 0% -> 0% of each run, Pallas kernels for 31% -> 32%
where the time goes in v4:
time: 66.8 us; the launch traced here: 66.7 us
  starting transfers between devices  28.6 us (43%)
  Pallas kernels  23.3 us (35%)
  waiting for transfers between devices  13.9 us (21%)
  between operations  0.79 us (1%)
    ppermute x8, starting transfers between devices, hop(): return lax.ppermute(values, ('tensor', 'mirror'), pairs)  18.3 us
    ppermute x7, starting transfers between devices, swap(): return lax.ppermute(values, 'dp', [(i, i ^ distance) for i in range(size)])  10.3 us
    ppermute x8, waiting for transfers between devices, hop(): return lax.ppermute(values, ('tensor', 'mirror'), pairs)  6.55 us
    pallas_call x1, Pallas kernels, input_partials(): pl.pallas_call(functools.partial(partials_kernel, pieces), in_specs=[NEAR...  5.92 us
    pallas_call x1, Pallas kernels, attention_grads(): pl.pallas_call(attention_kernel, in_specs=[FAR] * 7, out_specs=[NEAR, NEA...  5.39 us
    ppermute x7, waiting for transfers between devices, swap(): return lax.ppermute(values, 'dp', [(i, i ^ distance) for i in range(size)])  4.56 us
    pallas_call x2, Pallas kernels, early_sums(): pl.pallas_call(functools.partial(early_kernel, size, side, places), in_sp...  4.03 us
    pallas_call x1, Pallas kernels, average(): pl.pallas_call(functools.partial(average_kernel, replicas), grid=(rows //...  2.84 us
  transfers between devices with their start and end apart: 16, of which 7 were waited for; matrix products, arithmetic and copies ran while one was open for 0% of the time, Pallas kernels for 32%

profile of v4, /device:TPU:0, one launch (start us, length us, event | category | flops | bytes accessed | tf_op | source)
XLA Modules:
  0.0 66.7 jit_solution(14211604304274490702)
XLA Ops:
  0.6 1.2 %split_columns.1 = (bf16[64,1024]{1,0:T(8,128)(2,1)S(1)}, bf16[64,1024]{1,0:T(8,128)(2,1)S(1)}, bf16[64,1024]{1,0:T(8,128)(2,1)S(1)}, bf16[64,1024]{1,0:T(8,128)(2,1)S(1)}) custom-call(bf16[64,4096]{1,0:T(8,128)(2,1)} %bitcast.24), custom_call_target="tpu_custom_call" | custom-call | flops 1 | bytes 1 | tf_op jit(solution)/shard_map/split_columns/pallas_call | solution.py:196
  1.8 3.0 %collective-permute-start = (bf16[64,1024]{1,0:T(8,128)(2,1)S(1)}, bf16[64,1024]{1,0:T(8,128)(2,1)S(1)}, u32[]{:S(2)}, u32[]{:S(2)}) collective-permute-start(bf16[64,1024]{1,0:T(8,128)(2,1)S(1)} %get-tuple-element.20), channel_id=1, source_target_pairs={{0,1},{1,0},{2,3},{3,2},{4,5},{5,4},{6,7},{7,6},{8,9},{9,8},{10,11... | collective-permute-start | bytes 393224 | tf_op jit(solution)/shard_map/ppermute | solution.py:491
  4.8 1.5 %collective-permute-start.1 = (bf16[64,1024]{1,0:T(8,128)(2,1)S(1)}, bf16[64,1024]{1,0:T(8,128)(2,1)S(1)}, u32[]{:S(2)}, u32[]{:S(2)}) collective-permute-start(bf16[64,1024]{1,0:T(8,128)(2,1)S(1)} %get-tuple-element.21), channel_id=1, source_target_pairs={{0,2},{1,3},{2,0},{3,1},{4,6},{5,7},{6,4},{7,5},{8,10},{9,11},{10,... | collective-permute-start | bytes 393224 | tf_op jit(solution)/shard_map/ppermute | solution.py:491
  6.3 0.0 collective-permute-start.2
  6.3 5.4 %attention_grads.1 = (bf16[2,256,1024]{2,1,0:T(8,128)(2,1)S(1)}, bf16[3072,2,1024]{2,1,0:T(2,128)(2,1)S(1)}) custom-call(s32[2,1,128]{2,1,0:T(1,128)} %bitcast.25, f32[2,128,128]{2,1,0:T(8,128)} %constant.2.clone.table_ref, bf16[256,1024]{1,0:T(8,128)(2,1)} %bitcast.19, bf16[256,1024]{1,0:T(8,128)(2,1)} %bitcast.20, bf16[256,1024]{1,0:T(8,128)(2,1)} %bitcast.21, ...), custom_call_target="tpu_custom_call" | custom-call | flops 1 | bytes 1 | tf_op jit(solution)/shard_map/attention_grads/pallas_call | solution.py:103
  11.7 0.0 collective-permute-done.refs_1_
  11.7 0.8 %collective-permute-done.1.refs_2_ = bf16[64,1024]{1,0:T(8,128)(2,1)S(1)} collective-permute-done((bf16[64,1024]{1,0:T(8,128)(2,1)S(1)}, bf16[64,1024]{1,0:T(8,128)(2,1)S(1)}, u32[]{:S(2)}, u32[]{:S(2)}) %collective-permute-start.1) | collective-permute-done | bytes 131104 | tf_op jit(solution)/shard_map/ppermute | solution.py:491
  12.6 0.0 collective-permute-done.2.refs_3_
  12.6 1.6 %collective-permute-start.6 = (bf16[256,1024]{1,0:T(8,128)(2,1)S(1)}, bf16[256,1024]{1,0:T(8,128)(2,1)S(1)}, u32[]{:S(2)}, u32[]{:S(2)}) collective-permute-start(bf16[256,1024]{1,0:T(8,128)(2,1)S(1)} %merge_tokens.1.refs_0_.refs_1_), channel_id=1, source_target_pairs={{0,8},{4,12},{8,0},{12,4},{16,24},{20,28},{24,16},{28,20},{1,9},{5... | collective-permute-start | bytes 1572872 | tf_op jit(solution)/shard_map/ppermute | solution.py:235
  14.3 0.0 collective-permute-start.3
  14.3 1.5 %collective-permute-start.12 = (bf16[2,256,1024]{2,1,0:T(8,128)(2,1)S(1)}, bf16[2,256,1024]{2,1,0:T(8,128)(2,1)S(1)}, u32[]{:S(2)}, u32[]{:S(2)}) collective-permute-start(bf16[2,256,1024]{2,1,0:T(8,128)(2,1)S(1)} %get-tuple-element.28.grad_ref.refs_5_.refs_8_), channel_id=1, source_target_pairs={{0,2},{1,3},{2,0},{3,1},{4,6},{5,7},{6,4},{7,5},{8,10},{9,11},{10,... | collective-permute-start | bytes 3145736 | tf_op jit(solution)/shard_map/ppermute | solution.py:491
  15.8 1.2 %collective-permute-start.11 = (bf16[2,256,1024]{2,1,0:T(8,128)(2,1)S(1)}, bf16[2,256,1024]{2,1,0:T(8,128)(2,1)S(1)}, u32[]{:S(2)}, u32[]{:S(2)}) collective-permute-start(bf16[2,256,1024]{2,1,0:T(8,128)(2,1)S(1)} %get-tuple-element.28.grad_ref.refs_5_.refs_8_), channel_id=1, source_target_pairs={{0,1},{1,0},{2,3},{3,2},{4,5},{5,4},{6,7},{7,6},{8,9},{9,8},{10,11... | collective-permute-start | bytes 3145736 | tf_op jit(solution)/shard_map/ppermute | solution.py:491
  16.9 5.9 %input_partials.1 = bf16[4,4,64,1024]{3,2,1,0:T(8,128)(2,1)S(1)} custom-call(bf16[2,256,1024]{2,1,0:T(8,128)(2,1)S(1)} %get-tuple-element.28.grad_ref.refs_5_.refs_8_, bf16[3072,2,1024]{2,1,0:T(2,128)(2,1)S(1)} %get-tuple-element.29.near_ref, bf16[4096,2,1024]{2,1,0:T(2,128)(2,1)} %w_ref.3), custom_call_target="tpu_custom_call" | custom-call | flops 1 | bytes 1 | tf_op jit(solution)/shard_map/input_partials/pallas_call | solution.py:160
  22.9 2.2 %collective-permute-done.6.flow_ref.refs_1_.refs_2_ = bf16[256,1024]{1,0:T(8,128)(2,1)S(1)} collective-permute-done((bf16[256,1024]{1,0:T(8,128)(2,1)S(1)}, bf16[256,1024]{1,0:T(8,128)(2,1)S(1)}, u32[]{:S(2)}, u32[]{:S(2)}) %collective-permute-start.6) | collective-permute-done | bytes 524320 | tf_op jit(solution)/shard_map/ppermute | solution.py:235
  25.1 0.1 collective-permute-start.7
  25.2 0.0 collective-permute-done.3.flow_ref.refs_3_.refs_5_
  25.2 0.1 pass_on.6
  25.2 3.4 %collective-permute-start.4 = (bf16[256,1024]{1,0:T(8,128)(2,1)S(1)}, bf16[256,1024]{1,0:T(8,128)(2,1)S(1)}, u32[]{:S(2)}, u32[]{:S(2)}) collective-permute-start(bf16[256,1024]{1,0:T(8,128)(2,1)S(1)} %pass_on.6), channel_id=1, source_target_pairs={{0,8},{4,12},{8,0},{12,4},{16,24},{20,28},{24,16},{28,20},{1,9},{5... | collective-permute-start | bytes 1572872 | tf_op jit(solution)/shard_map/ppermute | solution.py:235
  28.6 0.0 collective-permute-done.7.flow_ref.refs_4_.refs_6_
  28.7 10.5 %collective-permute-start.8 = (bf16[256,1024]{1,0:T(8,128)(2,1)S(1)}, bf16[256,1024]{1,0:T(8,128)(2,1)S(1)}, u32[]{:S(2)}, u32[]{:S(2)}) collective-permute-start(bf16[256,1024]{1,0:T(8,128)(2,1)S(1)} %pass_on.10), channel_id=1, source_target_pairs={{0,8},{4,12},{8,0},{12,4},{16,24},{20,28},{24,16},{28,20},{1,9},{5... | collective-permute-start | bytes 1572872 | tf_op jit(solution)/shard_map/ppermute | solution.py:235
  39.2 2.3 %collective-permute-done.4.flow_ref.refs_2_.refs_3_ = bf16[256,1024]{1,0:T(8,128)(2,1)S(1)} collective-permute-done((bf16[256,1024]{1,0:T(8,128)(2,1)S(1)}, bf16[256,1024]{1,0:T(8,128)(2,1)S(1)}, u32[]{:S(2)}, u32[]{:S(2)}) %collective-permute-start.4) | collective-permute-done | bytes 524320 | tf_op jit(solution)/shard_map/ppermute | solution.py:235
  41.5 0.1 collective-permute-start.5
  41.6 0.0 collective-permute-done.12.refs_7_.refs_10_
  41.6 1.5 %collective-permute-start.14 = (bf16[256,1024]{1,0:T(8,128)(2,1)S(1)}, bf16[256,1024]{1,0:T(8,128)(2,1)S(1)}, u32[]{:S(2)}, u32[]{:S(2)}) collective-permute-start(bf16[256,1024]{1,0:T(8,128)(2,1)S(1)} %slice_bitcast_fusion), channel_id=1, source_target_pairs={{0,1},{1,0},{2,3},{3,2},{4,5},{5,4},{6,7},{7,6},{8,9},{9,8},{10,11... | collective-permute-start | bytes 1572872 | tf_op jit(solution)/shard_map/ppermute | solution.py:491
  43.1 0.0 collective-permute-done.11.refs_6_.refs_9_
  43.2 1.5 %collective-permute-start.13 = (bf16[256,1024]{1,0:T(8,128)(2,1)S(1)}, bf16[256,1024]{1,0:T(8,128)(2,1)S(1)}, u32[]{:S(2)}, u32[]{:S(2)}) collective-permute-start(bf16[256,1024]{1,0:T(8,128)(2,1)S(1)} %slice_bitcast_fusion.1), channel_id=1, source_target_pairs={{0,2},{1,3},{2,0},{3,1},{4,6},{5,7},{6,4},{7,5},{8,10},{9,11},{10,... | collective-permute-start | bytes 1572872 | tf_op jit(solution)/shard_map/ppermute | solution.py:491
  44.7 1.9 %early_sums.3.refs_0_ = f32[512,2048]{1,0:T(8,128)S(1)} custom-call(bf16[256,1024]{1,0:T(8,128)(2,1)S(1)} %merge_tokens.1.refs_0_.refs_1_, bf16[256,1024]{1,0:T(8,128)(2,1)S(1)} %collective-permute-done.6.flow_ref.refs_1_.refs_2_, bf16[256,1024]{1,0:T(8,128)(2,1)S(1)} %collective-permute-done.4.flow_ref.refs_2_.refs_3_, ...), custom_call_target="tpu_custom_call" | custom-call | flops 34359738368 | bytes 8388608 | tf_op jit(solution)/shard_map/early_sums/pallas_call | solution.py:432
  46.6 2.1 %early_sums.2.refs_0_ = f32[512,2048]{1,0:T(8,128)S(1)} custom-call(bf16[256,1024]{1,0:T(8,128)(2,1)S(1)} %merge_tokens.1.refs_0_.refs_1_, bf16[256,1024]{1,0:T(8,128)(2,1)S(1)} %collective-permute-done.6.flow_ref.refs_1_.refs_2_, bf16[256,1024]{1,0:T(8,128)(2,1)S(1)} %collective-permute-done.4.flow_ref.refs_2_.refs_3_, ...), custom_call_target="tpu_custom_call" | custom-call | flops 34359738368 | bytes 8388608 | tf_op jit(solution)/shard_map/early_sums/pallas_call | solution.py:432
  48.8 2.1 %collective-permute-done.8.flow_ref.refs_4_ = bf16[256,1024]{1,0:T(8,128)(2,1)S(1)} collective-permute-done((bf16[256,1024]{1,0:T(8,128)(2,1)S(1)}, bf16[256,1024]{1,0:T(8,128)(2,1)S(1)}, u32[]{:S(2)}, u32[]{:S(2)}) %collective-permute-start.8) | collective-permute-done | bytes 524320 | tf_op jit(solution)/shard_map/ppermute | solution.py:235
  50.9 0.0 collective-permute-done.5.flow_ref.refs_7_
  50.9 0.1 pass_on.8
  51.0 2.6 %collective-permute-start.9 = (bf16[256,1024]{1,0:T(8,128)(2,1)S(1)}, bf16[256,1024]{1,0:T(8,128)(2,1)S(1)}, u32[]{:S(2)}, u32[]{:S(2)}) collective-permute-start(bf16[256,1024]{1,0:T(8,128)(2,1)S(1)} %pass_on.8), channel_id=1, source_target_pairs={{0,8},{4,12},{8,0},{12,4},{16,24},{20,28},{24,16},{28,20},{1,9},{5... | collective-permute-start | bytes 1572872 | tf_op jit(solution)/shard_map/ppermute | solution.py:235
  53.6 0.0 collective-permute-start.10
  53.6 2.4 %collective-permute-done.14.refs_12_ = bf16[256,1024]{1,0:T(8,128)(2,1)S(1)} collective-permute-done((bf16[256,1024]{1,0:T(8,128)(2,1)S(1)}, bf16[256,1024]{1,0:T(8,128)(2,1)S(1)}, u32[]{:S(2)}, u32[]{:S(2)}) %collective-permute-start.14) | collective-permute-done | bytes 524320 | tf_op jit(solution)/shard_map/ppermute | solution.py:491
  56.0 1.3 %collective-permute-done.13.refs_11_ = bf16[256,1024]{1,0:T(8,128)(2,1)S(1)} collective-permute-done((bf16[256,1024]{1,0:T(8,128)(2,1)S(1)}, bf16[256,1024]{1,0:T(8,128)(2,1)S(1)}, u32[]{:S(2)}, u32[]{:S(2)}) %collective-permute-start.13) | collective-permute-done | bytes 524320 | tf_op jit(solution)/shard_map/ppermute | solution.py:491
  57.3 1.4 %late_sums.3 = bf16[512,2048]{1,0:T(8,128)(2,1)S(1)} custom-call(f32[512,2048]{1,0:T(8,128)S(1)} %early_sums.3.refs_0_, bf16[256,1024]{1,0:T(8,128)(2,1)S(1)} %merge_tokens.1.refs_0_.refs_1_, bf16[256,1024]{1,0:T(8,128)(2,1)S(1)} %collective-permute-done.6.flow_ref.refs_1_.refs_2_, bf16[256,1024]{1,0:T(8,128)(2,1)S(1)} %collective-permute-done.4.flow_ref.refs_2_.refs_3_, ...), custom_call_target="tpu_custom_call" | custom-call | flops 34359738368 | bytes 8388608 | tf_op jit(solution)/shard_map/late_sums/pallas_call | solution.py:450
  58.7 0.1 collective-permute-start.15
  58.7 1.4 %late_sums.2.own_ref = f32[512,2048]{1,0:T(8,128)S(1)} custom-call(f32[512,2048]{1,0:T(8,128)S(1)} %early_sums.2.refs_0_, bf16[256,1024]{1,0:T(8,128)(2,1)S(1)} %merge_tokens.1.refs_0_.refs_1_, bf16[256,1024]{1,0:T(8,128)(2,1)S(1)} %collective-permute-done.6.flow_ref.refs_1_.refs_2_, bf16[256,1024]{1,0:T(8,128)(2,1)S(1)} %collective-permute-done.4.flow_ref.refs_2_.refs_3_, ...), custom_call_target="tpu_custom_call" | custom-call | flops 34359738368 | bytes 8388608 | tf_op jit(solution)/shard_map/late_sums/pallas_call | solution.py:450
  60.1 2.8 %collective-permute-done.15.refs_0_ = bf16[512,2048]{1,0:T(8,128)(2,1)S(1)} collective-permute-done((bf16[512,2048]{1,0:T(8,128)(2,1)S(1)}, bf16[512,2048]{1,0:T(8,128)(2,1)S(1)}, u32[]{:S(2)}, u32[]{:S(2)}) %collective-permute-start.15) | collective-permute-done | bytes 2097184 | tf_op jit(solution)/shard_map/ppermute | solution.py:495
  62.9 2.8 %average_weight_grad.1 = f32[512,2,1024]{2,1,0:T(2,128)} custom-call(f32[512,2048]{1,0:T(8,128)S(1)} %late_sums.2.own_ref, bf16[512,2048]{1,0:T(8,128)(2,1)S(1)} %collective-permute-done.15.refs_0_), custom_call_target="tpu_custom_call" | custom-call | flops 1 | bytes 1 | tf_op jit(solution)/shard_map/average_weight_grad/pallas_call | solution.py:478
  65.7 0.0 collective-permute-done.9.even_ref
  65.7 0.0 collective-permute-done.10.odd_ref
  65.7 0.9 %finish_input_grad.1 = bf16[64,4096]{1,0:T(8,128)(2,1)} custom-call(bf16[256,1024]{1,0:T(8,128)(2,1)S(1)} %collective-permute-done.9.even_ref, bf16[256,1024]{1,0:T(8,128)(2,1)S(1)} %collective-permute-done.10.odd_ref, bf16[4,256,1024]{2,1,0:T(8,128)(2,1)S(1)} %bitcast.18), custom_call_target="tpu_custom_call" | custom-call | flops 1 | bytes 1 | tf_op jit(solution)/shard_map/finish_input_grad/pallas_call | solution.py:305
  (7 shorter events, 0.2 us)
Async XLA Ops:
  1.8 9.9 %collective-permute-start = (bf16[64,1024]{1,0:T(8,128)(2,1)S(1)}, bf16[64,1024]{1,0:T(8,128)(2,1)S(1)}, u32[]{:S(2)}, u32[]{:S(2)}) collective-permute-start(bf16[64,1024]{1,0:T(8,128)(2,1)S(1)} %get-tuple-element.20), channel_id=1, source_target_pairs={{0,1},{1,0},{2,3},{3,2},{4,5},{5,4},{6,7},{7,6},{8,9},{9,8},{10,11... | collective-permute-start | bytes 393224 | tf_op jit(solution)/shard_map/ppermute | solution.py:491
  4.8 7.8 %collective-permute-start.1 = (bf16[64,1024]{1,0:T(8,128)(2,1)S(1)}, bf16[64,1024]{1,0:T(8,128)(2,1)S(1)}, u32[]{:S(2)}, u32[]{:S(2)}) collective-permute-start(bf16[64,1024]{1,0:T(8,128)(2,1)S(1)} %get-tuple-element.21), channel_id=1, source_target_pairs={{0,2},{1,3},{2,0},{3,1},{4,6},{5,7},{6,4},{7,5},{8,10},{9,11},{10,... | collective-permute-start | bytes 393224 | tf_op jit(solution)/shard_map/ppermute | solution.py:491
  6.3 6.3 %collective-permute-start.2 = (bf16[64,1024]{1,0:T(8,128)(2,1)S(1)}, bf16[64,1024]{1,0:T(8,128)(2,1)S(1)}, u32[]{:S(2)}, u32[]{:S(2)}) collective-permute-start(bf16[64,1024]{1,0:T(8,128)(2,1)S(1)} %get-tuple-element.22), channel_id=1, source_target_pairs={{0,3},{1,2},{2,1},{3,0},{4,7},{5,6},{6,5},{7,4},{8,11},{9,10},{10,... | collective-permute-start | bytes 393224 | tf_op jit(solution)/shard_map/ppermute | solution.py:491
  12.6 12.4 %collective-permute-start.6 = (bf16[256,1024]{1,0:T(8,128)(2,1)S(1)}, bf16[256,1024]{1,0:T(8,128)(2,1)S(1)}, u32[]{:S(2)}, u32[]{:S(2)}) collective-permute-start(bf16[256,1024]{1,0:T(8,128)(2,1)S(1)} %merge_tokens.1.refs_0_.refs_1_), channel_id=1, source_target_pairs={{0,8},{4,12},{8,0},{12,4},{16,24},{20,28},{24,16},{28,20},{1,9},{5... | collective-permute-start | bytes 1572872 | tf_op jit(solution)/shard_map/ppermute | solution.py:235
  14.3 10.9 %collective-permute-start.3 = (bf16[256,1024]{1,0:T(8,128)(2,1)S(1)}, bf16[256,1024]{1,0:T(8,128)(2,1)S(1)}, u32[]{:S(2)}, u32[]{:S(2)}) collective-permute-start(bf16[256,1024]{1,0:T(8,128)(2,1)S(1)} %merge_tokens.1.refs_0_.refs_1_), channel_id=1, source_target_pairs={{0,4},{4,0},{8,16},{12,20},{16,8},{20,12},{24,28},{28,24},{1,5},{5... | collective-permute-start | bytes 1572872 | tf_op jit(solution)/shard_map/ppermute | solution.py:235
  14.3 27.3 %collective-permute-start.12 = (bf16[2,256,1024]{2,1,0:T(8,128)(2,1)S(1)}, bf16[2,256,1024]{2,1,0:T(8,128)(2,1)S(1)}, u32[]{:S(2)}, u32[]{:S(2)}) collective-permute-start(bf16[2,256,1024]{2,1,0:T(8,128)(2,1)S(1)} %get-tuple-element.28.grad_ref.refs_5_.refs_8_), channel_id=1, source_target_pairs={{0,2},{1,3},{2,0},{3,1},{4,6},{5,7},{6,4},{7,5},{8,10},{9,11},{10,... | collective-permute-start | bytes 3145736 | tf_op jit(solution)/shard_map/ppermute | solution.py:491
  15.8 27.4 %collective-permute-start.11 = (bf16[2,256,1024]{2,1,0:T(8,128)(2,1)S(1)}, bf16[2,256,1024]{2,1,0:T(8,128)(2,1)S(1)}, u32[]{:S(2)}, u32[]{:S(2)}) collective-permute-start(bf16[2,256,1024]{2,1,0:T(8,128)(2,1)S(1)} %get-tuple-element.28.grad_ref.refs_5_.refs_8_), channel_id=1, source_target_pairs={{0,1},{1,0},{2,3},{3,2},{4,5},{5,4},{6,7},{7,6},{8,9},{9,8},{10,11... | collective-permute-start | bytes 3145736 | tf_op jit(solution)/shard_map/ppermute | solution.py:491
  25.1 3.5 %collective-permute-start.7 = (bf16[256,1024]{1,0:T(8,128)(2,1)S(1)}, bf16[256,1024]{1,0:T(8,128)(2,1)S(1)}, u32[]{:S(2)}, u32[]{:S(2)}) collective-permute-start(bf16[256,1024]{1,0:T(8,128)(2,1)S(1)} %pass_on.9), channel_id=1, source_target_pairs={{0,4},{4,0},{8,16},{12,20},{16,8},{20,12},{24,28},{28,24},{1,5},{5... | collective-permute-start | bytes 1572872 | tf_op jit(solution)/shard_map/ppermute | solution.py:235
  25.2 16.2 %collective-permute-start.4 = (bf16[256,1024]{1,0:T(8,128)(2,1)S(1)}, bf16[256,1024]{1,0:T(8,128)(2,1)S(1)}, u32[]{:S(2)}, u32[]{:S(2)}) collective-permute-start(bf16[256,1024]{1,0:T(8,128)(2,1)S(1)} %pass_on.6), channel_id=1, source_target_pairs={{0,8},{4,12},{8,0},{12,4},{16,24},{20,28},{24,16},{28,20},{1,9},{5... | collective-permute-start | bytes 1572872 | tf_op jit(solution)/shard_map/ppermute | solution.py:235
  28.7 22.2 %collective-permute-start.8 = (bf16[256,1024]{1,0:T(8,128)(2,1)S(1)}, bf16[256,1024]{1,0:T(8,128)(2,1)S(1)}, u32[]{:S(2)}, u32[]{:S(2)}) collective-permute-start(bf16[256,1024]{1,0:T(8,128)(2,1)S(1)} %pass_on.10), channel_id=1, source_target_pairs={{0,8},{4,12},{8,0},{12,4},{16,24},{20,28},{24,16},{28,20},{1,9},{5... | collective-permute-start | bytes 1572872 | tf_op jit(solution)/shard_map/ppermute | solution.py:235
  41.5 9.4 %collective-permute-start.5 = (bf16[256,1024]{1,0:T(8,128)(2,1)S(1)}, bf16[256,1024]{1,0:T(8,128)(2,1)S(1)}, u32[]{:S(2)}, u32[]{:S(2)}) collective-permute-start(bf16[256,1024]{1,0:T(8,128)(2,1)S(1)} %pass_on.7), channel_id=1, source_target_pairs={{0,4},{4,0},{8,16},{12,20},{16,8},{20,12},{24,28},{28,24},{1,5},{5... | collective-permute-start | bytes 1572872 | tf_op jit(solution)/shard_map/ppermute | solution.py:235
  41.6 14.4 %collective-permute-start.14 = (bf16[256,1024]{1,0:T(8,128)(2,1)S(1)}, bf16[256,1024]{1,0:T(8,128)(2,1)S(1)}, u32[]{:S(2)}, u32[]{:S(2)}) collective-permute-start(bf16[256,1024]{1,0:T(8,128)(2,1)S(1)} %slice_bitcast_fusion), channel_id=1, source_target_pairs={{0,1},{1,0},{2,3},{3,2},{4,5},{5,4},{6,7},{7,6},{8,9},{9,8},{10,11... | collective-permute-start | bytes 1572872 | tf_op jit(solution)/shard_map/ppermute | solution.py:491
  43.2 14.1 %collective-permute-start.13 = (bf16[256,1024]{1,0:T(8,128)(2,1)S(1)}, bf16[256,1024]{1,0:T(8,128)(2,1)S(1)}, u32[]{:S(2)}, u32[]{:S(2)}) collective-permute-start(bf16[256,1024]{1,0:T(8,128)(2,1)S(1)} %slice_bitcast_fusion.1), channel_id=1, source_target_pairs={{0,2},{1,3},{2,0},{3,1},{4,6},{5,7},{6,4},{7,5},{8,10},{9,11},{10,... | collective-permute-start | bytes 1572872 | tf_op jit(solution)/shard_map/ppermute | solution.py:491
  51.0 14.8 %collective-permute-start.9 = (bf16[256,1024]{1,0:T(8,128)(2,1)S(1)}, bf16[256,1024]{1,0:T(8,128)(2,1)S(1)}, u32[]{:S(2)}, u32[]{:S(2)}) collective-permute-start(bf16[256,1024]{1,0:T(8,128)(2,1)S(1)} %pass_on.8), channel_id=1, source_target_pairs={{0,8},{4,12},{8,0},{12,4},{16,24},{20,28},{24,16},{28,20},{1,9},{5... | collective-permute-start | bytes 1572872 | tf_op jit(solution)/shard_map/ppermute | solution.py:235
  53.6 12.2 %collective-permute-start.10 = (bf16[256,1024]{1,0:T(8,128)(2,1)S(1)}, bf16[256,1024]{1,0:T(8,128)(2,1)S(1)}, u32[]{:S(2)}, u32[]{:S(2)}) collective-permute-start(bf16[256,1024]{1,0:T(8,128)(2,1)S(1)} %pass_on.11), channel_id=1, source_target_pairs={{0,4},{4,0},{8,16},{12,20},{16,8},{20,12},{24,28},{28,24},{1,5},{5... | collective-permute-start | bytes 1572872 | tf_op jit(solution)/shard_map/ppermute | solution.py:235
  58.7 4.2 %collective-permute-start.15 = (bf16[512,2048]{1,0:T(8,128)(2,1)S(1)}, bf16[512,2048]{1,0:T(8,128)(2,1)S(1)}, u32[]{:S(2)}, u32[]{:S(2)}) collective-permute-start(bf16[512,2048]{1,0:T(8,128)(2,1)S(1)} %late_sums.3), channel_id=1, source_target_pairs={{0,4},{4,0},{1,5},{5,1},{2,6},{6,2},{3,7},{7,3},{8,12},{12,8},{9,1... | collective-permute-start | bytes 6291464 | tf_op jit(solution)/shard_map/ppermute | solution.py:495

commit v5 on v4

--- a/solution.py
+++ b/solution.py
@@ -13,6 +13,7 @@
 SEQ = 128
 GROUP = 4
 SPAN = 1024
+PARTS = 1
 MIB = 1 << 20
 ROWS = (((1,), (1,)), ((), ()))
 COLS = (((0,), (0,)), ((), ()))
@@ -241,76 +242,98 @@
     return (partner >= 0) & (partner < size), ahead
 
 
-def pass_kernel(parity, distance, flow_ref, part_ref, out_ref):
-    size = part_ref.shape[0]
+def pass_kernel(parity, distance, part, flow_ref, partial_ref, out_ref):
+    size = partial_ref.shape[0]
     me = lax.axis_index("tensor")
     ahead = lax.rem(me, 2) == parity
     owner = jnp.where(ahead, me + distance, me - distance)
     active = (owner >= 0) & (owner < size)
     flows, _ = has_partner(me, 1 - parity, size)
     owner = jnp.clip(owner, 0, size - 1)
+    height = out_ref.shape[0]
+    rows = slice(part * height, (part + 1) * height)
+    flow_rows = rows if flow_ref.shape[0] > height else slice(0, height)
 
     @pl.when(flows & active)
     def _():
-        out_ref[...] = flow_ref[...] + part_ref[owner]
+        out_ref[...] = flow_ref[flow_rows] + partial_ref[owner, rows]
 
     @pl.when(jnp.logical_not(flows))
     def _():
-        out_ref[...] = part_ref[owner]
+        out_ref[...] = partial_ref[owner, rows]
 
     @pl.when(flows & jnp.logical_not(active))
     def _():
-        out_ref[...] = flow_ref[...]
-
-
-def pass_on(flow, partials, parity, distance):
-    return pl.pallas_call(
-        functools.partial(pass_kernel, parity, distance),
+        out_ref[...] = flow_ref[flow_rows]
+
+
+def pass_on(flow, partials, parity, distance, part, parts):
+    _, rows, columns = partials.shape
+    return pl.pallas_call(
+        functools.partial(pass_kernel, parity, distance, part),
         in_specs=[NEAR, NEAR],
         out_specs=NEAR,
-        out_shape=jax.ShapeDtypeStruct(flow.shape, flow.dtype),
+        out_shape=jax.ShapeDtypeStruct((rows // parts, columns), partials.dtype),
         cost_estimate=BRIEF,
         compiler_params=params(16),
         name="pass_on",
     )(flow, partials)
 
 
-def finish_kernel(blocks, even_ref, odd_ref, part_ref, out_ref):
-    size = part_ref.shape[0]
+def finish_kernel(blocks, parts, *refs):
+    odd_refs, even_refs, (partial_ref, out_ref) = refs[:parts], refs[parts : 2 * parts], refs[2 * parts :]
+    size = partial_ref.shape[0]
     me = lax.axis_index("tensor")
     tokens, columns = out_ref.shape[0], out_ref.shape[1] // blocks
-
-    def store(total):
+    has_even, has_odd = (has_partner(me, parity, size)[0] for parity in range(2))
+
+    def store(*flows):
         for block in range(blocks):
-            rows = total[block * tokens : (block + 1) * tokens]
-            out_ref[:, block * columns : (block + 1) * columns] = rows.astype(out_ref.dtype)
-
-    for parity, (flow_ref, other_ref) in enumerate(((odd_ref, even_ref), (even_ref, odd_ref))):
-        alone = jnp.logical_not(has_partner(me, 1 - parity, size)[0])
-
-        @pl.when(alone)
-        def _(other_ref=other_ref):
-            store(part_ref[me].astype(jnp.float32) + other_ref[...].astype(jnp.float32))
-
-    both = has_partner(me, 0, size)[0] & has_partner(me, 1, size)[0]
-
-    @pl.when(both)
+            per = blocks // parts
+            rows = slice(block % per * tokens, (block % per + 1) * tokens)
+            total = partial_ref[me, block * tokens : (block + 1) * tokens].astype(jnp.float32)
+            for refs in flows:
+                total = total + refs[block // per][rows].astype(jnp.float32)
+            out_ref[:, block * columns : (block + 1) * columns] = total.astype(out_ref.dtype)
+
+    @pl.when(has_even & has_odd)
     def _():
-        total = part_ref[me].astype(jnp.float32) + even_ref[...].astype(jnp.float32)
-        store(total + odd_ref[...].astype(jnp.float32))
+        store(even_refs, odd_refs)
+
+    @pl.when(jnp.logical_not(has_odd))
+    def _():
+        store(even_refs)
+
+    @pl.when(jnp.logical_not(has_even))
+    def _():
+        store(odd_refs)
 
 
 def finish(even, odd, partials, blocks):
-    rows, columns = even.shape
-    return pl.pallas_call(
-        functools.partial(finish_kernel, blocks),
-        in_specs=[NEAR, NEAR, NEAR],
+    _, rows, columns = partials.shape
+    return pl.pallas_call(
+        functools.partial(finish_kernel, blocks, len(even)),
+        in_specs=[NEAR] * (2 * len(even) + 1),
         out_specs=NEAR,
-        out_shape=jax.ShapeDtypeStruct((rows // blocks, columns * blocks), even.dtype),
+        out_shape=jax.ShapeDtypeStruct((rows // blocks, columns * blocks), partials.dtype),
         cost_estimate=BRIEF,
         compiler_params=params(16),
         name="finish_input_grad",
-    )(even, odd, partials)
+    )(*odd, *even, partials)
+
+
+def grouped(refs, counts):
+    groups, at = [], 0
+    for count in counts:
+        groups.append(refs[at : at + count])
+        at += count
+    return groups
+
+
+def replica_rows(parts, k, own_tokens):
+    height = parts[0].shape[0]
+    start = k * own_tokens % height
+    return parts[k * own_tokens // height], slice(start, start + own_tokens)
 
 
 def piece_cases(me, size, even_refs, odd_refs):
@@ -332,11 +355,11 @@
     return [[(c, refs[hop - 1] if hop <= len(refs) else None, hop == size - 1) for c, refs, hop in case] for case in cases]
 
 
-def early_kernel(size, side, places, *refs):
+def early_kernel(size, side, counts, places, *refs):
     out_ref, x_s = refs[-2:]
-    hops = size - 2
-    own_ref, even_refs, odd_refs = refs[0], refs[1 : 1 + hops], refs[1 + hops : 1 + 2 * hops]
-    grad_refs = views(refs[1 + 2 * hops : -2], places)
+    pieces = grouped(refs[: sum(counts)], counts)
+    own_ref, odd_refs, even_refs = pieces[0], pieces[1 : size - 1], pieces[size - 1 :]
+    grad_refs = views(refs[sum(counts) : -2], places)
     count = len(grad_refs) // 2
     me = lax.axis_index("tensor")
     tokens, rows = x_s.shape[1:]
@@ -349,7 +372,8 @@
             if ref is None:
                 values = jnp.zeros((own_tokens, rows), x_s.dtype)
             else:
-                values = ref[k * own_tokens : (k + 1) * own_tokens, side * rows : (side + 1) * rows]
+                part, at = replica_rows(ref, k, own_tokens)
+                values = part[at, side * rows : (side + 1) * rows]
             x_s[k, pl.ds(start, own_tokens), :] = values
 
     place(own_ref, 0)
@@ -369,23 +393,23 @@
         out_ref[:, j * width : (j + 1) * width] = total
 
 
-def late_kernel(size, side, places, *refs):
+def late_kernel(size, side, counts, places, *refs):
     sum_ref, refs = refs[0], refs[1:]
     out_ref, x_s, last_s, grad_s = refs[-4:]
-    hops = size - 1
-    own_ref, even_refs, odd_refs = refs[0], refs[1 : 1 + hops], refs[1 + hops : 1 + 2 * hops]
-    grad_refs = views(refs[1 + 2 * hops : -4], places)
+    pieces = grouped(refs[: sum(counts)], counts)
+    own_ref, odd_refs, even_refs = pieces[0], pieces[1:size], pieces[size:]
+    grad_refs = views(refs[sum(counts) : -4], places)
     count = len(grad_refs) // 2
     me = lax.axis_index("tensor")
     tokens, rows = x_s.shape
     own_tokens = tokens // size
     width = out_ref.shape[1] // 2
     columns = slice(side * rows, (side + 1) * rows)
-    far = slice((count - 1) * own_tokens, count * own_tokens)
 
     def place(ref, slot):
         start = pl.multiple_of(lax.rem(me - slot + size, size) * own_tokens, own_tokens)
-        x_s[pl.ds(start, own_tokens), :] = ref[far, columns]
+        part, at = replica_rows(ref, count - 1, own_tokens)
+        x_s[pl.ds(start, own_tokens), :] = part[at, columns]
 
     place(own_ref, 0)
     last_s[...] = jnp.zeros_like(last_s)
@@ -396,7 +420,9 @@
             def _(ref=ref, slot=slot, last=last):
                 place(ref, slot)
                 if last:
-                    last_s[...] = ref[: last_s.shape[0], columns]
+                    for k in range(count - 1):
+                        part, at = replica_rows(ref, k, own_tokens)
+                        last_s[k * own_tokens : (k + 1) * own_tokens, :] = part[at, columns]
 
     owner = jnp.where(me == 0, size - 1, 0)
     start = pl.multiple_of(owner * own_tokens, own_tokens)
@@ -428,9 +454,10 @@
     rows = own.shape[1] // mirrors
     grads, places = grad_operands([g for half in grads for g in half[:-1]])
     tokens, width = grads[0].shape[-2:]
-    pieces = [own, *even, *odd]
-    return pl.pallas_call(
-        functools.partial(early_kernel, size, side, places),
+    counts = [1] + [len(parts) for parts in odd + even]
+    pieces = [own] + [part for parts in odd + even for part in parts]
+    return pl.pallas_call(
+        functools.partial(early_kernel, size, side, counts, places),
         in_specs=[NEAR] * (len(pieces) + len(grads)),
         out_specs=NEAR,
         out_shape=jax.ShapeDtypeStruct((rows, 2 * width), jnp.float32),
@@ -445,10 +472,11 @@
     rows = own.shape[1] // mirrors
     grads, places = grad_operands([g for half in grads for g in half])
     tokens, width = grads[0].shape[-2:]
-    pieces = [sums, own, *even, *odd]
+    counts = [1] + [len(parts) for parts in odd + even]
+    pieces = [sums, own] + [part for parts in odd + even for part in parts]
     last = (len(places) // 2 - 1) * (tokens // size)
     return pl.pallas_call(
-        functools.partial(late_kernel, size, side, places),
+        functools.partial(late_kernel, size, side, counts, places),
         in_specs=[NEAR] * (len(pieces) + len(grads)),
         out_specs=NEAR,
         out_shape=jax.ShapeDtypeStruct((rows, 2 * width), dtype),
@@ -528,14 +556,18 @@
     partials = input_partials(grads, weight_rows, qk_weight, size, data_count)
     partials = partials.reshape(size, *piece.shape)
 
-    even, odd = [hop(piece, 0, size, mirrors)], [hop(piece, 1, size, mirrors)]
+    even, odd = [(hop(piece, 0, size, mirrors),)], [(hop(piece, 1, size, mirrors),)]
+    own_piece = piece
     for distance in range(size - 1, 0, -1):
-        send_even = pass_on(odd[-1], partials, 0, distance)
-        send_odd = pass_on(even[-1], partials, 1, distance)
-        if distance == 1:
-            send_even, send_odd, own_piece = lax.optimization_barrier((send_even, send_odd, piece))
-        even.append(hop(send_even, 0, size, mirrors))
-        odd.append(hop(send_odd, 1, size, mirrors))
+        send = {}
+        for part in range(PARTS):
+            for parity, came in ((0, odd[-1]), (1, even[-1])):
+                flow = came[part % len(came)]
+                send[parity, part] = pass_on(flow, partials, parity, distance, part, PARTS)
+                if distance == 1:
+                    send[parity, part], own_piece = lax.optimization_barrier((send[parity, part], own_piece))
+        for parity, hops in ((0, even), (1, odd)):
+            hops.append(tuple(hop(send[parity, part], parity, size, mirrors) for part in range(PARTS)))
 
     grads = gathered(grads, data_count)
     sides = range(mirrors)
@@ -546,7 +578,7 @@
         away.append(across(sums, side, mirrors))
     own = late_sums(early[0], own_piece, even[:-1], odd[:-1], grads, mirrors, 0, size, jnp.float32)
     weight_grad = average(own, away, mirrors * data_count)
-    last_even, last_odd, weight_grad = lax.optimization_barrier((even[-1], odd[-1], weight_grad))
+    last_odd, last_even, weight_grad = lax.optimization_barrier((odd[-1], even[-1], weight_grad))
     input_grad = finish(last_even, last_odd, partials, data_count)[None]
     return (input_grad, weight_grad)
 

time: 66.8 us -> 65.3 us (0.978)
  starting transfers between devices: 28.6 us -> 22.9 us
  waiting for transfers between devices: 13.9 us -> 17.8 us
    ppermute x8, waiting for transfers between devices: 6.55 us -> 13.5 us  [hop(): return lax.ppermute(values, ('tensor', 'mirror'), pairs)]
    ppermute x8, starting transfers between devices: 18.3 us -> 12.9 us  [hop(): return lax.ppermute(values, ('tensor', 'mirror'), pairs)]
    ppermute x7, waiting for transfers between devices: 4.56 us -> 1.58 us  [swap(): return lax.ppermute(values, 'dp', [(i, i ^ distance) for i in range(size)])]
  transfers between devices with their start and end apart: 16 -> 16, of which waited for: 7 -> 7; matrix products, arithmetic and copies ran while one was open for 0% -> 0% of each run, Pallas kernels for 32% -> 33%
where the time goes in v5:
time: 65.3 us; the launch traced here: 65 us
  Pallas kernels  23.3 us (36%)
  starting transfers between devices  22.9 us (35%)
  waiting for transfers between devices  17.8 us (27%)
  between operations  0.81 us (1%)
    ppermute x8, waiting for transfers between devices, hop(): return lax.ppermute(values, ('tensor', 'mirror'), pairs)  13.5 us
    ppermute x8, starting transfers between devices, hop(): return lax.ppermute(values, ('tensor', 'mirror'), pairs)  12.9 us
    ppermute x7, starting transfers between devices, swap(): return lax.ppermute(values, 'dp', [(i, i ^ distance) for i in range(size)])  10 us
    pallas_call x1, Pallas kernels, input_partials(): pl.pallas_call(functools.partial(partials_kernel, pieces), in_specs=[NEAR...  5.92 us
    pallas_call x1, Pallas kernels, attention_grads(): pl.pallas_call(attention_kernel, in_specs=[FAR] * 7, out_specs=[NEAR, NEA...  5.39 us
    pallas_call x2, Pallas kernels, early_sums(): pl.pallas_call(functools.partial(early_kernel, size, side, counts, places...  4.03 us
    pallas_call x1, Pallas kernels, average(): pl.pallas_call(functools.partial(average_kernel, replicas), grid=(rows //...  2.84 us
    pallas_call x2, Pallas kernels, late_sums(): pl.pallas_call(functools.partial(late_kernel, size, side, counts, places)...  2.76 us
  transfers between devices with their start and end apart: 16, of which 7 were waited for; matrix products, arithmetic and copies ran while one was open for 0% of the time, Pallas kernels for 33%

profile of v5, /device:TPU:0, one launch (start us, length us, event | category | flops | bytes accessed | tf_op | source)
XLA Modules:
  0.0 65.0 jit_solution(2945290670142577985)
XLA Ops:
  0.6 1.2 %split_columns.1 = (bf16[64,1024]{1,0:T(8,128)(2,1)S(1)}, bf16[64,1024]{1,0:T(8,128)(2,1)S(1)}, bf16[64,1024]{1,0:T(8,128)(2,1)S(1)}, bf16[64,1024]{1,0:T(8,128)(2,1)S(1)}) custom-call(bf16[64,4096]{1,0:T(8,128)(2,1)} %bitcast.24), custom_call_target="tpu_custom_call" | custom-call | flops 1 | bytes 1 | tf_op jit(solution)/shard_map/split_columns/pallas_call | solution.py:197
  1.8 3.0 %collective-permute-start = (bf16[64,1024]{1,0:T(8,128)(2,1)S(1)}, bf16[64,1024]{1,0:T(8,128)(2,1)S(1)}, u32[]{:S(2)}, u32[]{:S(2)}) collective-permute-start(bf16[64,1024]{1,0:T(8,128)(2,1)S(1)} %get-tuple-element.21), channel_id=1, source_target_pairs={{0,1},{1,0},{2,3},{3,2},{4,5},{5,4},{6,7},{7,6},{8,9},{9,8},{10,11... | collective-permute-start | bytes 393224 | tf_op jit(solution)/shard_map/ppermute | solution.py:519
  4.8 1.5 %collective-permute-start.1 = (bf16[64,1024]{1,0:T(8,128)(2,1)S(1)}, bf16[64,1024]{1,0:T(8,128)(2,1)S(1)}, u32[]{:S(2)}, u32[]{:S(2)}) collective-permute-start(bf16[64,1024]{1,0:T(8,128)(2,1)S(1)} %get-tuple-element.22), channel_id=1, source_target_pairs={{0,2},{1,3},{2,0},{3,1},{4,6},{5,7},{6,4},{7,5},{8,10},{9,11},{10,... | collective-permute-start | bytes 393224 | tf_op jit(solution)/shard_map/ppermute | solution.py:519
  6.3 0.0 collective-permute-start.2
  6.3 5.4 %attention_grads.1 = (bf16[2,256,1024]{2,1,0:T(8,128)(2,1)S(1)}, bf16[3072,2,1024]{2,1,0:T(2,128)(2,1)S(1)}) custom-call(s32[2,1,128]{2,1,0:T(1,128)} %bitcast.25, f32[2,128,128]{2,1,0:T(8,128)} %constant.2.clone.table_ref, bf16[256,1024]{1,0:T(8,128)(2,1)} %bitcast.19, bf16[256,1024]{1,0:T(8,128)(2,1)} %bitcast.20, bf16[256,1024]{1,0:T(8,128)(2,1)} %bitcast.21, ...), custom_call_target="tpu_custom_call" | custom-call | flops 1 | bytes 1 | tf_op jit(solution)/shard_map/attention_grads/pallas_call | solution.py:104
  11.7 0.0 collective-permute-done.refs_1_
  11.7 0.8 %collective-permute-done.1.refs_2_ = bf16[64,1024]{1,0:T(8,128)(2,1)S(1)} collective-permute-done((bf16[64,1024]{1,0:T(8,128)(2,1)S(1)}, bf16[64,1024]{1,0:T(8,128)(2,1)S(1)}, u32[]{:S(2)}, u32[]{:S(2)}) %collective-permute-start.1) | collective-permute-done | bytes 131104 | tf_op jit(solution)/shard_map/ppermute | solution.py:519
  12.6 0.0 collective-permute-done.2.refs_3_
  12.6 0.1 collective-permute-start.6
  12.7 3.1 %collective-permute-start.3 = (bf16[256,1024]{1,0:T(8,128)(2,1)S(1)}, bf16[256,1024]{1,0:T(8,128)(2,1)S(1)}, u32[]{:S(2)}, u32[]{:S(2)}) collective-permute-start(bf16[256,1024]{1,0:T(8,128)(2,1)S(1)} %merge_tokens.1.refs_0_.refs_1_), channel_id=1, source_target_pairs={{0,8},{4,12},{8,0},{12,4},{16,24},{20,28},{24,16},{28,20},{1,9},{5... | collective-permute-start | bytes 1572872 | tf_op jit(solution)/shard_map/ppermute | solution.py:236
  15.8 1.5 %collective-permute-start.12 = (bf16[2,256,1024]{2,1,0:T(8,128)(2,1)S(1)}, bf16[2,256,1024]{2,1,0:T(8,128)(2,1)S(1)}, u32[]{:S(2)}, u32[]{:S(2)}) collective-permute-start(bf16[2,256,1024]{2,1,0:T(8,128)(2,1)S(1)} %get-tuple-element.29.grad_ref.refs_5_.refs_8_), channel_id=1, source_target_pairs={{0,2},{1,3},{2,0},{3,1},{4,6},{5,7},{6,4},{7,5},{8,10},{9,11},{10,... | collective-permute-start | bytes 3145736 | tf_op jit(solution)/shard_map/ppermute | solution.py:519
  17.3 1.2 %collective-permute-start.11 = (bf16[2,256,1024]{2,1,0:T(8,128)(2,1)S(1)}, bf16[2,256,1024]{2,1,0:T(8,128)(2,1)S(1)}, u32[]{:S(2)}, u32[]{:S(2)}) collective-permute-start(bf16[2,256,1024]{2,1,0:T(8,128)(2,1)S(1)} %get-tuple-element.29.grad_ref.refs_5_.refs_8_), channel_id=1, source_target_pairs={{0,1},{1,0},{2,3},{3,2},{4,5},{5,4},{6,7},{7,6},{8,9},{9,8},{10,11... | collective-permute-start | bytes 3145736 | tf_op jit(solution)/shard_map/ppermute | solution.py:519
  18.5 5.9 %input_partials.1 = bf16[4,4,64,1024]{3,2,1,0:T(8,128)(2,1)S(1)} custom-call(bf16[2,256,1024]{2,1,0:T(8,128)(2,1)S(1)} %get-tuple-element.29.grad_ref.refs_5_.refs_8_, bf16[3072,2,1024]{2,1,0:T(2,128)(2,1)S(1)} %get-tuple-element.30.near_ref, bf16[4096,2,1024]{2,1,0:T(2,128)(2,1)} %w_ref.3), custom_call_target="tpu_custom_call" | custom-call | flops 1 | bytes 1 | tf_op jit(solution)/shard_map/input_partials/pallas_call | solution.py:161
  24.4 0.0 collective-permute-done.6.flow_ref.refs_1_.refs_2_
  24.4 0.1 pass_on.9
  24.5 2.3 %collective-permute-start.7 = (bf16[256,1024]{1,0:T(8,128)(2,1)S(1)}, bf16[256,1024]{1,0:T(8,128)(2,1)S(1)}, u32[]{:S(2)}, u32[]{:S(2)}) collective-permute-start(bf16[256,1024]{1,0:T(8,128)(2,1)S(1)} %pass_on.9), channel_id=1, source_target_pairs={{0,8},{4,12},{8,0},{12,4},{16,24},{20,28},{24,16},{28,20},{1,9},{5... | collective-permute-start | bytes 1572872 | tf_op jit(solution)/shard_map/ppermute | solution.py:236
  26.8 1.8 %collective-permute-done.3.flow_ref.refs_3_.refs_5_ = bf16[256,1024]{1,0:T(8,128)(2,1)S(1)} collective-permute-done((bf16[256,1024]{1,0:T(8,128)(2,1)S(1)}, bf16[256,1024]{1,0:T(8,128)(2,1)S(1)}, u32[]{:S(2)}, u32[]{:S(2)}) %collective-permute-start.3) | collective-permute-done | bytes 524320 | tf_op jit(solution)/shard_map/ppermute | solution.py:236
  28.6 0.1 collective-permute-start.4
  28.7 9.6 %collective-permute-done.7.flow_ref.refs_4_.refs_6_ = bf16[256,1024]{1,0:T(8,128)(2,1)S(1)} collective-permute-done((bf16[256,1024]{1,0:T(8,128)(2,1)S(1)}, bf16[256,1024]{1,0:T(8,128)(2,1)S(1)}, u32[]{:S(2)}, u32[]{:S(2)}) %collective-permute-start.7) | collective-permute-done | bytes 524320 | tf_op jit(solution)/shard_map/ppermute | solution.py:236
  38.3 0.1 collective-permute-start.8
  38.4 0.0 collective-permute-done.4.flow_ref.refs_2_.refs_3_
  38.4 0.1 pass_on.7
  38.5 3.0 %collective-permute-start.5 = (bf16[256,1024]{1,0:T(8,128)(2,1)S(1)}, bf16[256,1024]{1,0:T(8,128)(2,1)S(1)}, u32[]{:S(2)}, u32[]{:S(2)}) collective-permute-start(bf16[256,1024]{1,0:T(8,128)(2,1)S(1)} %pass_on.7), channel_id=1, source_target_pairs={{0,8},{4,12},{8,0},{12,4},{16,24},{20,28},{24,16},{28,20},{1,9},{5... | collective-permute-start | bytes 1572872 | tf_op jit(solution)/shard_map/ppermute | solution.py:236
  41.5 0.0 collective-permute-done.12.refs_7_.refs_10_
  41.5 1.3 %collective-permute-start.14 = (bf16[256,1024]{1,0:T(8,128)(2,1)S(1)}, bf16[256,1024]{1,0:T(8,128)(2,1)S(1)}, u32[]{:S(2)}, u32[]{:S(2)}) collective-permute-start(bf16[256,1024]{1,0:T(8,128)(2,1)S(1)} %slice_bitcast_fusion), channel_id=1, source_target_pairs={{0,1},{1,0},{2,3},{3,2},{4,5},{5,4},{6,7},{7,6},{8,9},{9,8},{10,11... | collective-permute-start | bytes 1572872 | tf_op jit(solution)/shard_map/ppermute | solution.py:519
  42.8 0.0 collective-permute-done.11.refs_6_.refs_9_
  42.9 1.5 %collective-permute-start.13 = (bf16[256,1024]{1,0:T(8,128)(2,1)S(1)}, bf16[256,1024]{1,0:T(8,128)(2,1)S(1)}, u32[]{:S(2)}, u32[]{:S(2)}) collective-permute-start(bf16[256,1024]{1,0:T(8,128)(2,1)S(1)} %slice_bitcast_fusion.1), channel_id=1, source_target_pairs={{0,2},{1,3},{2,0},{3,1},{4,6},{5,7},{6,4},{7,5},{8,10},{9,11},{10,... | collective-permute-start | bytes 1572872 | tf_op jit(solution)/shard_map/ppermute | solution.py:519
  44.4 1.9 %early_sums.3.refs_0_ = f32[512,2048]{1,0:T(8,128)S(1)} custom-call(bf16[256,1024]{1,0:T(8,128)(2,1)S(1)} %merge_tokens.1.refs_0_.refs_1_, bf16[256,1024]{1,0:T(8,128)(2,1)S(1)} %collective-permute-done.6.flow_ref.refs_1_.refs_2_, bf16[256,1024]{1,0:T(8,128)(2,1)S(1)} %collective-permute-done.4.flow_ref.refs_2_.refs_3_, ...), custom_call_target="tpu_custom_call" | custom-call | flops 34359738368 | bytes 8388608 | tf_op jit(solution)/shard_map/early_sums/pallas_call | solution.py:459
  46.3 2.1 %early_sums.2.refs_0_ = f32[512,2048]{1,0:T(8,128)S(1)} custom-call(bf16[256,1024]{1,0:T(8,128)(2,1)S(1)} %merge_tokens.1.refs_0_.refs_1_, bf16[256,1024]{1,0:T(8,128)(2,1)S(1)} %collective-permute-done.6.flow_ref.refs_1_.refs_2_, bf16[256,1024]{1,0:T(8,128)(2,1)S(1)} %collective-permute-done.4.flow_ref.refs_2_.refs_3_, ...), custom_call_target="tpu_custom_call" | custom-call | flops 34359738368 | bytes 8388608 | tf_op jit(solution)/shard_map/early_sums/pallas_call | solution.py:459
  48.4 0.0 collective-permute-done.8.flow_ref.refs_4_
  48.4 0.1 pass_on.11
  48.5 4.1 %collective-permute-start.10 = (bf16[256,1024]{1,0:T(8,128)(2,1)S(1)}, bf16[256,1024]{1,0:T(8,128)(2,1)S(1)}, u32[]{:S(2)}, u32[]{:S(2)}) collective-permute-start(bf16[256,1024]{1,0:T(8,128)(2,1)S(1)} %pass_on.11), channel_id=1, source_target_pairs={{0,8},{4,12},{8,0},{12,4},{16,24},{20,28},{24,16},{28,20},{1,9},{5... | collective-permute-start | bytes 1572872 | tf_op jit(solution)/shard_map/ppermute | solution.py:236
  52.6 1.2 %collective-permute-done.5.flow_ref.refs_7_ = bf16[256,1024]{1,0:T(8,128)(2,1)S(1)} collective-permute-done((bf16[256,1024]{1,0:T(8,128)(2,1)S(1)}, bf16[256,1024]{1,0:T(8,128)(2,1)S(1)}, u32[]{:S(2)}, u32[]{:S(2)}) %collective-permute-start.5) | collective-permute-done | bytes 524320 | tf_op jit(solution)/shard_map/ppermute | solution.py:236
  53.9 0.1 collective-permute-start.9
  53.9 0.0 collective-permute-done.14.refs_12_
  54.0 0.7 %collective-permute-done.13.refs_11_ = bf16[256,1024]{1,0:T(8,128)(2,1)S(1)} collective-permute-done((bf16[256,1024]{1,0:T(8,128)(2,1)S(1)}, bf16[256,1024]{1,0:T(8,128)(2,1)S(1)}, u32[]{:S(2)}, u32[]{:S(2)}) %collective-permute-start.13) | collective-permute-done | bytes 524320 | tf_op jit(solution)/shard_map/ppermute | solution.py:519
  54.7 1.4 %late_sums.3 = bf16[512,2048]{1,0:T(8,128)(2,1)S(1)} custom-call(f32[512,2048]{1,0:T(8,128)S(1)} %early_sums.3.refs_0_, bf16[256,1024]{1,0:T(8,128)(2,1)S(1)} %merge_tokens.1.refs_0_.refs_1_, bf16[256,1024]{1,0:T(8,128)(2,1)S(1)} %collective-permute-done.6.flow_ref.refs_1_.refs_2_, bf16[256,1024]{1,0:T(8,128)(2,1)S(1)} %collective-permute-done.4.flow_ref.refs_2_.refs_3_, ...), custom_call_target="tpu_custom_call" | custom-call | flops 34359738368 | bytes 8388608 | tf_op jit(solution)/shard_map/late_sums/pallas_call | solution.py:478
  56.1 0.1 collective-permute-start.15
  56.2 1.4 %late_sums.2.own_ref = f32[512,2048]{1,0:T(8,128)S(1)} custom-call(f32[512,2048]{1,0:T(8,128)S(1)} %early_sums.2.refs_0_, bf16[256,1024]{1,0:T(8,128)(2,1)S(1)} %merge_tokens.1.refs_0_.refs_1_, bf16[256,1024]{1,0:T(8,128)(2,1)S(1)} %collective-permute-done.6.flow_ref.refs_1_.refs_2_, bf16[256,1024]{1,0:T(8,128)(2,1)S(1)} %collective-permute-done.4.flow_ref.refs_2_.refs_3_, ...), custom_call_target="tpu_custom_call" | custom-call | flops 34359738368 | bytes 8388608 | tf_op jit(solution)/shard_map/late_sums/pallas_call | solution.py:478
  57.5 2.8 %collective-permute-done.15.refs_0_ = bf16[512,2048]{1,0:T(8,128)(2,1)S(1)} collective-permute-done((bf16[512,2048]{1,0:T(8,128)(2,1)S(1)}, bf16[512,2048]{1,0:T(8,128)(2,1)S(1)}, u32[]{:S(2)}, u32[]{:S(2)}) %collective-permute-start.15) | collective-permute-done | bytes 2097184 | tf_op jit(solution)/shard_map/ppermute | solution.py:523
  60.3 2.8 %average_weight_grad.1 = f32[512,2,1024]{2,1,0:T(2,128)} custom-call(f32[512,2048]{1,0:T(8,128)S(1)} %late_sums.2.own_ref, bf16[512,2048]{1,0:T(8,128)(2,1)S(1)} %collective-permute-done.15.refs_0_), custom_call_target="tpu_custom_call" | custom-call | flops 1 | bytes 1 | tf_op jit(solution)/shard_map/average_weight_grad/pallas_call | solution.py:506
  63.1 0.9 %collective-permute-done.10.refs_1_ = bf16[256,1024]{1,0:T(8,128)(2,1)S(1)} collective-permute-done((bf16[256,1024]{1,0:T(8,128)(2,1)S(1)}, bf16[256,1024]{1,0:T(8,128)(2,1)S(1)}, u32[]{:S(2)}, u32[]{:S(2)}) %collective-permute-start.10) | collective-permute-done | bytes 524320 | tf_op jit(solution)/shard_map/ppermute | solution.py:236
  64.1 0.0 collective-permute-done.9.refs_0_
  64.1 0.9 %finish_input_grad.1 = bf16[64,4096]{1,0:T(8,128)(2,1)} custom-call(bf16[256,1024]{1,0:T(8,128)(2,1)S(1)} %collective-permute-done.9.refs_0_, bf16[256,1024]{1,0:T(8,128)(2,1)S(1)} %collective-permute-done.10.refs_1_, bf16[4,256,1024]{2,1,0:T(8,128)(2,1)S(1)} %bitcast.18), custom_call_target="tpu_custom_call" | custom-call | flops 1 | bytes 1 | tf_op jit(solution)/shard_map/finish_input_grad/pallas_call | solution.py:314
  (6 shorter events, 0.2 us)
Async XLA Ops:
  1.8 9.9 %collective-permute-start = (bf16[64,1024]{1,0:T(8,128)(2,1)S(1)}, bf16[64,1024]{1,0:T(8,128)(2,1)S(1)}, u32[]{:S(2)}, u32[]{:S(2)}) collective-permute-start(bf16[64,1024]{1,0:T(8,128)(2,1)S(1)} %get-tuple-element.21), channel_id=1, source_target_pairs={{0,1},{1,0},{2,3},{3,2},{4,5},{5,4},{6,7},{7,6},{8,9},{9,8},{10,11... | collective-permute-start | bytes 393224 | tf_op jit(solution)/shard_map/ppermute | solution.py:519
  4.8 7.8 %collective-permute-start.1 = (bf16[64,1024]{1,0:T(8,128)(2,1)S(1)}, bf16[64,1024]{1,0:T(8,128)(2,1)S(1)}, u32[]{:S(2)}, u32[]{:S(2)}) collective-permute-start(bf16[64,1024]{1,0:T(8,128)(2,1)S(1)} %get-tuple-element.22), channel_id=1, source_target_pairs={{0,2},{1,3},{2,0},{3,1},{4,6},{5,7},{6,4},{7,5},{8,10},{9,11},{10,... | collective-permute-start | bytes 393224 | tf_op jit(solution)/shard_map/ppermute | solution.py:519
  6.3 6.3 %collective-permute-start.2 = (bf16[64,1024]{1,0:T(8,128)(2,1)S(1)}, bf16[64,1024]{1,0:T(8,128)(2,1)S(1)}, u32[]{:S(2)}, u32[]{:S(2)}) collective-permute-start(bf16[64,1024]{1,0:T(8,128)(2,1)S(1)} %get-tuple-element.23), channel_id=1, source_target_pairs={{0,3},{1,2},{2,1},{3,0},{4,7},{5,6},{6,5},{7,4},{8,11},{9,10},{10,... | collective-permute-start | bytes 393224 | tf_op jit(solution)/shard_map/ppermute | solution.py:519
  12.6 11.8 %collective-permute-start.6 = (bf16[256,1024]{1,0:T(8,128)(2,1)S(1)}, bf16[256,1024]{1,0:T(8,128)(2,1)S(1)}, u32[]{:S(2)}, u32[]{:S(2)}) collective-permute-start(bf16[256,1024]{1,0:T(8,128)(2,1)S(1)} %merge_tokens.1.refs_0_.refs_1_), channel_id=1, source_target_pairs={{0,4},{4,0},{8,16},{12,20},{16,8},{20,12},{24,28},{28,24},{1,5},{5... | collective-permute-start | bytes 1572872 | tf_op jit(solution)/shard_map/ppermute | solution.py:236
  12.7 15.9 %collective-permute-start.3 = (bf16[256,1024]{1,0:T(8,128)(2,1)S(1)}, bf16[256,1024]{1,0:T(8,128)(2,1)S(1)}, u32[]{:S(2)}, u32[]{:S(2)}) collective-permute-start(bf16[256,1024]{1,0:T(8,128)(2,1)S(1)} %merge_tokens.1.refs_0_.refs_1_), channel_id=1, source_target_pairs={{0,8},{4,12},{8,0},{12,4},{16,24},{20,28},{24,16},{28,20},{1,9},{5... | collective-permute-start | bytes 1572872 | tf_op jit(solution)/shard_map/ppermute | solution.py:236
  15.8 25.7 %collective-permute-start.12 = (bf16[2,256,1024]{2,1,0:T(8,128)(2,1)S(1)}, bf16[2,256,1024]{2,1,0:T(8,128)(2,1)S(1)}, u32[]{:S(2)}, u32[]{:S(2)}) collective-permute-start(bf16[2,256,1024]{2,1,0:T(8,128)(2,1)S(1)} %get-tuple-element.29.grad_ref.refs_5_.refs_8_), channel_id=1, source_target_pairs={{0,2},{1,3},{2,0},{3,1},{4,6},{5,7},{6,4},{7,5},{8,10},{9,11},{10,... | collective-permute-start | bytes 3145736 | tf_op jit(solution)/shard_map/ppermute | solution.py:519
  17.3 25.5 %collective-permute-start.11 = (bf16[2,256,1024]{2,1,0:T(8,128)(2,1)S(1)}, bf16[2,256,1024]{2,1,0:T(8,128)(2,1)S(1)}, u32[]{:S(2)}, u32[]{:S(2)}) collective-permute-start(bf16[2,256,1024]{2,1,0:T(8,128)(2,1)S(1)} %get-tuple-element.29.grad_ref.refs_5_.refs_8_), channel_id=1, source_target_pairs={{0,1},{1,0},{2,3},{3,2},{4,5},{5,4},{6,7},{7,6},{8,9},{9,8},{10,11... | collective-permute-start | bytes 3145736 | tf_op jit(solution)/shard_map/ppermute | solution.py:519
  24.5 13.8 %collective-permute-start.7 = (bf16[256,1024]{1,0:T(8,128)(2,1)S(1)}, bf16[256,1024]{1,0:T(8,128)(2,1)S(1)}, u32[]{:S(2)}, u32[]{:S(2)}) collective-permute-start(bf16[256,1024]{1,0:T(8,128)(2,1)S(1)} %pass_on.9), channel_id=1, source_target_pairs={{0,8},{4,12},{8,0},{12,4},{16,24},{20,28},{24,16},{28,20},{1,9},{5... | collective-permute-start | bytes 1572872 | tf_op jit(solution)/shard_map/ppermute | solution.py:236
  28.6 9.8 %collective-permute-start.4 = (bf16[256,1024]{1,0:T(8,128)(2,1)S(1)}, bf16[256,1024]{1,0:T(8,128)(2,1)S(1)}, u32[]{:S(2)}, u32[]{:S(2)}) collective-permute-start(bf16[256,1024]{1,0:T(8,128)(2,1)S(1)} %pass_on.6), channel_id=1, source_target_pairs={{0,4},{4,0},{8,16},{12,20},{16,8},{20,12},{24,28},{28,24},{1,5},{5... | collective-permute-start | bytes 1572872 | tf_op jit(solution)/shard_map/ppermute | solution.py:236
  38.3 10.1 %collective-permute-start.8 = (bf16[256,1024]{1,0:T(8,128)(2,1)S(1)}, bf16[256,1024]{1,0:T(8,128)(2,1)S(1)}, u32[]{:S(2)}, u32[]{:S(2)}) collective-permute-start(bf16[256,1024]{1,0:T(8,128)(2,1)S(1)} %pass_on.10), channel_id=1, source_target_pairs={{0,4},{4,0},{8,16},{12,20},{16,8},{20,12},{24,28},{28,24},{1,5},{5... | collective-permute-start | bytes 1572872 | tf_op jit(solution)/shard_map/ppermute | solution.py:236
  38.5 15.4 %collective-permute-start.5 = (bf16[256,1024]{1,0:T(8,128)(2,1)S(1)}, bf16[256,1024]{1,0:T(8,128)(2,1)S(1)}, u32[]{:S(2)}, u32[]{:S(2)}) collective-permute-start(bf16[256,1024]{1,0:T(8,128)(2,1)S(1)} %pass_on.7), channel_id=1, source_target_pairs={{0,8},{4,12},{8,0},{12,4},{16,24},{20,28},{24,16},{28,20},{1,9},{5... | collective-permute-start | bytes 1572872 | tf_op jit(solution)/shard_map/ppermute | solution.py:236
  41.5 12.4 %collective-permute-start.14 = (bf16[256,1024]{1,0:T(8,128)(2,1)S(1)}, bf16[256,1024]{1,0:T(8,128)(2,1)S(1)}, u32[]{:S(2)}, u32[]{:S(2)}) collective-permute-start(bf16[256,1024]{1,0:T(8,128)(2,1)S(1)} %slice_bitcast_fusion), channel_id=1, source_target_pairs={{0,1},{1,0},{2,3},{3,2},{4,5},{5,4},{6,7},{7,6},{8,9},{9,8},{10,11... | collective-permute-start | bytes 1572872 | tf_op jit(solution)/shard_map/ppermute | solution.py:519
  42.9 11.8 %collective-permute-start.13 = (bf16[256,1024]{1,0:T(8,128)(2,1)S(1)}, bf16[256,1024]{1,0:T(8,128)(2,1)S(1)}, u32[]{:S(2)}, u32[]{:S(2)}) collective-permute-start(bf16[256,1024]{1,0:T(8,128)(2,1)S(1)} %slice_bitcast_fusion.1), channel_id=1, source_target_pairs={{0,2},{1,3},{2,0},{3,1},{4,6},{5,7},{6,4},{7,5},{8,10},{9,11},{10,... | collective-permute-start | bytes 1572872 | tf_op jit(solution)/shard_map/ppermute | solution.py:519
  48.5 15.6 %collective-permute-start.10 = (bf16[256,1024]{1,0:T(8,128)(2,1)S(1)}, bf16[256,1024]{1,0:T(8,128)(2,1)S(1)}, u32[]{:S(2)}, u32[]{:S(2)}) collective-permute-start(bf16[256,1024]{1,0:T(8,128)(2,1)S(1)} %pass_on.11), channel_id=1, source_target_pairs={{0,8},{4,12},{8,0},{12,4},{16,24},{20,28},{24,16},{28,20},{1,9},{5... | collective-permute-start | bytes 1572872 | tf_op jit(solution)/shard_map/ppermute | solution.py:236
  53.9 10.2 %collective-permute-start.9 = (bf16[256,1024]{1,0:T(8,128)(2,1)S(1)}, bf16[256,1024]{1,0:T(8,128)(2,1)S(1)}, u32[]{:S(2)}, u32[]{:S(2)}) collective-permute-start(bf16[256,1024]{1,0:T(8,128)(2,1)S(1)} %pass_on.8), channel_id=1, source_target_pairs={{0,4},{4,0},{8,16},{12,20},{16,8},{20,12},{24,28},{28,24},{1,5},{5... | collective-permute-start | bytes 1572872 | tf_op jit(solution)/shard_map/ppermute | solution.py:236
  56.1 4.2 %collective-permute-start.15 = (bf16[512,2048]{1,0:T(8,128)(2,1)S(1)}, bf16[512,2048]{1,0:T(8,128)(2,1)S(1)}, u32[]{:S(2)}, u32[]{:S(2)}) collective-permute-start(bf16[512,2048]{1,0:T(8,128)(2,1)S(1)} %late_sums.3), channel_id=1, source_target_pairs={{0,4},{4,0},{1,5},{5,1},{2,6},{6,2},{3,7},{7,3},{8,12},{12,8},{9,1... | collective-permute-start | bytes 6291464 | tf_op jit(solution)/shard_map/ppermute | solution.py:523

commit v6 on v5

--- a/solution.py
+++ b/solution.py
@@ -281,11 +281,15 @@
 
 
 def finish_kernel(blocks, parts, *refs):
-    odd_refs, even_refs, (partial_ref, out_ref) = refs[:parts], refs[parts : 2 * parts], refs[2 * parts :]
+    odd_refs, even_refs, (partial_ref, out_ref, out_s, sem) = refs[:parts], refs[parts : 2 * parts], refs[2 * parts :]
     size = partial_ref.shape[0]
     me = lax.axis_index("tensor")
     tokens, columns = out_ref.shape[0], out_ref.shape[1] // blocks
     has_even, has_odd = (has_partner(me, parity, size)[0] for parity in range(2))
+
+    def store_block(block):
+        at = pl.ds(block * columns, columns)
+        return pltpu.make_async_copy(out_s.at[:, at], out_ref.at[:, at], sem.at[block])
 
     def store(*flows):
         for block in range(blocks):
@@ -294,7 +298,8 @@
             total = partial_ref[me, block * tokens : (block + 1) * tokens].astype(jnp.float32)
             for refs in flows:
                 total = total + refs[block // per][rows].astype(jnp.float32)
-            out_ref[:, block * columns : (block + 1) * columns] = total.astype(out_ref.dtype)
+            out_s[:, block * columns : (block + 1) * columns] = total.astype(out_s.dtype)
+            store_block(block).start()
 
     @pl.when(has_even & has_odd)
     def _():
@@ -308,14 +313,21 @@
     def _():
         store(odd_refs)
 
+    for block in range(blocks):
+        store_block(block).wait()
+
 
 def finish(even, odd, partials, blocks):
     _, rows, columns = partials.shape
     return pl.pallas_call(
         functools.partial(finish_kernel, blocks, len(even)),
         in_specs=[NEAR] * (2 * len(even) + 1),
-        out_specs=NEAR,
+        out_specs=FAR,
         out_shape=jax.ShapeDtypeStruct((rows // blocks, columns * blocks), partials.dtype),
+        scratch_shapes=[
+            pltpu.VMEM((rows // blocks, columns * blocks), partials.dtype),
+            pltpu.SemaphoreType.DMA((blocks,)),
+        ],
         cost_estimate=BRIEF,
         compiler_params=params(16),
         name="finish_input_grad",
@@ -547,7 +559,7 @@
 
     columns = split_columns(layer_input[0], mirrors, data_count)
     columns = [columns[0]] + [swap(columns[d], d, data_count) for d in range(1, data_count)]
-    near = (3 * data_count + 3) // 4 * (layer_input.shape[2] // data_count)
+    near = 3 * data_count // 4 * (layer_input.shape[2] // data_count)
     grads, weight_rows = attention_grads(
         query_proj[0], key_proj[0], value_proj[0], head_grad[0], doc_ids[0], qk_weight, near
     )

time: 65.3 us -> 65.3 us (level)
  no operation moved by 1% of the time
where the time goes in v6:
time: 65.3 us; the launch traced here: 65.1 us
  Pallas kernels  23.3 us (36%)
  starting transfers between devices  22.9 us (35%)
  waiting for transfers between devices  17.8 us (27%)
  between operations  0.97 us (1%)
    ppermute x8, waiting for transfers between devices, hop(): return lax.ppermute(values, ('tensor', 'mirror'), pairs)  13.5 us
    ppermute x8, starting transfers between devices, hop(): return lax.ppermute(values, ('tensor', 'mirror'), pairs)  12.9 us
    ppermute x7, starting transfers between devices, swap(): return lax.ppermute(values, 'dp', [(i, i ^ distance) for i in range(size)])  10 us
    pallas_call x1, Pallas kernels, input_partials(): pl.pallas_call(functools.partial(partials_kernel, pieces), in_specs=[NEAR...  5.92 us
    pallas_call x1, Pallas kernels, attention_grads(): pl.pallas_call(attention_kernel, in_specs=[FAR] * 7, out_specs=[NEAR, NEA...  5.39 us
    pallas_call x2, Pallas kernels, early_sums(): pl.pallas_call(functools.partial(early_kernel, size, side, counts, places...  4.03 us
    pallas_call x1, Pallas kernels, average(): pl.pallas_call(functools.partial(average_kernel, replicas), grid=(rows //...  2.84 us
    pallas_call x2, Pallas kernels, late_sums(): pl.pallas_call(functools.partial(late_kernel, size, side, counts, places)...  2.76 us
  transfers between devices with their start and end apart: 16, of which 7 were waited for; matrix products, arithmetic and copies ran while one was open for 0% of the time, Pallas kernels for 33%

profile of v6, /device:TPU:0, one launch (start us, length us, event | category | flops | bytes accessed | tf_op | source)
XLA Modules:
  0.0 65.1 jit_solution(8261085970193889822)
XLA Ops:
  0.6 1.2 %split_columns.1 = (bf16[64,1024]{1,0:T(8,128)(2,1)S(1)}, bf16[64,1024]{1,0:T(8,128)(2,1)S(1)}, bf16[64,1024]{1,0:T(8,128)(2,1)S(1)}, bf16[64,1024]{1,0:T(8,128)(2,1)S(1)}) custom-call(bf16[64,4096]{1,0:T(8,128)(2,1)} %bitcast.24), custom_call_target="tpu_custom_call" | custom-call | flops 1 | bytes 1 | tf_op jit(solution)/shard_map/split_columns/pallas_call | solution.py:197
  1.8 3.0 %collective-permute-start = (bf16[64,1024]{1,0:T(8,128)(2,1)S(1)}, bf16[64,1024]{1,0:T(8,128)(2,1)S(1)}, u32[]{:S(2)}, u32[]{:S(2)}) collective-permute-start(bf16[64,1024]{1,0:T(8,128)(2,1)S(1)} %get-tuple-element.21), channel_id=1, source_target_pairs={{0,1},{1,0},{2,3},{3,2},{4,5},{5,4},{6,7},{7,6},{8,9},{9,8},{10,11... | collective-permute-start | bytes 393224 | tf_op jit(solution)/shard_map/ppermute | solution.py:531
  4.8 1.5 %collective-permute-start.1 = (bf16[64,1024]{1,0:T(8,128)(2,1)S(1)}, bf16[64,1024]{1,0:T(8,128)(2,1)S(1)}, u32[]{:S(2)}, u32[]{:S(2)}) collective-permute-start(bf16[64,1024]{1,0:T(8,128)(2,1)S(1)} %get-tuple-element.22), channel_id=1, source_target_pairs={{0,2},{1,3},{2,0},{3,1},{4,6},{5,7},{6,4},{7,5},{8,10},{9,11},{10,... | collective-permute-start | bytes 393224 | tf_op jit(solution)/shard_map/ppermute | solution.py:531
  6.3 0.0 collective-permute-start.2
  6.3 5.4 %attention_grads.1 = (bf16[2,256,1024]{2,1,0:T(8,128)(2,1)S(1)}, bf16[3072,2,1024]{2,1,0:T(2,128)(2,1)S(1)}) custom-call(s32[2,1,128]{2,1,0:T(1,128)} %bitcast.25, f32[2,128,128]{2,1,0:T(8,128)} %constant.2.clone.table_ref, bf16[256,1024]{1,0:T(8,128)(2,1)} %bitcast.19, bf16[256,1024]{1,0:T(8,128)(2,1)} %bitcast.20, bf16[256,1024]{1,0:T(8,128)(2,1)} %bitcast.21, ...), custom_call_target="tpu_custom_call" | custom-call | flops 1 | bytes 1 | tf_op jit(solution)/shard_map/attention_grads/pallas_call | solution.py:104
  11.7 0.0 collective-permute-done.refs_1_
  11.7 0.8 %collective-permute-done.1.refs_2_ = bf16[64,1024]{1,0:T(8,128)(2,1)S(1)} collective-permute-done((bf16[64,1024]{1,0:T(8,128)(2,1)S(1)}, bf16[64,1024]{1,0:T(8,128)(2,1)S(1)}, u32[]{:S(2)}, u32[]{:S(2)}) %collective-permute-start.1) | collective-permute-done | bytes 131104 | tf_op jit(solution)/shard_map/ppermute | solution.py:531
  12.6 0.0 collective-permute-done.2.refs_3_
  12.6 0.1 collective-permute-start.6
  12.7 3.1 %collective-permute-start.3 = (bf16[256,1024]{1,0:T(8,128)(2,1)S(1)}, bf16[256,1024]{1,0:T(8,128)(2,1)S(1)}, u32[]{:S(2)}, u32[]{:S(2)}) collective-permute-start(bf16[256,1024]{1,0:T(8,128)(2,1)S(1)} %merge_tokens.1.refs_0_.refs_1_), channel_id=1, source_target_pairs={{0,8},{4,12},{8,0},{12,4},{16,24},{20,28},{24,16},{28,20},{1,9},{5... | collective-permute-start | bytes 1572872 | tf_op jit(solution)/shard_map/ppermute | solution.py:236
  15.8 1.5 %collective-permute-start.12 = (bf16[2,256,1024]{2,1,0:T(8,128)(2,1)S(1)}, bf16[2,256,1024]{2,1,0:T(8,128)(2,1)S(1)}, u32[]{:S(2)}, u32[]{:S(2)}) collective-permute-start(bf16[2,256,1024]{2,1,0:T(8,128)(2,1)S(1)} %get-tuple-element.29.grad_ref.refs_5_.refs_8_), channel_id=1, source_target_pairs={{0,2},{1,3},{2,0},{3,1},{4,6},{5,7},{6,4},{7,5},{8,10},{9,11},{10,... | collective-permute-start | bytes 3145736 | tf_op jit(solution)/shard_map/ppermute | solution.py:531
  17.3 1.2 %collective-permute-start.11 = (bf16[2,256,1024]{2,1,0:T(8,128)(2,1)S(1)}, bf16[2,256,1024]{2,1,0:T(8,128)(2,1)S(1)}, u32[]{:S(2)}, u32[]{:S(2)}) collective-permute-start(bf16[2,256,1024]{2,1,0:T(8,128)(2,1)S(1)} %get-tuple-element.29.grad_ref.refs_5_.refs_8_), channel_id=1, source_target_pairs={{0,1},{1,0},{2,3},{3,2},{4,5},{5,4},{6,7},{7,6},{8,9},{9,8},{10,11... | collective-permute-start | bytes 3145736 | tf_op jit(solution)/shard_map/ppermute | solution.py:531
  18.5 5.9 %input_partials.1 = bf16[4,4,64,1024]{3,2,1,0:T(8,128)(2,1)S(1)} custom-call(bf16[2,256,1024]{2,1,0:T(8,128)(2,1)S(1)} %get-tuple-element.29.grad_ref.refs_5_.refs_8_, bf16[3072,2,1024]{2,1,0:T(2,128)(2,1)S(1)} %get-tuple-element.30.near_ref, bf16[4096,2,1024]{2,1,0:T(2,128)(2,1)} %w_ref.3), custom_call_target="tpu_custom_call" | custom-call | flops 1 | bytes 1 | tf_op jit(solution)/shard_map/input_partials/pallas_call | solution.py:161
  24.4 0.0 collective-permute-done.6.flow_ref.refs_1_.refs_2_
  24.4 0.1 pass_on.9
  24.5 2.3 %collective-permute-start.7 = (bf16[256,1024]{1,0:T(8,128)(2,1)S(1)}, bf16[256,1024]{1,0:T(8,128)(2,1)S(1)}, u32[]{:S(2)}, u32[]{:S(2)}) collective-permute-start(bf16[256,1024]{1,0:T(8,128)(2,1)S(1)} %pass_on.9), channel_id=1, source_target_pairs={{0,8},{4,12},{8,0},{12,4},{16,24},{20,28},{24,16},{28,20},{1,9},{5... | collective-permute-start | bytes 1572872 | tf_op jit(solution)/shard_map/ppermute | solution.py:236
  26.8 1.8 %collective-permute-done.3.flow_ref.refs_3_.refs_5_ = bf16[256,1024]{1,0:T(8,128)(2,1)S(1)} collective-permute-done((bf16[256,1024]{1,0:T(8,128)(2,1)S(1)}, bf16[256,1024]{1,0:T(8,128)(2,1)S(1)}, u32[]{:S(2)}, u32[]{:S(2)}) %collective-permute-start.3) | collective-permute-done | bytes 524320 | tf_op jit(solution)/shard_map/ppermute | solution.py:236
  28.6 0.1 collective-permute-start.4
  28.7 9.6 %collective-permute-done.7.flow_ref.refs_4_.refs_6_ = bf16[256,1024]{1,0:T(8,128)(2,1)S(1)} collective-permute-done((bf16[256,1024]{1,0:T(8,128)(2,1)S(1)}, bf16[256,1024]{1,0:T(8,128)(2,1)S(1)}, u32[]{:S(2)}, u32[]{:S(2)}) %collective-permute-start.7) | collective-permute-done | bytes 524320 | tf_op jit(solution)/shard_map/ppermute | solution.py:236
  38.3 0.1 collective-permute-start.8
  38.4 0.0 collective-permute-done.4.flow_ref.refs_2_.refs_3_
  38.4 0.1 pass_on.7
  38.5 3.0 %collective-permute-start.5 = (bf16[256,1024]{1,0:T(8,128)(2,1)S(1)}, bf16[256,1024]{1,0:T(8,128)(2,1)S(1)}, u32[]{:S(2)}, u32[]{:S(2)}) collective-permute-start(bf16[256,1024]{1,0:T(8,128)(2,1)S(1)} %pass_on.7), channel_id=1, source_target_pairs={{0,8},{4,12},{8,0},{12,4},{16,24},{20,28},{24,16},{28,20},{1,9},{5... | collective-permute-start | bytes 1572872 | tf_op jit(solution)/shard_map/ppermute | solution.py:236
  41.5 0.0 collective-permute-done.12.refs_7_.refs_10_
  41.5 1.3 %collective-permute-start.14 = (bf16[256,1024]{1,0:T(8,128)(2,1)S(1)}, bf16[256,1024]{1,0:T(8,128)(2,1)S(1)}, u32[]{:S(2)}, u32[]{:S(2)}) collective-permute-start(bf16[256,1024]{1,0:T(8,128)(2,1)S(1)} %slice_bitcast_fusion), channel_id=1, source_target_pairs={{0,1},{1,0},{2,3},{3,2},{4,5},{5,4},{6,7},{7,6},{8,9},{9,8},{10,11... | collective-permute-start | bytes 1572872 | tf_op jit(solution)/shard_map/ppermute | solution.py:531
  42.8 0.0 collective-permute-done.11.refs_6_.refs_9_
  42.9 1.5 %collective-permute-start.13 = (bf16[256,1024]{1,0:T(8,128)(2,1)S(1)}, bf16[256,1024]{1,0:T(8,128)(2,1)S(1)}, u32[]{:S(2)}, u32[]{:S(2)}) collective-permute-start(bf16[256,1024]{1,0:T(8,128)(2,1)S(1)} %slice_bitcast_fusion.1), channel_id=1, source_target_pairs={{0,2},{1,3},{2,0},{3,1},{4,6},{5,7},{6,4},{7,5},{8,10},{9,11},{10,... | collective-permute-start | bytes 1572872 | tf_op jit(solution)/shard_map/ppermute | solution.py:531
  44.4 1.9 %early_sums.3.refs_0_ = f32[512,2048]{1,0:T(8,128)S(1)} custom-call(bf16[256,1024]{1,0:T(8,128)(2,1)S(1)} %merge_tokens.1.refs_0_.refs_1_, bf16[256,1024]{1,0:T(8,128)(2,1)S(1)} %collective-permute-done.6.flow_ref.refs_1_.refs_2_, bf16[256,1024]{1,0:T(8,128)(2,1)S(1)} %collective-permute-done.4.flow_ref.refs_2_.refs_3_, ...), custom_call_target="tpu_custom_call" | custom-call | flops 34359738368 | bytes 8388608 | tf_op jit(solution)/shard_map/early_sums/pallas_call | solution.py:471
  46.3 2.1 %early_sums.2.refs_0_ = f32[512,2048]{1,0:T(8,128)S(1)} custom-call(bf16[256,1024]{1,0:T(8,128)(2,1)S(1)} %merge_tokens.1.refs_0_.refs_1_, bf16[256,1024]{1,0:T(8,128)(2,1)S(1)} %collective-permute-done.6.flow_ref.refs_1_.refs_2_, bf16[256,1024]{1,0:T(8,128)(2,1)S(1)} %collective-permute-done.4.flow_ref.refs_2_.refs_3_, ...), custom_call_target="tpu_custom_call" | custom-call | flops 34359738368 | bytes 8388608 | tf_op jit(solution)/shard_map/early_sums/pallas_call | solution.py:471
  48.4 0.0 collective-permute-done.8.flow_ref.refs_4_
  48.4 0.1 pass_on.11
  48.5 4.1 %collective-permute-start.10 = (bf16[256,1024]{1,0:T(8,128)(2,1)S(1)}, bf16[256,1024]{1,0:T(8,128)(2,1)S(1)}, u32[]{:S(2)}, u32[]{:S(2)}) collective-permute-start(bf16[256,1024]{1,0:T(8,128)(2,1)S(1)} %pass_on.11), channel_id=1, source_target_pairs={{0,8},{4,12},{8,0},{12,4},{16,24},{20,28},{24,16},{28,20},{1,9},{5... | collective-permute-start | bytes 1572872 | tf_op jit(solution)/shard_map/ppermute | solution.py:236
  52.6 1.2 %collective-permute-done.5.flow_ref.refs_7_ = bf16[256,1024]{1,0:T(8,128)(2,1)S(1)} collective-permute-done((bf16[256,1024]{1,0:T(8,128)(2,1)S(1)}, bf16[256,1024]{1,0:T(8,128)(2,1)S(1)}, u32[]{:S(2)}, u32[]{:S(2)}) %collective-permute-start.5) | collective-permute-done | bytes 524320 | tf_op jit(solution)/shard_map/ppermute | solution.py:236
  53.9 0.1 collective-permute-start.9
  53.9 0.0 collective-permute-done.14.refs_12_
  54.0 0.7 %collective-permute-done.13.refs_11_ = bf16[256,1024]{1,0:T(8,128)(2,1)S(1)} collective-permute-done((bf16[256,1024]{1,0:T(8,128)(2,1)S(1)}, bf16[256,1024]{1,0:T(8,128)(2,1)S(1)}, u32[]{:S(2)}, u32[]{:S(2)}) %collective-permute-start.13) | collective-permute-done | bytes 524320 | tf_op jit(solution)/shard_map/ppermute | solution.py:531
  54.7 1.4 %late_sums.3 = bf16[512,2048]{1,0:T(8,128)(2,1)S(1)} custom-call(f32[512,2048]{1,0:T(8,128)S(1)} %early_sums.3.refs_0_, bf16[256,1024]{1,0:T(8,128)(2,1)S(1)} %merge_tokens.1.refs_0_.refs_1_, bf16[256,1024]{1,0:T(8,128)(2,1)S(1)} %collective-permute-done.6.flow_ref.refs_1_.refs_2_, bf16[256,1024]{1,0:T(8,128)(2,1)S(1)} %collective-permute-done.4.flow_ref.refs_2_.refs_3_, ...), custom_call_target="tpu_custom_call" | custom-call | flops 34359738368 | bytes 8388608 | tf_op jit(solution)/shard_map/late_sums/pallas_call | solution.py:490
  56.1 0.1 collective-permute-start.15
  56.2 1.4 %late_sums.2.own_ref = f32[512,2048]{1,0:T(8,128)S(1)} custom-call(f32[512,2048]{1,0:T(8,128)S(1)} %early_sums.2.refs_0_, bf16[256,1024]{1,0:T(8,128)(2,1)S(1)} %merge_tokens.1.refs_0_.refs_1_, bf16[256,1024]{1,0:T(8,128)(2,1)S(1)} %collective-permute-done.6.flow_ref.refs_1_.refs_2_, bf16[256,1024]{1,0:T(8,128)(2,1)S(1)} %collective-permute-done.4.flow_ref.refs_2_.refs_3_, ...), custom_call_target="tpu_custom_call" | custom-call | flops 34359738368 | bytes 8388608 | tf_op jit(solution)/shard_map/late_sums/pallas_call | solution.py:490
  57.5 2.8 %collective-permute-done.15.refs_0_ = bf16[512,2048]{1,0:T(8,128)(2,1)S(1)} collective-permute-done((bf16[512,2048]{1,0:T(8,128)(2,1)S(1)}, bf16[512,2048]{1,0:T(8,128)(2,1)S(1)}, u32[]{:S(2)}, u32[]{:S(2)}) %collective-permute-start.15) | collective-permute-done | bytes 2097184 | tf_op jit(solution)/shard_map/ppermute | solution.py:535
  60.3 2.8 %average_weight_grad.1 = f32[512,2,1024]{2,1,0:T(2,128)} custom-call(f32[512,2048]{1,0:T(8,128)S(1)} %late_sums.2.own_ref, bf16[512,2048]{1,0:T(8,128)(2,1)S(1)} %collective-permute-done.15.refs_0_), custom_call_target="tpu_custom_call" | custom-call | flops 1 | bytes 1 | tf_op jit(solution)/shard_map/average_weight_grad/pallas_call | solution.py:518
  63.1 0.9 %collective-permute-done.10.refs_1_ = bf16[256,1024]{1,0:T(8,128)(2,1)S(1)} collective-permute-done((bf16[256,1024]{1,0:T(8,128)(2,1)S(1)}, bf16[256,1024]{1,0:T(8,128)(2,1)S(1)}, u32[]{:S(2)}, u32[]{:S(2)}) %collective-permute-start.10) | collective-permute-done | bytes 524320 | tf_op jit(solution)/shard_map/ppermute | solution.py:236
  64.1 0.0 collective-permute-done.9.refs_0_
  64.1 0.9 %finish_input_grad.1 = bf16[64,4096]{1,0:T(8,128)(2,1)} custom-call(bf16[256,1024]{1,0:T(8,128)(2,1)S(1)} %collective-permute-done.9.refs_0_, bf16[256,1024]{1,0:T(8,128)(2,1)S(1)} %collective-permute-done.10.refs_1_, bf16[4,256,1024]{2,1,0:T(8,128)(2,1)S(1)} %bitcast.18), custom_call_target="tpu_custom_call" | custom-call | flops 1 | bytes 1 | tf_op jit(solution)/shard_map/finish_input_grad/pallas_call | solution.py:322
  (6 shorter events, 0.2 us)
Async XLA Ops:
  1.8 9.9 %collective-permute-start = (bf16[64,1024]{1,0:T(8,128)(2,1)S(1)}, bf16[64,1024]{1,0:T(8,128)(2,1)S(1)}, u32[]{:S(2)}, u32[]{:S(2)}) collective-permute-start(bf16[64,1024]{1,0:T(8,128)(2,1)S(1)} %get-tuple-element.21), channel_id=1, source_target_pairs={{0,1},{1,0},{2,3},{3,2},{4,5},{5,4},{6,7},{7,6},{8,9},{9,8},{10,11... | collective-permute-start | bytes 393224 | tf_op jit(solution)/shard_map/ppermute | solution.py:531
  4.8 7.8 %collective-permute-start.1 = (bf16[64,1024]{1,0:T(8,128)(2,1)S(1)}, bf16[64,1024]{1,0:T(8,128)(2,1)S(1)}, u32[]{:S(2)}, u32[]{:S(2)}) collective-permute-start(bf16[64,1024]{1,0:T(8,128)(2,1)S(1)} %get-tuple-element.22), channel_id=1, source_target_pairs={{0,2},{1,3},{2,0},{3,1},{4,6},{5,7},{6,4},{7,5},{8,10},{9,11},{10,... | collective-permute-start | bytes 393224 | tf_op jit(solution)/shard_map/ppermute | solution.py:531
  6.3 6.3 %collective-permute-start.2 = (bf16[64,1024]{1,0:T(8,128)(2,1)S(1)}, bf16[64,1024]{1,0:T(8,128)(2,1)S(1)}, u32[]{:S(2)}, u32[]{:S(2)}) collective-permute-start(bf16[64,1024]{1,0:T(8,128)(2,1)S(1)} %get-tuple-element.23), channel_id=1, source_target_pairs={{0,3},{1,2},{2,1},{3,0},{4,7},{5,6},{6,5},{7,4},{8,11},{9,10},{10,... | collective-permute-start | bytes 393224 | tf_op jit(solution)/shard_map/ppermute | solution.py:531
  12.6 11.8 %collective-permute-start.6 = (bf16[256,1024]{1,0:T(8,128)(2,1)S(1)}, bf16[256,1024]{1,0:T(8,128)(2,1)S(1)}, u32[]{:S(2)}, u32[]{:S(2)}) collective-permute-start(bf16[256,1024]{1,0:T(8,128)(2,1)S(1)} %merge_tokens.1.refs_0_.refs_1_), channel_id=1, source_target_pairs={{0,4},{4,0},{8,16},{12,20},{16,8},{20,12},{24,28},{28,24},{1,5},{5... | collective-permute-start | bytes 1572872 | tf_op jit(solution)/shard_map/ppermute | solution.py:236
  12.7 15.9 %collective-permute-start.3 = (bf16[256,1024]{1,0:T(8,128)(2,1)S(1)}, bf16[256,1024]{1,0:T(8,128)(2,1)S(1)}, u32[]{:S(2)}, u32[]{:S(2)}) collective-permute-start(bf16[256,1024]{1,0:T(8,128)(2,1)S(1)} %merge_tokens.1.refs_0_.refs_1_), channel_id=1, source_target_pairs={{0,8},{4,12},{8,0},{12,4},{16,24},{20,28},{24,16},{28,20},{1,9},{5... | collective-permute-start | bytes 1572872 | tf_op jit(solution)/shard_map/ppermute | solution.py:236
  15.8 25.7 %collective-permute-start.12 = (bf16[2,256,1024]{2,1,0:T(8,128)(2,1)S(1)}, bf16[2,256,1024]{2,1,0:T(8,128)(2,1)S(1)}, u32[]{:S(2)}, u32[]{:S(2)}) collective-permute-start(bf16[2,256,1024]{2,1,0:T(8,128)(2,1)S(1)} %get-tuple-element.29.grad_ref.refs_5_.refs_8_), channel_id=1, source_target_pairs={{0,2},{1,3},{2,0},{3,1},{4,6},{5,7},{6,4},{7,5},{8,10},{9,11},{10,... | collective-permute-start | bytes 3145736 | tf_op jit(solution)/shard_map/ppermute | solution.py:531
  17.3 25.5 %collective-permute-start.11 = (bf16[2,256,1024]{2,1,0:T(8,128)(2,1)S(1)}, bf16[2,256,1024]{2,1,0:T(8,128)(2,1)S(1)}, u32[]{:S(2)}, u32[]{:S(2)}) collective-permute-start(bf16[2,256,1024]{2,1,0:T(8,128)(2,1)S(1)} %get-tuple-element.29.grad_ref.refs_5_.refs_8_), channel_id=1, source_target_pairs={{0,1},{1,0},{2,3},{3,2},{4,5},{5,4},{6,7},{7,6},{8,9},{9,8},{10,11... | collective-permute-start | bytes 3145736 | tf_op jit(solution)/shard_map/ppermute | solution.py:531
  24.5 13.8 %collective-permute-start.7 = (bf16[256,1024]{1,0:T(8,128)(2,1)S(1)}, bf16[256,1024]{1,0:T(8,128)(2,1)S(1)}, u32[]{:S(2)}, u32[]{:S(2)}) collective-permute-start(bf16[256,1024]{1,0:T(8,128)(2,1)S(1)} %pass_on.9), channel_id=1, source_target_pairs={{0,8},{4,12},{8,0},{12,4},{16,24},{20,28},{24,16},{28,20},{1,9},{5... | collective-permute-start | bytes 1572872 | tf_op jit(solution)/shard_map/ppermute | solution.py:236
  28.6 9.8 %collective-permute-start.4 = (bf16[256,1024]{1,0:T(8,128)(2,1)S(1)}, bf16[256,1024]{1,0:T(8,128)(2,1)S(1)}, u32[]{:S(2)}, u32[]{:S(2)}) collective-permute-start(bf16[256,1024]{1,0:T(8,128)(2,1)S(1)} %pass_on.6), channel_id=1, source_target_pairs={{0,4},{4,0},{8,16},{12,20},{16,8},{20,12},{24,28},{28,24},{1,5},{5... | collective-permute-start | bytes 1572872 | tf_op jit(solution)/shard_map/ppermute | solution.py:236
  38.3 10.1 %collective-permute-start.8 = (bf16[256,1024]{1,0:T(8,128)(2,1)S(1)}, bf16[256,1024]{1,0:T(8,128)(2,1)S(1)}, u32[]{:S(2)}, u32[]{:S(2)}) collective-permute-start(bf16[256,1024]{1,0:T(8,128)(2,1)S(1)} %pass_on.10), channel_id=1, source_target_pairs={{0,4},{4,0},{8,16},{12,20},{16,8},{20,12},{24,28},{28,24},{1,5},{5... | collective-permute-start | bytes 1572872 | tf_op jit(solution)/shard_map/ppermute | solution.py:236
  38.5 15.4 %collective-permute-start.5 = (bf16[256,1024]{1,0:T(8,128)(2,1)S(1)}, bf16[256,1024]{1,0:T(8,128)(2,1)S(1)}, u32[]{:S(2)}, u32[]{:S(2)}) collective-permute-start(bf16[256,1024]{1,0:T(8,128)(2,1)S(1)} %pass_on.7), channel_id=1, source_target_pairs={{0,8},{4,12},{8,0},{12,4},{16,24},{20,28},{24,16},{28,20},{1,9},{5... | collective-permute-start | bytes 1572872 | tf_op jit(solution)/shard_map/ppermute | solution.py:236
  41.5 12.4 %collective-permute-start.14 = (bf16[256,1024]{1,0:T(8,128)(2,1)S(1)}, bf16[256,1024]{1,0:T(8,128)(2,1)S(1)}, u32[]{:S(2)}, u32[]{:S(2)}) collective-permute-start(bf16[256,1024]{1,0:T(8,128)(2,1)S(1)} %slice_bitcast_fusion), channel_id=1, source_target_pairs={{0,1},{1,0},{2,3},{3,2},{4,5},{5,4},{6,7},{7,6},{8,9},{9,8},{10,11... | collective-permute-start | bytes 1572872 | tf_op jit(solution)/shard_map/ppermute | solution.py:531
  42.9 11.8 %collective-permute-start.13 = (bf16[256,1024]{1,0:T(8,128)(2,1)S(1)}, bf16[256,1024]{1,0:T(8,128)(2,1)S(1)}, u32[]{:S(2)}, u32[]{:S(2)}) collective-permute-start(bf16[256,1024]{1,0:T(8,128)(2,1)S(1)} %slice_bitcast_fusion.1), channel_id=1, source_target_pairs={{0,2},{1,3},{2,0},{3,1},{4,6},{5,7},{6,4},{7,5},{8,10},{9,11},{10,... | collective-permute-start | bytes 1572872 | tf_op jit(solution)/shard_map/ppermute | solution.py:531
  48.5 15.6 %collective-permute-start.10 = (bf16[256,1024]{1,0:T(8,128)(2,1)S(1)}, bf16[256,1024]{1,0:T(8,128)(2,1)S(1)}, u32[]{:S(2)}, u32[]{:S(2)}) collective-permute-start(bf16[256,1024]{1,0:T(8,128)(2,1)S(1)} %pass_on.11), channel_id=1, source_target_pairs={{0,8},{4,12},{8,0},{12,4},{16,24},{20,28},{24,16},{28,20},{1,9},{5... | collective-permute-start | bytes 1572872 | tf_op jit(solution)/shard_map/ppermute | solution.py:236
  53.9 10.2 %collective-permute-start.9 = (bf16[256,1024]{1,0:T(8,128)(2,1)S(1)}, bf16[256,1024]{1,0:T(8,128)(2,1)S(1)}, u32[]{:S(2)}, u32[]{:S(2)}) collective-permute-start(bf16[256,1024]{1,0:T(8,128)(2,1)S(1)} %pass_on.8), channel_id=1, source_target_pairs={{0,4},{4,0},{8,16},{12,20},{16,8},{20,12},{24,28},{28,24},{1,5},{5... | collective-permute-start | bytes 1572872 | tf_op jit(solution)/shard_map/ppermute | solution.py:236
  56.1 4.2 %collective-permute-start.15 = (bf16[512,2048]{1,0:T(8,128)(2,1)S(1)}, bf16[512,2048]{1,0:T(8,128)(2,1)S(1)}, u32[]{:S(2)}, u32[]{:S(2)}) collective-permute-start(bf16[512,2048]{1,0:T(8,128)(2,1)S(1)} %late_sums.3), channel_id=1, source_target_pairs={{0,4},{4,0},{1,5},{5,1},{2,6},{6,2},{3,7},{7,3},{8,12},{12,8},{9,1... | collective-permute-start | bytes 6291464 | tf_op jit(solution)/shard_map/ppermute | solution.py:535

commit v7 on v6

--- a/solution.py
+++ b/solution.py
@@ -12,7 +12,7 @@
 HD = 128
 SEQ = 128
 GROUP = 4
-SPAN = 1024
+SPAN = 3072
 PARTS = 1
 MIB = 1 << 20
 ROWS = (((1,), (1,)), ((), ()))

time: 65.3 us -> 65.3 us (level)
  no operation moved by 1% of the time
where the time goes in v7:
time: 65.3 us; the launch traced here: 65.1 us
  Pallas kernels  23.3 us (36%)
  starting transfers between devices  22.9 us (35%)
  waiting for transfers between devices  17.8 us (27%)
  between operations  0.97 us (1%)
    ppermute x8, waiting for transfers between devices, hop(): return lax.ppermute(values, ('tensor', 'mirror'), pairs)  13.5 us
    ppermute x8, starting transfers between devices, hop(): return lax.ppermute(values, ('tensor', 'mirror'), pairs)  12.8 us
    ppermute x7, starting transfers between devices, swap(): return lax.ppermute(values, 'dp', [(i, i ^ distance) for i in range(size)])  10 us
    pallas_call x1, Pallas kernels, input_partials(): pl.pallas_call(functools.partial(partials_kernel, pieces), in_specs=[NEAR...  5.97 us
    pallas_call x1, Pallas kernels, attention_grads(): pl.pallas_call(attention_kernel, in_specs=[FAR] * 7, out_specs=[NEAR, NEA...  5.39 us
    pallas_call x2, Pallas kernels, early_sums(): pl.pallas_call(functools.partial(early_kernel, size, side, counts, places...  4.03 us
    pallas_call x1, Pallas kernels, average(): pl.pallas_call(functools.partial(average_kernel, replicas), grid=(rows //...  2.84 us
    pallas_call x2, Pallas kernels, late_sums(): pl.pallas_call(functools.partial(late_kernel, size, side, counts, places)...  2.76 us
  transfers between devices with their start and end apart: 16, of which 7 were waited for; matrix products, arithmetic and copies ran while one was open for 0% of the time, Pallas kernels for 33%

profile of v7, /device:TPU:0, one launch (start us, length us, event | category | flops | bytes accessed | tf_op | source)
XLA Modules:
  0.0 65.1 jit_solution(14261593279694548907)
XLA Ops:
  0.6 1.2 %split_columns.1 = (bf16[64,1024]{1,0:T(8,128)(2,1)S(1)}, bf16[64,1024]{1,0:T(8,128)(2,1)S(1)}, bf16[64,1024]{1,0:T(8,128)(2,1)S(1)}, bf16[64,1024]{1,0:T(8,128)(2,1)S(1)}) custom-call(bf16[64,4096]{1,0:T(8,128)(2,1)} %bitcast.24), custom_call_target="tpu_custom_call" | custom-call | flops 1 | bytes 1 | tf_op jit(solution)/shard_map/split_columns/pallas_call | solution.py:197
  1.8 3.0 %collective-permute-start = (bf16[64,1024]{1,0:T(8,128)(2,1)S(1)}, bf16[64,1024]{1,0:T(8,128)(2,1)S(1)}, u32[]{:S(2)}, u32[]{:S(2)}) collective-permute-start(bf16[64,1024]{1,0:T(8,128)(2,1)S(1)} %get-tuple-element.21), channel_id=1, source_target_pairs={{0,1},{1,0},{2,3},{3,2},{4,5},{5,4},{6,7},{7,6},{8,9},{9,8},{10,11... | collective-permute-start | bytes 393224 | tf_op jit(solution)/shard_map/ppermute | solution.py:531
  4.8 1.5 %collective-permute-start.1 = (bf16[64,1024]{1,0:T(8,128)(2,1)S(1)}, bf16[64,1024]{1,0:T(8,128)(2,1)S(1)}, u32[]{:S(2)}, u32[]{:S(2)}) collective-permute-start(bf16[64,1024]{1,0:T(8,128)(2,1)S(1)} %get-tuple-element.22), channel_id=1, source_target_pairs={{0,2},{1,3},{2,0},{3,1},{4,6},{5,7},{6,4},{7,5},{8,10},{9,11},{10,... | collective-permute-start | bytes 393224 | tf_op jit(solution)/shard_map/ppermute | solution.py:531
  6.3 0.0 collective-permute-start.2
  6.3 5.4 %attention_grads.1 = (bf16[2,256,1024]{2,1,0:T(8,128)(2,1)S(1)}, bf16[3072,2,1024]{2,1,0:T(2,128)(2,1)S(1)}) custom-call(s32[2,1,128]{2,1,0:T(1,128)} %bitcast.25, f32[2,128,128]{2,1,0:T(8,128)} %constant.2.clone.table_ref, bf16[256,1024]{1,0:T(8,128)(2,1)} %bitcast.19, bf16[256,1024]{1,0:T(8,128)(2,1)} %bitcast.20, bf16[256,1024]{1,0:T(8,128)(2,1)} %bitcast.21, ...), custom_call_target="tpu_custom_call" | custom-call | flops 1 | bytes 1 | tf_op jit(solution)/shard_map/attention_grads/pallas_call | solution.py:104
  11.7 0.0 collective-permute-done.refs_1_
  11.7 0.8 %collective-permute-done.1.refs_2_ = bf16[64,1024]{1,0:T(8,128)(2,1)S(1)} collective-permute-done((bf16[64,1024]{1,0:T(8,128)(2,1)S(1)}, bf16[64,1024]{1,0:T(8,128)(2,1)S(1)}, u32[]{:S(2)}, u32[]{:S(2)}) %collective-permute-start.1) | collective-permute-done | bytes 131104 | tf_op jit(solution)/shard_map/ppermute | solution.py:531
  12.6 0.0 collective-permute-done.2.refs_3_
  12.6 0.1 collective-permute-start.6
  12.7 3.1 %collective-permute-start.3 = (bf16[256,1024]{1,0:T(8,128)(2,1)S(1)}, bf16[256,1024]{1,0:T(8,128)(2,1)S(1)}, u32[]{:S(2)}, u32[]{:S(2)}) collective-permute-start(bf16[256,1024]{1,0:T(8,128)(2,1)S(1)} %merge_tokens.1.refs_0_.refs_1_), channel_id=1, source_target_pairs={{0,8},{4,12},{8,0},{12,4},{16,24},{20,28},{24,16},{28,20},{1,9},{5... | collective-permute-start | bytes 1572872 | tf_op jit(solution)/shard_map/ppermute | solution.py:236
  15.8 1.5 %collective-permute-start.12 = (bf16[2,256,1024]{2,1,0:T(8,128)(2,1)S(1)}, bf16[2,256,1024]{2,1,0:T(8,128)(2,1)S(1)}, u32[]{:S(2)}, u32[]{:S(2)}) collective-permute-start(bf16[2,256,1024]{2,1,0:T(8,128)(2,1)S(1)} %get-tuple-element.29.grad_ref.refs_5_.refs_8_), channel_id=1, source_target_pairs={{0,2},{1,3},{2,0},{3,1},{4,6},{5,7},{6,4},{7,5},{8,10},{9,11},{10,... | collective-permute-start | bytes 3145736 | tf_op jit(solution)/shard_map/ppermute | solution.py:531
  17.3 1.2 %collective-permute-start.11 = (bf16[2,256,1024]{2,1,0:T(8,128)(2,1)S(1)}, bf16[2,256,1024]{2,1,0:T(8,128)(2,1)S(1)}, u32[]{:S(2)}, u32[]{:S(2)}) collective-permute-start(bf16[2,256,1024]{2,1,0:T(8,128)(2,1)S(1)} %get-tuple-element.29.grad_ref.refs_5_.refs_8_), channel_id=1, source_target_pairs={{0,1},{1,0},{2,3},{3,2},{4,5},{5,4},{6,7},{7,6},{8,9},{9,8},{10,11... | collective-permute-start | bytes 3145736 | tf_op jit(solution)/shard_map/ppermute | solution.py:531
  18.5 6.0 %input_partials.1 = bf16[4,4,64,1024]{3,2,1,0:T(8,128)(2,1)S(1)} custom-call(bf16[2,256,1024]{2,1,0:T(8,128)(2,1)S(1)} %get-tuple-element.29.grad_ref.refs_5_.refs_8_, bf16[3072,2,1024]{2,1,0:T(2,128)(2,1)S(1)} %get-tuple-element.30.near_ref, bf16[4096,2,1024]{2,1,0:T(2,128)(2,1)} %w_ref.3), custom_call_target="tpu_custom_call" | custom-call | flops 1 | bytes 1 | tf_op jit(solution)/shard_map/input_partials/pallas_call | solution.py:161
  24.5 0.0 collective-permute-done.6.flow_ref.refs_1_.refs_2_
  24.5 0.1 pass_on.9
  24.6 2.3 %collective-permute-start.7 = (bf16[256,1024]{1,0:T(8,128)(2,1)S(1)}, bf16[256,1024]{1,0:T(8,128)(2,1)S(1)}, u32[]{:S(2)}, u32[]{:S(2)}) collective-permute-start(bf16[256,1024]{1,0:T(8,128)(2,1)S(1)} %pass_on.9), channel_id=1, source_target_pairs={{0,8},{4,12},{8,0},{12,4},{16,24},{20,28},{24,16},{28,20},{1,9},{5... | collective-permute-start | bytes 1572872 | tf_op jit(solution)/shard_map/ppermute | solution.py:236
  26.8 1.8 %collective-permute-done.3.flow_ref.refs_3_.refs_5_ = bf16[256,1024]{1,0:T(8,128)(2,1)S(1)} collective-permute-done((bf16[256,1024]{1,0:T(8,128)(2,1)S(1)}, bf16[256,1024]{1,0:T(8,128)(2,1)S(1)}, u32[]{:S(2)}, u32[]{:S(2)}) %collective-permute-start.3) | collective-permute-done | bytes 524320 | tf_op jit(solution)/shard_map/ppermute | solution.py:236
  28.6 0.1 collective-permute-start.4
  28.7 9.6 %collective-permute-done.7.flow_ref.refs_4_.refs_6_ = bf16[256,1024]{1,0:T(8,128)(2,1)S(1)} collective-permute-done((bf16[256,1024]{1,0:T(8,128)(2,1)S(1)}, bf16[256,1024]{1,0:T(8,128)(2,1)S(1)}, u32[]{:S(2)}, u32[]{:S(2)}) %collective-permute-start.7) | collective-permute-done | bytes 524320 | tf_op jit(solution)/shard_map/ppermute | solution.py:236
  38.3 0.1 collective-permute-start.8
  38.4 0.0 collective-permute-done.4.flow_ref.refs_2_.refs_3_
  38.4 0.1 pass_on.7
  38.5 3.0 %collective-permute-start.5 = (bf16[256,1024]{1,0:T(8,128)(2,1)S(1)}, bf16[256,1024]{1,0:T(8,128)(2,1)S(1)}, u32[]{:S(2)}, u32[]{:S(2)}) collective-permute-start(bf16[256,1024]{1,0:T(8,128)(2,1)S(1)} %pass_on.7), channel_id=1, source_target_pairs={{0,8},{4,12},{8,0},{12,4},{16,24},{20,28},{24,16},{28,20},{1,9},{5... | collective-permute-start | bytes 1572872 | tf_op jit(solution)/shard_map/ppermute | solution.py:236
  41.5 0.0 collective-permute-done.12.refs_7_.refs_10_
  41.5 1.3 %collective-permute-start.14 = (bf16[256,1024]{1,0:T(8,128)(2,1)S(1)}, bf16[256,1024]{1,0:T(8,128)(2,1)S(1)}, u32[]{:S(2)}, u32[]{:S(2)}) collective-permute-start(bf16[256,1024]{1,0:T(8,128)(2,1)S(1)} %slice_bitcast_fusion), channel_id=1, source_target_pairs={{0,1},{1,0},{2,3},{3,2},{4,5},{5,4},{6,7},{7,6},{8,9},{9,8},{10,11... | collective-permute-start | bytes 1572872 | tf_op jit(solution)/shard_map/ppermute | solution.py:531
  42.8 0.0 collective-permute-done.11.refs_6_.refs_9_
  42.9 1.5 %collective-permute-start.13 = (bf16[256,1024]{1,0:T(8,128)(2,1)S(1)}, bf16[256,1024]{1,0:T(8,128)(2,1)S(1)}, u32[]{:S(2)}, u32[]{:S(2)}) collective-permute-start(bf16[256,1024]{1,0:T(8,128)(2,1)S(1)} %slice_bitcast_fusion.1), channel_id=1, source_target_pairs={{0,2},{1,3},{2,0},{3,1},{4,6},{5,7},{6,4},{7,5},{8,10},{9,11},{10,... | collective-permute-start | bytes 1572872 | tf_op jit(solution)/shard_map/ppermute | solution.py:531
  44.4 1.9 %early_sums.3.refs_0_ = f32[512,2048]{1,0:T(8,128)S(1)} custom-call(bf16[256,1024]{1,0:T(8,128)(2,1)S(1)} %merge_tokens.1.refs_0_.refs_1_, bf16[256,1024]{1,0:T(8,128)(2,1)S(1)} %collective-permute-done.6.flow_ref.refs_1_.refs_2_, bf16[256,1024]{1,0:T(8,128)(2,1)S(1)} %collective-permute-done.4.flow_ref.refs_2_.refs_3_, ...), custom_call_target="tpu_custom_call" | custom-call | flops 34359738368 | bytes 8388608 | tf_op jit(solution)/shard_map/early_sums/pallas_call | solution.py:471
  46.3 2.1 %early_sums.2.refs_0_ = f32[512,2048]{1,0:T(8,128)S(1)} custom-call(bf16[256,1024]{1,0:T(8,128)(2,1)S(1)} %merge_tokens.1.refs_0_.refs_1_, bf16[256,1024]{1,0:T(8,128)(2,1)S(1)} %collective-permute-done.6.flow_ref.refs_1_.refs_2_, bf16[256,1024]{1,0:T(8,128)(2,1)S(1)} %collective-permute-done.4.flow_ref.refs_2_.refs_3_, ...), custom_call_target="tpu_custom_call" | custom-call | flops 34359738368 | bytes 8388608 | tf_op jit(solution)/shard_map/early_sums/pallas_call | solution.py:471
  48.4 0.0 collective-permute-done.8.flow_ref.refs_4_
  48.4 0.1 pass_on.11
  48.5 4.1 %collective-permute-start.10 = (bf16[256,1024]{1,0:T(8,128)(2,1)S(1)}, bf16[256,1024]{1,0:T(8,128)(2,1)S(1)}, u32[]{:S(2)}, u32[]{:S(2)}) collective-permute-start(bf16[256,1024]{1,0:T(8,128)(2,1)S(1)} %pass_on.11), channel_id=1, source_target_pairs={{0,8},{4,12},{8,0},{12,4},{16,24},{20,28},{24,16},{28,20},{1,9},{5... | collective-permute-start | bytes 1572872 | tf_op jit(solution)/shard_map/ppermute | solution.py:236
  52.6 1.2 %collective-permute-done.5.flow_ref.refs_7_ = bf16[256,1024]{1,0:T(8,128)(2,1)S(1)} collective-permute-done((bf16[256,1024]{1,0:T(8,128)(2,1)S(1)}, bf16[256,1024]{1,0:T(8,128)(2,1)S(1)}, u32[]{:S(2)}, u32[]{:S(2)}) %collective-permute-start.5) | collective-permute-done | bytes 524320 | tf_op jit(solution)/shard_map/ppermute | solution.py:236
  53.9 0.1 collective-permute-start.9
  53.9 0.0 collective-permute-done.14.refs_12_
  54.0 0.7 %collective-permute-done.13.refs_11_ = bf16[256,1024]{1,0:T(8,128)(2,1)S(1)} collective-permute-done((bf16[256,1024]{1,0:T(8,128)(2,1)S(1)}, bf16[256,1024]{1,0:T(8,128)(2,1)S(1)}, u32[]{:S(2)}, u32[]{:S(2)}) %collective-permute-start.13) | collective-permute-done | bytes 524320 | tf_op jit(solution)/shard_map/ppermute | solution.py:531
  54.7 1.4 %late_sums.3 = bf16[512,2048]{1,0:T(8,128)(2,1)S(1)} custom-call(f32[512,2048]{1,0:T(8,128)S(1)} %early_sums.3.refs_0_, bf16[256,1024]{1,0:T(8,128)(2,1)S(1)} %merge_tokens.1.refs_0_.refs_1_, bf16[256,1024]{1,0:T(8,128)(2,1)S(1)} %collective-permute-done.6.flow_ref.refs_1_.refs_2_, bf16[256,1024]{1,0:T(8,128)(2,1)S(1)} %collective-permute-done.4.flow_ref.refs_2_.refs_3_, ...), custom_call_target="tpu_custom_call" | custom-call | flops 34359738368 | bytes 8388608 | tf_op jit(solution)/shard_map/late_sums/pallas_call | solution.py:490
  56.1 0.1 collective-permute-start.15
  56.2 1.4 %late_sums.2.own_ref = f32[512,2048]{1,0:T(8,128)S(1)} custom-call(f32[512,2048]{1,0:T(8,128)S(1)} %early_sums.2.refs_0_, bf16[256,1024]{1,0:T(8,128)(2,1)S(1)} %merge_tokens.1.refs_0_.refs_1_, bf16[256,1024]{1,0:T(8,128)(2,1)S(1)} %collective-permute-done.6.flow_ref.refs_1_.refs_2_, bf16[256,1024]{1,0:T(8,128)(2,1)S(1)} %collective-permute-done.4.flow_ref.refs_2_.refs_3_, ...), custom_call_target="tpu_custom_call" | custom-call | flops 34359738368 | bytes 8388608 | tf_op jit(solution)/shard_map/late_sums/pallas_call | solution.py:490
  57.5 2.8 %collective-permute-done.15.refs_0_ = bf16[512,2048]{1,0:T(8,128)(2,1)S(1)} collective-permute-done((bf16[512,2048]{1,0:T(8,128)(2,1)S(1)}, bf16[512,2048]{1,0:T(8,128)(2,1)S(1)}, u32[]{:S(2)}, u32[]{:S(2)}) %collective-permute-start.15) | collective-permute-done | bytes 2097184 | tf_op jit(solution)/shard_map/ppermute | solution.py:535
  60.3 2.8 %average_weight_grad.1 = f32[512,2,1024]{2,1,0:T(2,128)} custom-call(f32[512,2048]{1,0:T(8,128)S(1)} %late_sums.2.own_ref, bf16[512,2048]{1,0:T(8,128)(2,1)S(1)} %collective-permute-done.15.refs_0_), custom_call_target="tpu_custom_call" | custom-call | flops 1 | bytes 1 | tf_op jit(solution)/shard_map/average_weight_grad/pallas_call | solution.py:518
  63.1 0.9 %collective-permute-done.10.refs_1_ = bf16[256,1024]{1,0:T(8,128)(2,1)S(1)} collective-permute-done((bf16[256,1024]{1,0:T(8,128)(2,1)S(1)}, bf16[256,1024]{1,0:T(8,128)(2,1)S(1)}, u32[]{:S(2)}, u32[]{:S(2)}) %collective-permute-start.10) | collective-permute-done | bytes 524320 | tf_op jit(solution)/shard_map/ppermute | solution.py:236
  64.1 0.0 collective-permute-done.9.refs_0_
  64.1 0.9 %finish_input_grad.1 = bf16[64,4096]{1,0:T(8,128)(2,1)} custom-call(bf16[256,1024]{1,0:T(8,128)(2,1)S(1)} %collective-permute-done.9.refs_0_, bf16[256,1024]{1,0:T(8,128)(2,1)S(1)} %collective-permute-done.10.refs_1_, bf16[4,256,1024]{2,1,0:T(8,128)(2,1)S(1)} %bitcast.18), custom_call_target="tpu_custom_call" | custom-call | flops 1 | bytes 1 | tf_op jit(solution)/shard_map/finish_input_grad/pallas_call | solution.py:322
  (6 shorter events, 0.2 us)
Async XLA Ops:
  1.8 9.9 %collective-permute-start = (bf16[64,1024]{1,0:T(8,128)(2,1)S(1)}, bf16[64,1024]{1,0:T(8,128)(2,1)S(1)}, u32[]{:S(2)}, u32[]{:S(2)}) collective-permute-start(bf16[64,1024]{1,0:T(8,128)(2,1)S(1)} %get-tuple-element.21), channel_id=1, source_target_pairs={{0,1},{1,0},{2,3},{3,2},{4,5},{5,4},{6,7},{7,6},{8,9},{9,8},{10,11... | collective-permute-start | bytes 393224 | tf_op jit(solution)/shard_map/ppermute | solution.py:531
  4.8 7.8 %collective-permute-start.1 = (bf16[64,1024]{1,0:T(8,128)(2,1)S(1)}, bf16[64,1024]{1,0:T(8,128)(2,1)S(1)}, u32[]{:S(2)}, u32[]{:S(2)}) collective-permute-start(bf16[64,1024]{1,0:T(8,128)(2,1)S(1)} %get-tuple-element.22), channel_id=1, source_target_pairs={{0,2},{1,3},{2,0},{3,1},{4,6},{5,7},{6,4},{7,5},{8,10},{9,11},{10,... | collective-permute-start | bytes 393224 | tf_op jit(solution)/shard_map/ppermute | solution.py:531
  6.3 6.3 %collective-permute-start.2 = (bf16[64,1024]{1,0:T(8,128)(2,1)S(1)}, bf16[64,1024]{1,0:T(8,128)(2,1)S(1)}, u32[]{:S(2)}, u32[]{:S(2)}) collective-permute-start(bf16[64,1024]{1,0:T(8,128)(2,1)S(1)} %get-tuple-element.23), channel_id=1, source_target_pairs={{0,3},{1,2},{2,1},{3,0},{4,7},{5,6},{6,5},{7,4},{8,11},{9,10},{10,... | collective-permute-start | bytes 393224 | tf_op jit(solution)/shard_map/ppermute | solution.py:531
  12.6 11.9 %collective-permute-start.6 = (bf16[256,1024]{1,0:T(8,128)(2,1)S(1)}, bf16[256,1024]{1,0:T(8,128)(2,1)S(1)}, u32[]{:S(2)}, u32[]{:S(2)}) collective-permute-start(bf16[256,1024]{1,0:T(8,128)(2,1)S(1)} %merge_tokens.1.refs_0_.refs_1_), channel_id=1, source_target_pairs={{0,4},{4,0},{8,16},{12,20},{16,8},{20,12},{24,28},{28,24},{1,5},{5... | collective-permute-start | bytes 1572872 | tf_op jit(solution)/shard_map/ppermute | solution.py:236
  12.7 15.9 %collective-permute-start.3 = (bf16[256,1024]{1,0:T(8,128)(2,1)S(1)}, bf16[256,1024]{1,0:T(8,128)(2,1)S(1)}, u32[]{:S(2)}, u32[]{:S(2)}) collective-permute-start(bf16[256,1024]{1,0:T(8,128)(2,1)S(1)} %merge_tokens.1.refs_0_.refs_1_), channel_id=1, source_target_pairs={{0,8},{4,12},{8,0},{12,4},{16,24},{20,28},{24,16},{28,20},{1,9},{5... | collective-permute-start | bytes 1572872 | tf_op jit(solution)/shard_map/ppermute | solution.py:236
  15.8 25.7 %collective-permute-start.12 = (bf16[2,256,1024]{2,1,0:T(8,128)(2,1)S(1)}, bf16[2,256,1024]{2,1,0:T(8,128)(2,1)S(1)}, u32[]{:S(2)}, u32[]{:S(2)}) collective-permute-start(bf16[2,256,1024]{2,1,0:T(8,128)(2,1)S(1)} %get-tuple-element.29.grad_ref.refs_5_.refs_8_), channel_id=1, source_target_pairs={{0,2},{1,3},{2,0},{3,1},{4,6},{5,7},{6,4},{7,5},{8,10},{9,11},{10,... | collective-permute-start | bytes 3145736 | tf_op jit(solution)/shard_map/ppermute | solution.py:531
  17.3 25.5 %collective-permute-start.11 = (bf16[2,256,1024]{2,1,0:T(8,128)(2,1)S(1)}, bf16[2,256,1024]{2,1,0:T(8,128)(2,1)S(1)}, u32[]{:S(2)}, u32[]{:S(2)}) collective-permute-start(bf16[2,256,1024]{2,1,0:T(8,128)(2,1)S(1)} %get-tuple-element.29.grad_ref.refs_5_.refs_8_), channel_id=1, source_target_pairs={{0,1},{1,0},{2,3},{3,2},{4,5},{5,4},{6,7},{7,6},{8,9},{9,8},{10,11... | collective-permute-start | bytes 3145736 | tf_op jit(solution)/shard_map/ppermute | solution.py:531
  24.6 13.7 %collective-permute-start.7 = (bf16[256,1024]{1,0:T(8,128)(2,1)S(1)}, bf16[256,1024]{1,0:T(8,128)(2,1)S(1)}, u32[]{:S(2)}, u32[]{:S(2)}) collective-permute-start(bf16[256,1024]{1,0:T(8,128)(2,1)S(1)} %pass_on.9), channel_id=1, source_target_pairs={{0,8},{4,12},{8,0},{12,4},{16,24},{20,28},{24,16},{28,20},{1,9},{5... | collective-permute-start | bytes 1572872 | tf_op jit(solution)/shard_map/ppermute | solution.py:236
  28.6 9.8 %collective-permute-start.4 = (bf16[256,1024]{1,0:T(8,128)(2,1)S(1)}, bf16[256,1024]{1,0:T(8,128)(2,1)S(1)}, u32[]{:S(2)}, u32[]{:S(2)}) collective-permute-start(bf16[256,1024]{1,0:T(8,128)(2,1)S(1)} %pass_on.6), channel_id=1, source_target_pairs={{0,4},{4,0},{8,16},{12,20},{16,8},{20,12},{24,28},{28,24},{1,5},{5... | collective-permute-start | bytes 1572872 | tf_op jit(solution)/shard_map/ppermute | solution.py:236
  38.3 10.1 %collective-permute-start.8 = (bf16[256,1024]{1,0:T(8,128)(2,1)S(1)}, bf16[256,1024]{1,0:T(8,128)(2,1)S(1)}, u32[]{:S(2)}, u32[]{:S(2)}) collective-permute-start(bf16[256,1024]{1,0:T(8,128)(2,1)S(1)} %pass_on.10), channel_id=1, source_target_pairs={{0,4},{4,0},{8,16},{12,20},{16,8},{20,12},{24,28},{28,24},{1,5},{5... | collective-permute-start | bytes 1572872 | tf_op jit(solution)/shard_map/ppermute | solution.py:236
  38.5 15.4 %collective-permute-start.5 = (bf16[256,1024]{1,0:T(8,128)(2,1)S(1)}, bf16[256,1024]{1,0:T(8,128)(2,1)S(1)}, u32[]{:S(2)}, u32[]{:S(2)}) collective-permute-start(bf16[256,1024]{1,0:T(8,128)(2,1)S(1)} %pass_on.7), channel_id=1, source_target_pairs={{0,8},{4,12},{8,0},{12,4},{16,24},{20,28},{24,16},{28,20},{1,9},{5... | collective-permute-start | bytes 1572872 | tf_op jit(solution)/shard_map/ppermute | solution.py:236
  41.5 12.4 %collective-permute-start.14 = (bf16[256,1024]{1,0:T(8,128)(2,1)S(1)}, bf16[256,1024]{1,0:T(8,128)(2,1)S(1)}, u32[]{:S(2)}, u32[]{:S(2)}) collective-permute-start(bf16[256,1024]{1,0:T(8,128)(2,1)S(1)} %slice_bitcast_fusion), channel_id=1, source_target_pairs={{0,1},{1,0},{2,3},{3,2},{4,5},{5,4},{6,7},{7,6},{8,9},{9,8},{10,11... | collective-permute-start | bytes 1572872 | tf_op jit(solution)/shard_map/ppermute | solution.py:531
  42.9 11.8 %collective-permute-start.13 = (bf16[256,1024]{1,0:T(8,128)(2,1)S(1)}, bf16[256,1024]{1,0:T(8,128)(2,1)S(1)}, u32[]{:S(2)}, u32[]{:S(2)}) collective-permute-start(bf16[256,1024]{1,0:T(8,128)(2,1)S(1)} %slice_bitcast_fusion.1), channel_id=1, source_target_pairs={{0,2},{1,3},{2,0},{3,1},{4,6},{5,7},{6,4},{7,5},{8,10},{9,11},{10,... | collective-permute-start | bytes 1572872 | tf_op jit(solution)/shard_map/ppermute | solution.py:531
  48.5 15.6 %collective-permute-start.10 = (bf16[256,1024]{1,0:T(8,128)(2,1)S(1)}, bf16[256,1024]{1,0:T(8,128)(2,1)S(1)}, u32[]{:S(2)}, u32[]{:S(2)}) collective-permute-start(bf16[256,1024]{1,0:T(8,128)(2,1)S(1)} %pass_on.11), channel_id=1, source_target_pairs={{0,8},{4,12},{8,0},{12,4},{16,24},{20,28},{24,16},{28,20},{1,9},{5... | collective-permute-start | bytes 1572872 | tf_op jit(solution)/shard_map/ppermute | solution.py:236
  53.9 10.2 %collective-permute-start.9 = (bf16[256,1024]{1,0:T(8,128)(2,1)S(1)}, bf16[256,1024]{1,0:T(8,128)(2,1)S(1)}, u32[]{:S(2)}, u32[]{:S(2)}) collective-permute-start(bf16[256,1024]{1,0:T(8,128)(2,1)S(1)} %pass_on.8), channel_id=1, source_target_pairs={{0,4},{4,0},{8,16},{12,20},{16,8},{20,12},{24,28},{28,24},{1,5},{5... | collective-permute-start | bytes 1572872 | tf_op jit(solution)/shard_map/ppermute | solution.py:236
  56.1 4.2 %collective-permute-start.15 = (bf16[512,2048]{1,0:T(8,128)(2,1)S(1)}, bf16[512,2048]{1,0:T(8,128)(2,1)S(1)}, u32[]{:S(2)}, u32[]{:S(2)}) collective-permute-start(bf16[512,2048]{1,0:T(8,128)(2,1)S(1)} %late_sums.3), channel_id=1, source_target_pairs={{0,4},{4,0},{1,5},{5,1},{2,6},{6,2},{3,7},{7,3},{8,12},{12,8},{9,1... | collective-permute-start | bytes 6291464 | tf_op jit(solution)/shard_map/ppermute | solution.py:535
